TPU v7x, 32 devices: a whole 2x2x4 slice. The times are simulated.
32 devices in a mesh: fsdp: 4 (over x, core), ctx: 8 (over z, y).
Axes of the slice: x: 2, y: 2, z: 4, core: 2. Of those that a mesh axis runs over, the one named last changes fastest.
Arguments:
- inputs: bfloat16 [4, 1024, 1600], P('fsdp', 'ctx'), may hold values from -6 to 6
- cotangent: bfloat16 [4, 1024, 1600], P('fsdp', 'ctx'), may hold values from -6 to 6
- slot_order: int32 [4, 16], P('fsdp'), may hold values from 0 to 15, each once within a row
- weights: bfloat16 [240000, 128], P(('fsdp', 'ctx')), may hold values from -0.61 to 0.61
- vectors: bfloat16 [12, 1600], P('fsdp', 'ctx'), may hold values from -1.2 to 1.4
- first_w: float32 [240000, 128], P(('fsdp', 'ctx')), may hold values from -25.728 to 25.728
- second_w: float32 [240000, 128], P(('fsdp', 'ctx')), may hold values from 0.025 to 5.912986
- first_vec: float32 [12, 1600], P('fsdp', 'ctx'), may hold values from -42.624 to 42.624
- second_vec: float32 [12, 1600], P('fsdp', 'ctx'), may hold values from 0.36864 to 16.42496
Outputs:
- outputs: bfloat16 [4, 1024, 1600], P('fsdp', 'ctx')
- input_grad: bfloat16 [4, 1024, 1600], P('fsdp', 'ctx')
- moment_w: float32 [240000, 128], P(('fsdp', 'ctx'))
- squares_w: float32 [240000, 128], P(('fsdp', 'ctx'))
- weight_w: float32 [240000, 128], P(('fsdp', 'ctx'))
- moment_vec: float32 [12, 1600], P('fsdp', 'ctx')
- squares_vec: float32 [12, 1600], P('fsdp', 'ctx')
- weight_vec: float32 [12, 1600], P('fsdp', 'ctx')
Inputs may be any that keep to these rules, and one draw needn't show every extreme that they name: Each row is a permutation: slot j of a sequence (its rows j * 64 to j * 64 + 63) holds the positions slot_order[seq, j] * 64 onward.
All inputs are finite; a program needn't handle non-finite values.
Results may differ from a plain program's by a relative error of at most 0.025.
Values may be sent and summed in bfloat16 or wider, within the bound.
A program may use at most 512 MiB of HBM per device.

v0:
```python
import jax
import jax.numpy as jnp
from jax import lax
from jax.sharding import PartitionSpec as P

HEADS = 25
HD = 64
FF = 6400
STEP = 10


epsilon_norm = 1e-05
beta_first = 0.9
beta_second = 0.999
epsilon_adam = 1e-08
weight_decay = 0.1
rate_matrix = 0.1
rate_vector = 0.8


def shifted(value, axis, steps):
    count = lax.axis_size(axis)
    pairs = [(source, (source + steps) % count) for source in range(count)]
    return lax.ppermute(value, axis, pairs)


def layer_norm(value, gain, shift):
    center = value - jnp.mean(value, -1, keepdims=True)
    spread = jnp.mean(center * center, -1, keepdims=True)
    return center * lax.rsqrt(spread + epsilon_norm) * gain + shift


def gelu_tanh(value):
    return jax.nn.gelu(value, approximate=True)


def key_positions(slot_order, first_slot, slots, block):
    groups = lax.dynamic_slice_in_dim(slot_order, first_slot, slots, 1)
    offsets = jnp.arange(block, dtype=jnp.int32)
    return (groups[:, :, None] * block + offsets).reshape(slot_order.shape[0], slots * block)


def unpack_flat(flat, width, hidden):
    flat = flat.reshape(-1)
    first_end = 3 * width * width
    second_end = 4 * width * width
    third_end = 4 * width * width + width * hidden
    return (
        flat[:first_end].reshape(width, 3 * width),
        flat[first_end:second_end].reshape(width, width),
        flat[second_end:third_end].reshape(width, hidden),
        flat[third_end:].reshape(hidden, width),
    )


def gather_params(weights, vectors):
    local = weights.reshape(1, weights.shape[0], weights.shape[1])
    part = (
        lax.all_gather(local, "fsdp", axis=0, tiled=True),
        lax.all_gather(vectors, "fsdp", axis=0, tiled=True),
    )
    return (
        lax.all_gather(part[0], "ctx", axis=1, tiled=True),
        lax.all_gather(part[1], "ctx", axis=1, tiled=True),
    )


def reduce_grads(grad_flat, grad_vec):
    part = (
        lax.psum_scatter(
            grad_flat.astype(jnp.bfloat16), "fsdp", scatter_dimension=0, tiled=True
        ).astype(jnp.float32),
        lax.psum_scatter(
            grad_vec.astype(jnp.bfloat16), "fsdp", scatter_dimension=0, tiled=True
        ).astype(jnp.float32),
    )
    return (
        lax.psum_scatter(
            part[0].astype(jnp.bfloat16), "ctx", scatter_dimension=1, tiled=True
        ).astype(jnp.float32),
        lax.psum_scatter(
            part[1].astype(jnp.bfloat16), "ctx", scatter_dimension=1, tiled=True
        ).astype(jnp.float32),
    )


def pass_grads(grad_pairs):
    return shifted(grad_pairs.astype(jnp.bfloat16), "ctx", 1).astype(grad_pairs.dtype)


def adamw(weight, grad, first, second, rate, decay):
    first = beta_first * first + (1.0 - beta_first) * grad
    second = beta_second * second + (1.0 - beta_second) * grad * grad
    first_hat = first / (1.0 - beta_first**STEP)
    second_hat = second / (1.0 - beta_second**STEP)
    weight = weight.astype(jnp.float32)
    updated = weight - rate * (first_hat / (jnp.sqrt(second_hat) + epsilon_adam) + decay * weight)
    return (first, second, updated)


def per_device(
    inputs, cotangent, slot_order, weights, vectors, first_w, second_w, first_vec, second_vec
):
    seqs, rows, width = inputs.shape
    tokens = seqs * rows
    block = rows // 2
    cycle = lax.axis_size("ctx")
    shards = lax.axis_size("fsdp")
    me = lax.axis_index("ctx")
    full_flat, full_vec = gather_params(weights, vectors)
    full_qkv, full_out, full_fc, full_proj = unpack_flat(full_flat, width, FF)
    vec = full_vec.astype(jnp.float32)
    bias_fc = vec[8:].reshape(-1)
    x_in = inputs.reshape(tokens, width).astype(jnp.float32)
    h_first, pull_first = jax.vjp(layer_norm, x_in, vec[0], vec[1])
    h_first_b = h_first.astype(jnp.bfloat16)
    zero_row = jnp.zeros((width,), jnp.float32)
    qkv = jnp.dot(h_first_b, full_qkv, preferred_element_type=jnp.float32)
    qkv_b = (qkv + jnp.concatenate([vec[2], zero_row, vec[3]])).astype(jnp.bfloat16)
    query_heads = qkv_b[:, :width].reshape(seqs, rows, HEADS, HD)
    key_value = qkv_b[:, width:].reshape(seqs, rows, 2, width)
    query_pos = key_positions(slot_order, 2 * me, 2, block)

    def online(state, item):
        top, total, accum = state
        keys_i, values_i, pos_i = item
        scores = (
            jnp.einsum("sqhd,skhd->shqk", query_heads, keys_i, preferred_element_type=jnp.float32)
            * 0.125
        )
        allowed = pos_i[:, None, None, :] <= query_pos[:, None, :, None]
        scores = jnp.where(allowed, scores, -1e30)
        peak = jnp.maximum(top, jnp.max(scores, -1))
        weights_p = jnp.where(allowed, jnp.exp(scores - peak[..., None]), 0.0)
        factor = jnp.exp(top - peak)
        total = total * factor + jnp.sum(weights_p, -1)
        mixed = jnp.einsum(
            "shqk,skhd->sqhd",
            weights_p.astype(jnp.bfloat16),
            values_i,
            preferred_element_type=jnp.float32,
        )
        accum = accum * jnp.transpose(factor, (0, 2, 1))[..., None] + mixed
        return ((peak, total, accum), None)

    start_state = (
        jnp.full((seqs, HEADS, rows), -1e30, jnp.float32),
        jnp.zeros((seqs, HEADS, rows), jnp.float32),
        jnp.zeros((seqs, rows, HEADS, HD), jnp.float32),
    )
    state = start_state
    piece = lax.all_gather(key_value, "ctx", axis=1, tiled=True)
    count = piece.shape[1]
    turns = count // rows
    pos_all = key_positions(slot_order, jnp.int32(0) // block, count // block, block)
    stack = piece.reshape(seqs, turns, rows, 2, HEADS, HD).transpose(1, 0, 2, 3, 4, 5)
    pos_stack = pos_all.reshape(seqs, turns, rows).transpose(1, 0, 2)
    state, _ = lax.scan(online, state, (stack[:, :, :, 0], stack[:, :, :, 1], pos_stack))
    top, total, accum = state
    attn = accum / jnp.transpose(total, (0, 2, 1))[..., None]
    logsum = top + jnp.log(total)
    attn_b = attn.reshape(tokens, width).astype(jnp.bfloat16)
    resid = x_in + jnp.dot(attn_b, full_out, preferred_element_type=jnp.float32) + vec[4]
    h_second, pull_second = jax.vjp(layer_norm, resid, vec[5], vec[6])
    h_second_b = h_second.astype(jnp.bfloat16)
    pre = jnp.dot(h_second_b, full_fc, preferred_element_type=jnp.float32) + bias_fc
    act, pull_gelu = jax.vjp(gelu_tanh, pre)
    act_b = act.astype(jnp.bfloat16)
    result = resid + jnp.dot(act_b, full_proj, preferred_element_type=jnp.float32) + vec[7]
    outputs = result.astype(jnp.bfloat16).reshape(seqs, rows, width)
    back_b = cotangent.reshape(tokens, width)
    back = back_b.astype(jnp.float32)
    grad_proj = jnp.einsum("tf,td->fd", act_b, back_b, preferred_element_type=jnp.float32)
    grad_bp = jnp.sum(back, 0)
    dact = jnp.einsum("td,fd->tf", back_b, full_proj, preferred_element_type=jnp.float32)
    dpre_b = pull_gelu(dact)[0].astype(jnp.bfloat16)
    grad_fc = jnp.einsum("td,tf->df", h_second_b, dpre_b, preferred_element_type=jnp.float32)
    grad_bf = jnp.sum(dpre_b, 0, dtype=jnp.float32)
    dh_second = jnp.einsum("tf,df->td", dpre_b, full_fc, preferred_element_type=jnp.float32)
    dres_ln, grad_g2, grad_b2 = pull_second(dh_second)
    dresid = back + dres_ln
    dbranch_b = dresid.astype(jnp.bfloat16)
    grad_bo = jnp.sum(dbranch_b, 0, dtype=jnp.float32)
    grad_out = jnp.einsum("td,te->de", attn_b, dbranch_b, preferred_element_type=jnp.float32)
    dattn_b = jnp.einsum(
        "te,de->td", dbranch_b, full_out, preferred_element_type=jnp.float32
    ).astype(jnp.bfloat16)
    grad_heads = dattn_b.reshape(seqs, rows, HEADS, HD)
    delta = jnp.transpose(jnp.sum(grad_heads.astype(jnp.float32) * attn, -1), (0, 2, 1))

    def contribute(pair, source):
        pos_k = key_positions(slot_order, 2 * source, 2, block)
        key_h = pair[:, :, 0].reshape(seqs, rows, HEADS, HD)
        value_h = pair[:, :, 1].reshape(seqs, rows, HEADS, HD)
        scores = (
            jnp.einsum("sqhd,skhd->shqk", query_heads, key_h, preferred_element_type=jnp.float32)
            * 0.125
        )
        allowed = pos_k[:, None, None, :] <= query_pos[:, None, :, None]
        probs = jnp.where(allowed, jnp.exp(scores - logsum[..., None]), 0.0)
        dvalue = jnp.einsum(
            "shqk,sqhd->skhd",
            probs.astype(jnp.bfloat16),
            grad_heads,
            preferred_element_type=jnp.float32,
        )
        dprobs = jnp.einsum(
            "sqhd,skhd->shqk", grad_heads, value_h, preferred_element_type=jnp.float32
        )
        dscores = (probs * (dprobs - delta[..., None])).astype(jnp.bfloat16)
        dquery = (
            jnp.einsum("shqk,skhd->sqhd", dscores, key_h, preferred_element_type=jnp.float32)
            * 0.125
        )
        dkey = (
            jnp.einsum("shqk,sqhd->skhd", dscores, query_heads, preferred_element_type=jnp.float32)
            * 0.125
        )
        return (dquery, jnp.stack((dkey, dvalue), 2))

    dq_own, dkv_own = contribute(key_value, me)

    def turn(step, state):
        pair, dkv_acc, dq_acc = state
        pair = shifted(pair, "ctx", 1)
        dkv_acc = pass_grads(dkv_acc)
        source = (me - step) % cycle
        dq_part, dkv_part = contribute(pair, source)
        return (pair, dkv_acc + dkv_part, dq_acc + dq_part)

    final = lax.fori_loop(1, cycle, turn, (key_value, dkv_own, dq_own))
    dkv = pass_grads(final[1])
    dqkv_b = jnp.concatenate(
        [final[2].reshape(tokens, width), dkv.reshape(tokens, 2 * width)], 1
    ).astype(jnp.bfloat16)
    grad_qkv = jnp.einsum("td,te->de", h_first_b, dqkv_b, preferred_element_type=jnp.float32)
    bias_sums = jnp.sum(dqkv_b, 0, dtype=jnp.float32)
    dh_first = jnp.einsum("te,de->td", dqkv_b, full_qkv, preferred_element_type=jnp.float32)
    dx_ln, grad_g1, grad_b1 = pull_first(dh_first)
    input_grad = (dresid + dx_ln).astype(jnp.bfloat16).reshape(seqs, rows, width)
    grad_vec = jnp.concatenate(
        [
            jnp.stack(
                [
                    grad_g1,
                    grad_b1,
                    bias_sums[:width],
                    bias_sums[2 * width :],
                    grad_bo,
                    grad_g2,
                    grad_b2,
                    grad_bp,
                ]
            ),
            grad_bf.reshape(-1, width),
        ],
        0,
    )
    grad_flat = jnp.concatenate(
        [grad_qkv.reshape(-1), grad_out.reshape(-1), grad_fc.reshape(-1), grad_proj.reshape(-1)]
    ).reshape(shards, -1, 128)
    owned_flat, owned_vec = reduce_grads(grad_flat, grad_vec)
    owned_flat = owned_flat.reshape(weights.shape[0], 128)
    new_w = adamw(weights, owned_flat, first_w, second_w, rate_matrix, weight_decay)
    new_vec = adamw(vectors, owned_vec, first_vec, second_vec, rate_vector, 0.0)
    return (outputs, input_grad, new_w[0], new_w[1], new_w[2], new_vec[0], new_vec[1], new_vec[2])


def solution(mesh):
    in_specs = (
        P("fsdp", "ctx", None),
        P("fsdp", "ctx", None),
        P("fsdp", None),
        P(("fsdp", "ctx"), None),
        P("fsdp", "ctx"),
        P(("fsdp", "ctx"), None),
        P(("fsdp", "ctx"), None),
        P("fsdp", "ctx"),
        P("fsdp", "ctx"),
    )
    out_specs = (
        P("fsdp", "ctx", None),
        P("fsdp", "ctx", None),
        P(("fsdp", "ctx"), None),
        P(("fsdp", "ctx"), None),
        P(("fsdp", "ctx"), None),
        P("fsdp", "ctx"),
        P("fsdp", "ctx"),
        P("fsdp", "ctx"),
    )
    return jax.shard_map(
        per_device, mesh=mesh, in_specs=in_specs, out_specs=out_specs, check_vma=False
    )
```

profile of v0, /device:TPU:0, one launch (start us, length us, event | category | flops | bytes accessed | tf_op | source)
XLA Modules:
  0.0 3232.0 jit_solution(15376447373134807615)
XLA Ops:
  7.9 58.6 %all-gather.12.cloned.1.call-done = bf16[4,7500,128]{2,1,0:T(8,128)(2,1)} async-done(((bf16[1,7500,128]{2,1,0:T(8,128)(2,1)}), bf16[4,7500,128]{2,1,0:T(8,128)(2,1)}) %all-gather.12.cloned.1.call-update) | async-done | bytes 7680016 | tf_op jit(solution)/shard_map/all_gather | solution.py:59
  66.6 28.1 copy.40
  100.5 111.3 %all-gather.2 = bf16[8,200,12]{1,2,0:T(8,128)(2,1)S(1)} all-gather(bf16[1,200,12]{1,2,0:T(8,128)(2,1)S(1)} %bitcast.325), channel_id=1, replica_groups=mesh['fsdp'=4,'ctx'=8] {'ctx'}, dimensions={0}, use_global_device_ids=true | all-gather | bytes 43200 | tf_op jit(solution)/shard_map/all_gather | solution.py:64
  213.3 1043.5 %all-gather.8.cloned.1.call-done = bf16[4,60000,128]{2,0,1:T(4,128)(2,1)} async-done(((bf16[4,7500,128]{2,0,1:T(4,128)(2,1)}), bf16[4,60000,128]{2,0,1:T(4,128)(2,1)}) %all-gather.8.cloned.1.call-update) | async-done | bytes 61440016 | tf_op jit(solution)/shard_map/all_gather | solution.py:63
  1256.7 304.7 %slice_reduce_fusion = bf16[60000,128]{1,0:T(8,128)(2,1)} fusion(bf16[4,60000,128]{2,0,1:T(4,128)(2,1)} %all-gather.8.cloned.1.call-done), kind=kLoop, calls=%fused_computation.47 | loop fusion | bytes 30720000 | tf_op jit(solution)/shard_map/slice | solution.py:49
  1561.4 25.3 reshape.677
  1601.4 41.8 %copy.43 = bf16[4,60000,128]{2,1,0:T(8,128)(2,1)} copy(bf16[4,60000,128]{2,0,1:T(4,128)(2,1)} %all-gather.8.cloned.1.call-done) | data formatting | bytes 122880000 | tf_op jit(solution)/shard_map/all_gather | solution.py:63
  1643.2 99.2 %slice.102 = bf16[19200,1600]{1,0:T(8,128)(2,1)} reshape(bf16[4,60000,128]{2,1,0:T(8,128)(2,1)} %copy.43) | data formatting | bytes 122880000 | tf_op jit(solution)/shard_map/slice | solution.py:50
  1742.5 103.1 %slice.107 = bf16[4800,6400]{1,0:T(8,128)(2,1)} reshape(bf16[4,60000,128]{2,1,0:T(8,128)(2,1)} %copy.43) | data formatting | bytes 122880000 | tf_op jit(solution)/shard_map/slice | solution.py:51
  1856.9 28.1 while.36
  1948.9 281.7 %while.35 = (s32[]{:T(128)}, bf16[1,128,2,1600]{1,3,2,0:T(8,128)(2,1)}, bf16[1,128,2,25,64]{1,4,3,2,0:T(8,128)(2,1)}, f32[1,128,25,64]{1,3,2,0:T(8,128)S(1)}, s3...) while((s32[]{:T(128)}, ...), condition=%wide.region_12.13_spmd.clone, body=%wide.region_11.12_spmd.clone.sunk | while | flops 267280656 | bytes 26689976 | solution.py:231
  2034.6 23.5 collective-permute-done
  2075.7 23.5 collective-permute-done
  2116.0 23.5 collective-permute-done
  2155.3 23.5 collective-permute-done
  2193.7 23.5 collective-permute-done
  2242.9 29.8 copy.45
  2272.6 39.4 %reshape.693 = bf16[10240000]{0:T(1024)(128)(2,1)} reshape(bf16[6400,1600]{1,0:T(8,128)(2,1)} %copy.45) | data formatting | bytes 40960000 | tf_op jit(solution)/shard_map/reshape | solution.py:260
  2312.1 37.7 %reshape.692 = bf16[10240000]{0:T(1024)(128)(2,1)} reshape(bf16[1600,6400]{1,0:T(8,128)(2,1)} %convolution_convert_fusion.1) | data formatting | bytes 40960000 | tf_op jit(solution)/shard_map/reshape | solution.py:260
  2372.9 27.1 reshape.690
  2400.1 81.3 %pad_maximum_fusion = bf16[30720000]{0:T(1024)(128)(2,1)} fusion(bf16[10240000]{0:T(1024)(128)(2,1)} %reshape.693, bf16[10240000]{0:T(1024)(128)(2,1)} %reshape.692, bf16[2560000]{0:T(1024)(128)(2,1)} %reshape.691, bf16[7680000]{0:T(1024)(128)(2,1)} %reshape.690), kind=kLoop, calls=%fused_computation.46 | loop fusion | flops 245760000 | bytes 122880000 | tf_op jit(solution)/shard_map/concatenate | solution.py:259
  2527.9 37.8 %all-reduce.3 = bf16[3,1600]{1,0:T(4,128)(2,1)S(1)} all-reduce(bf16[3,1600]{1,0:T(4,128)(2,1)S(1)} %constant_dynamic-slice_fusion.1), channel_id=6, replica_groups=mesh['fsdp'=4,'ctx'=8] {'ctx'}, use_global_device_ids=true, to_apply=%region_26.27.clone | all-reduce | flops 4800 | bytes 19200
  2566.8 331.7 %reduce-scatter.8.cloned.1.call-done = bf16[1,60000,128]{2,1,0:T(8,128)(2,1)} async-done(((bf16[4,60000,128]{2,1,0:T(8,128)(2,1)}), bf16[1,60000,128]{2,1,0:T(8,128)(2,1)}) %reduce-scatter.8.cloned.1.call-update) | async-done | bytes 15360016
  2898.5 307.4 %fusion.4 = bf16[7504,128]{1,0:T(8,128)(2,1)S(1)} fusion(bf16[1,60000,128]{2,1,0:T(8,128)(2,1)} %reduce-scatter.8.cloned.1.call-done), kind=kCustom, calls=%all-reduce-scatter | all-reduce-scatter fusion | flops 7684097 | bytes 17281536
  (423 shorter events, 389.2 us)
Async XLA Ops:
  7.2 59.4 %all-gather.12.cloned.1.call-start = ((), (), s32[]{:S(2)}) async-start(), calls=%async_computation.3 | async-start | bytes 9605120 | tf_op jit(solution)/shard_map/all_gather | solution.py:59
  7.9 1248.8 %all-gather.8.cloned.1.call-start = ((), (), s32[]{:S(2)}) async-start(), calls=%async_computation.1 | async-start | bytes 69120000 | tf_op jit(solution)/shard_map/all_gather | solution.py:63
  94.7 1751.8 %all-gather.10.cloned.1.call-start = ((), (), s32[]{:S(2)}) async-start(), calls=%async_computation.2 | async-start | bytes 7372800 | tf_op jit(solution)/shard_map/all_gather | solution.py:152
  212.7 1374.0 %copy-start.20 = (f32[1600]{0:T(1024)}, f32[1600]{0:T(1024)S(1)}, u32[]{:S(2)}) copy-start(f32[1600]{0:T(1024)S(1)} %get-tuple-element.436) | copy-start | bytes 19204
  212.7 1374.0 %copy-start.24 = (f32[1600]{0:T(1024)}, f32[1600]{0:T(1024)S(1)}, u32[]{:S(2)}) copy-start(f32[1600]{0:T(1024)S(1)} %get-tuple-element.435) | copy-start | bytes 19204
  213.0 1373.7 %copy-start.26 = (f32[128]{0:T(128)}, f32[128]{0:T(128)S(1)}, u32[]{:S(2)}) copy-start(f32[128]{0:T(128)S(1)} %broadcast_multiply_fusion.1) | copy-start | bytes 1540
  213.2 1373.5 %copy-start.31 = (f32[128]{0:T(128)}, f32[128]{0:T(128)S(1)}, u32[]{:S(2)}) copy-start(f32[128]{0:T(128)S(1)} %fusion.122) | copy-start | bytes 1540
  1600.0 1298.5 %reduce-scatter.8.cloned.1.call-start = ((), (), s32[]{:S(2)}) async-start(), calls=%async_computation.4 | async-start | bytes 76800000
  1948.9 24.0 collective-permute-start
  1949.5 40.1 %collective-permute-start.1 = (bf16[1,128,2,25,64]{1,4,3,2,0:T(8,128)(2,1)}, bf16[1,128,2,25,64]{1,4,3,2,0:T(8,128)(2,1)}, u32[]{:S(2)}, u32[]{:S(2)}) collective-permute-start(bf16[1,128,2,25,64]{1,4,3,2,0:T(8,128)(2,1)} %get-tuple-element.693), channel_id=1, source_target_pairs={{0,1},{1,2},{2,3},{3,4},{4,5},{5,6},{6,7},{7,0},{8,9},{9,10},{10,1... | collective-permute-start | bytes 2457608 | tf_op jit(solution)/shard_map/while/body/eval_jaxpr/ppermute | solution.py:24
  1991.9 24.1 collective-permute-start
  1991.9 39.8 %collective-permute-start.1 = (bf16[1,128,2,25,64]{1,4,3,2,0:T(8,128)(2,1)}, bf16[1,128,2,25,64]{1,4,3,2,0:T(8,128)(2,1)}, u32[]{:S(2)}, u32[]{:S(2)}) collective-permute-start(bf16[1,128,2,25,64]{1,4,3,2,0:T(8,128)(2,1)} %get-tuple-element.693), channel_id=1, source_target_pairs={{0,1},{1,2},{2,3},{3,4},{4,5},{5,6},{6,7},{7,0},{8,9},{9,10},{10,1... | collective-permute-start | bytes 2457608 | tf_op jit(solution)/shard_map/while/body/eval_jaxpr/ppermute | solution.py:24
  2034.0 24.1 collective-permute-start
  2034.0 38.9 %collective-permute-start.1 = (bf16[1,128,2,25,64]{1,4,3,2,0:T(8,128)(2,1)}, bf16[1,128,2,25,64]{1,4,3,2,0:T(8,128)(2,1)}, u32[]{:S(2)}, u32[]{:S(2)}) collective-permute-start(bf16[1,128,2,25,64]{1,4,3,2,0:T(8,128)(2,1)} %get-tuple-element.693), channel_id=1, source_target_pairs={{0,1},{1,2},{2,3},{3,4},{4,5},{5,6},{6,7},{7,0},{8,9},{9,10},{10,1... | collective-permute-start | bytes 2457608 | tf_op jit(solution)/shard_map/while/body/eval_jaxpr/ppermute | solution.py:24
  2075.2 24.1 collective-permute-start
  2075.2 37.9 %collective-permute-start.1 = (bf16[1,128,2,25,64]{1,4,3,2,0:T(8,128)(2,1)}, bf16[1,128,2,25,64]{1,4,3,2,0:T(8,128)(2,1)}, u32[]{:S(2)}, u32[]{:S(2)}) collective-permute-start(bf16[1,128,2,25,64]{1,4,3,2,0:T(8,128)(2,1)} %get-tuple-element.693), channel_id=1, source_target_pairs={{0,1},{1,2},{2,3},{3,4},{4,5},{5,6},{6,7},{7,0},{8,9},{9,10},{10,1... | collective-permute-start | bytes 2457608 | tf_op jit(solution)/shard_map/while/body/eval_jaxpr/ppermute | solution.py:24
  2115.4 24.1 collective-permute-start
  2115.4 37.0 %collective-permute-start.1 = (bf16[1,128,2,25,64]{1,4,3,2,0:T(8,128)(2,1)}, bf16[1,128,2,25,64]{1,4,3,2,0:T(8,128)(2,1)}, u32[]{:S(2)}, u32[]{:S(2)}) collective-permute-start(bf16[1,128,2,25,64]{1,4,3,2,0:T(8,128)(2,1)} %get-tuple-element.693), channel_id=1, source_target_pairs={{0,1},{1,2},{2,3},{3,4},{4,5},{5,6},{6,7},{7,0},{8,9},{9,10},{10,1... | collective-permute-start | bytes 2457608 | tf_op jit(solution)/shard_map/while/body/eval_jaxpr/ppermute | solution.py:24
  2154.7 24.1 collective-permute-start
  2154.7 36.1 %collective-permute-start.1 = (bf16[1,128,2,25,64]{1,4,3,2,0:T(8,128)(2,1)}, bf16[1,128,2,25,64]{1,4,3,2,0:T(8,128)(2,1)}, u32[]{:S(2)}, u32[]{:S(2)}) collective-permute-start(bf16[1,128,2,25,64]{1,4,3,2,0:T(8,128)(2,1)} %get-tuple-element.693), channel_id=1, source_target_pairs={{0,1},{1,2},{2,3},{3,4},{4,5},{5,6},{6,7},{7,0},{8,9},{9,10},{10,1... | collective-permute-start | bytes 2457608 | tf_op jit(solution)/shard_map/while/body/eval_jaxpr/ppermute | solution.py:24
  2193.2 24.1 collective-permute-start
  2193.2 35.2 %collective-permute-start.1 = (bf16[1,128,2,25,64]{1,4,3,2,0:T(8,128)(2,1)}, bf16[1,128,2,25,64]{1,4,3,2,0:T(8,128)(2,1)}, u32[]{:S(2)}, u32[]{:S(2)}) collective-permute-start(bf16[1,128,2,25,64]{1,4,3,2,0:T(8,128)(2,1)} %get-tuple-element.693), channel_id=1, source_target_pairs={{0,1},{1,2},{2,3},{3,4},{4,5},{5,6},{6,7},{7,0},{8,9},{9,10},{10,1... | collective-permute-start | bytes 2457608 | tf_op jit(solution)/shard_map/while/body/eval_jaxpr/ppermute | solution.py:24
  2230.6 134.1 %collective-permute-start.2 = (bf16[1,128,2,25,64]{1,4,3,2,0:T(8,128)(2,1)}, bf16[1,128,2,25,64]{1,4,3,2,0:T(8,128)(2,1)S(1)}, u32[]{:S(2)}, u32[]{:S(2)}) collective-permute-start(bf16[1,128,2,25,64]{1,4,3,2,0:T(8,128)(2,1)} %get-tuple-element.327), channel_id=1, source_target_pairs={{0,1},{1,2},{2,3},{3,4},{4,5},{5,6},{6,7},{7,0},{8,9},{9,10},{10,1... | collective-permute-start | bytes 2457608 | tf_op jit(solution)/shard_map/ppermute | solution.py:24
  3205.9 2.6 collective-permute-start.3
  (46 other events, 4000.5 us)
Sparse Core Ops, SparseCore 0:
  9.6 56.9 all-gather.11
  94.8 1161.8 all-gather.7
  1600.1 103.0 all-gather.9
  2481.6 416.8 reduce-scatter.7
where the time goes:
time: 3250 us; the launch traced here: 3230 us
  waiting for transfers between devices  1660 us (51%)
  local copies, waits for them, and re-layouts  783 us (24%)
  blocking collectives  472 us (15%)
  matrix products  169 us (5%)
  other arithmetic  120 us (4%)
    all_gather x1, waiting for transfers between devices, gather_params(): lax.all_gather(part[0], 'ctx', axis=1, tiled=True)  1040 us
    unnamed x3, blocking collectives  356 us
    unnamed x6, waiting for transfers between devices  333 us
    slice x1, local copies, waits for them, and re-layouts, unpack_flat(): flat[:first_end].reshape(width, 3 * width)  305 us
    ppermute x15, waiting for transfers between devices, shifted(): return lax.ppermute(value, axis, pairs)  230 us
    all_gather x1, blocking collectives, gather_params(): lax.all_gather(part[1], 'ctx', axis=1, tiled=True)  111 us
    slice x1, local copies, waits for them, and re-layouts, unpack_flat(): flat[second_end:third_end].reshape(width, hidden)  103 us
    slice x1, local copies, waits for them, and re-layouts, unpack_flat(): flat[first_end:second_end].reshape(width, width)  99.2 us
  transfers between devices with their start and end apart: 20, of which 18 were waited for; matrix products, arithmetic and copies ran while one was open for 14% of the time, Pallas kernels for 0%

commit v1 on v0

--- a/solution.py
+++ b/solution.py
@@ -1,6 +1,8 @@
 import jax
 import jax.numpy as jnp
 from jax import lax
+from jax.experimental import pallas as pl
+from jax.experimental.pallas import tpu as pltpu
 from jax.sharding import PartitionSpec as P
 
 HEADS = 25
@@ -98,7 +100,7 @@
     return (first, second, updated)
 
 
-def per_device(
+def per_device_ring(
     inputs, cotangent, slot_order, weights, vectors, first_w, second_w, first_vec, second_vec
 ):
     seqs, rows, width = inputs.shape
@@ -266,6 +268,1038 @@
     return (outputs, input_grad, new_w[0], new_w[1], new_w[2], new_vec[0], new_vec[1], new_vec[2])
 
 
+MEMBERS = 8
+GROUPS = 4
+DEVICES = MEMBERS * GROUPS
+MESH = pl.DeviceIdType.MESH
+SLOTS = 4
+VMEM_BYTES = 60 * 1024 * 1024
+OUT_FIRST = 24
+FC_FIRST = 32
+PROJ_FIRST = 64
+
+
+def head_start(member):
+    return HEADS * member // MEMBERS
+
+
+class Place:
+    def __init__(self):
+        self.fsdp, self.ctx = lax.axis_index("fsdp"), lax.axis_index("ctx")
+        self.x, self.core = self.fsdp // 2, self.fsdp % 2
+        self.far, self.near, self.y = self.ctx // 4, self.ctx // 2 % 2, self.ctx % 2
+        self.me = self.member()
+        self.group = 2 * self.y + self.far
+        self.linear = self.fsdp * MEMBERS + self.ctx
+
+    def member(self, x=None, near=None, core=None):
+        x = self.x if x is None else x
+        near = self.near if near is None else near
+        core = self.core if core is None else core
+        return 4 * core + 2 * near + x
+
+    def target(self, x=None, core=None, far=None, near=None, y=None):
+        x = self.x if x is None else x
+        near = self.near if near is None else near
+        core = self.core if core is None else core
+        far = self.far if far is None else far
+        y = self.y if y is None else y
+        return (2 * x + core, 4 * far + 2 * near + y)
+
+    def is_me(self, target):
+        return jnp.logical_and(target[0] == self.fsdp, target[1] == self.ctx)
+
+
+def greet_all(place):
+    barrier = pltpu.get_barrier_semaphore()
+
+    def one(step, carry):
+        other = (place.linear + step) % DEVICES
+        pl.semaphore_signal(
+            barrier, inc=1, device_id=(other // MEMBERS, other % MEMBERS), device_id_type=MESH
+        )
+        return carry
+
+    lax.fori_loop(1, DEVICES, one, 0)
+    pl.semaphore_wait(barrier, DEVICES - 1)
+
+
+def greet(targets):
+    barrier = pltpu.get_barrier_semaphore()
+    for target in targets:
+        pl.semaphore_signal(barrier, inc=1, device_id=target, device_id_type=MESH)
+    pl.semaphore_wait(barrier, len(targets))
+
+
+def remote(source, landing, sems, index, target):
+    return pltpu.make_async_remote_copy(
+        src_ref=source,
+        dst_ref=landing,
+        send_sem=sems.at[0, index],
+        recv_sem=sems.at[1, index],
+        device_id=target,
+        device_id_type=MESH,
+    )
+
+
+def arrived(landing, sem):
+    pltpu.make_async_copy(landing, landing, sem).wait()
+
+
+class Move:
+    def __init__(self, place, source, landing, send_sem, recv_sem, target, valid=None):
+        here = place.is_me(target)
+        away = jnp.logical_not(here)
+        if valid is not None:
+            here, away = jnp.logical_and(here, valid), jnp.logical_and(away, valid)
+        self.away = away
+        self.copy = pltpu.make_async_remote_copy(
+            src_ref=source,
+            dst_ref=landing,
+            send_sem=send_sem,
+            recv_sem=recv_sem,
+            device_id=target,
+            device_id_type=MESH,
+        )
+
+        @pl.when(here)
+        def _():
+            pltpu.make_async_copy(source, landing, recv_sem).start()
+
+        @pl.when(away)
+        def _():
+            self.copy.start()
+
+    def sent(self):
+        @pl.when(self.away)
+        def _():
+            self.copy.wait_send()
+
+
+class Gather:
+    def __init__(self, place, out, sems):
+        p = place
+        step, turn = 1 - p.core, p.core
+        x1, near1 = p.x + step * (1 - 2 * p.x), p.near + turn * (1 - 2 * p.near)
+        x2, near2 = p.x + turn * (1 - 2 * p.x), p.near + step * (1 - 2 * p.near)
+        self.out, self.sems, self.me = out, sems, p.me
+        self.first = p.target(x=x1, near=near1)
+        self.second = p.target(x=x2, near=near2)
+        self.other = p.target(core=1 - p.core)
+        self.of_first = p.member(x=x1, near=near1)
+        self.of_second = p.member(x=x2, near=near2)
+        self.of_both = p.member(x=1 - p.x, near=1 - p.near)
+        self.copies = {}
+
+    def _go(self, name, index, block, target):
+        item = remote(self.out.at[block], self.out.at[block], self.sems, index, target)
+        item.start()
+        self.copies[name] = item
+
+    def begin(self):
+        self._go("a", 0, self.me, self.first)
+        self._go("b", 1, self.me, self.second)
+        self._go("c", 2, self.me, self.other)
+
+    def second_hop(self):
+        self.copies["a"].wait_recv()
+        self._go("d", 3, self.of_first, self.second)
+        self._go("e", 4, self.of_first, self.other)
+
+    def third_hop(self):
+        self.copies["b"].wait_recv()
+        self._go("f", 5, self.of_second, self.other)
+
+    def last_hop(self):
+        self.copies["d"].wait_recv()
+        self._go("g", 6, self.of_both, self.other)
+
+    def finish(self):
+        for name in "cefg":
+            self.copies[name].wait_recv()
+        for item in self.copies.values():
+            item.wait_send()
+
+
+class Spread:
+    def __init__(self, place, at, sems, first):
+        p = place
+        self.at, self.sems, self.first = at, sems, first
+        self.mine, self.theirs = at(p.far, p.y), at(1 - p.far, p.y)
+        self.to_far, self.to_y = p.target(far=1 - p.far), p.target(y=1 - p.y)
+
+    def begin(self):
+        self.a = remote(self.mine, self.mine, self.sems, self.first, self.to_far)
+        self.b = remote(self.mine, self.mine, self.sems, self.first + 1, self.to_y)
+        self.a.start()
+        self.b.start()
+
+    def middle(self):
+        self.a.wait_recv()
+        self.c = remote(self.theirs, self.theirs, self.sems, self.first + 2, self.to_y)
+        self.c.start()
+
+    def finish(self):
+        self.b.wait_recv()
+        self.c.wait_recv()
+        for item in (self.a, self.b, self.c):
+            item.wait_send()
+
+
+def shard_of(third):
+    shard = third // 3
+    return (shard // MEMBERS, shard % MEMBERS), third % 3
+
+
+def intake_kernel(
+    x_in, back_in, order_in, vec_in, qkv_in, fc_in, rows_in,
+    x_all, back_all, order, vec_all, qkv, fc, proj, out,
+    move_sem, qkv_sem, fc_send, fc_recv, rows_sem, x_sem, back_sem, out_sem, spread_sem, tree_sem,
+):
+    p = Place()
+    greet_all(p)
+    home = p.target(
+        x=p.ctx % 2, near=p.ctx // 2 % 2, core=p.ctx // 4, y=p.fsdp // 2, far=p.fsdp % 2
+    )
+    home_member = p.ctx
+    x_move = Move(
+        p, x_in, x_all.at[home_member], move_sem.at[0, 0], move_sem.at[1, 0], home
+    )
+    order_move = Move(p, order_in, order, move_sem.at[0, 1], move_sem.at[1, 1], home)
+    owner = p.fsdp == 0
+    qkv_moves = []
+    for member in (1, 0, 3, 2, 5, 4, 7, 6):
+        target = p.target(x=member % 2, near=member // 2 % 2, core=member // 4)
+        qkv_moves.append(
+            Move(
+                p, qkv_in.at[member], qkv.at[p.far, p.near, p.y],
+                qkv_sem.at[0, member], qkv_sem.at[1, p.near], target, owner,
+            )
+        )
+    def vec_copy(step):
+        other = (p.linear + step) % DEVICES
+        return pltpu.make_async_remote_copy(
+            src_ref=vec_in,
+            dst_ref=vec_all.at[p.linear],
+            send_sem=move_sem.at[0, 2],
+            recv_sem=move_sem.at[1, 2],
+            device_id=(other // MEMBERS, other % MEMBERS),
+            device_id_type=MESH,
+        )
+
+    def vec_send(step, carry):
+        vec_copy(step).start()
+        return carry
+
+    lax.fori_loop(1, DEVICES, vec_send, 0)
+    pltpu.make_async_copy(vec_in, vec_all.at[p.linear], move_sem.at[1, 2]).start()
+
+    arrived(x_all.at[p.me], move_sem.at[1, 0])
+    gather_x = Gather(p, x_all, x_sem)
+    gather_x.begin()
+    back_move = Move(
+        p, back_in, back_all.at[home_member], move_sem.at[0, 3], move_sem.at[1, 3], home
+    )
+    spreads = []
+    for near in range(2):
+        spreads.append(
+            Spread(p, lambda far, y, near=near: qkv.at[far, near, y], spread_sem, 3 * near)
+        )
+    for near in range(2):
+        arrived(qkv.at[p.far, near, p.y], qkv_sem.at[1, near])
+        spreads[near].begin()
+    gather_x.second_hop()
+    gather_x.third_hop()
+    fc_moves, rows_moves = [], []
+    for part in range(3):
+        third = 3 * p.linear + part
+        unit = third - FC_FIRST
+        valid = jnp.logical_and(unit >= 0, third < PROJ_FIRST)
+        unit = jnp.where(valid, unit, 0)
+        ctx, slot = unit // 4, unit % 4
+        far, near, y = ctx // 4, ctx // 2 % 2, ctx % 2
+        for member in (1, 0, 3, 2, 5, 4, 7, 6):
+            target = p.target(
+                x=member % 2, near=member // 2 % 2, core=member // 4, far=far, y=y
+            )
+            fc_moves.append(
+                Move(
+                    p, fc_in.at[part, member], fc.at[far, near, y, slot],
+                    fc_send.at[part, member], fc_recv.at[4 * near + slot], target, valid,
+                )
+            )
+    for part in range(3):
+        third = 3 * p.linear + part
+        valid = third >= PROJ_FIRST
+        unit = jnp.where(valid, third - PROJ_FIRST, 0)
+        member, group = unit // 4, unit % 4
+        target = p.target(
+            x=member % 2, near=member // 2 % 2, core=member // 4, y=group // 2, far=group % 2
+        )
+        rows_moves.append(
+            Move(
+                p, rows_in.at[part], proj.at[group // 2, group % 2],
+                rows_sem.at[0, part], rows_sem.at[1, 0], target, valid,
+            )
+        )
+        valid = jnp.logical_and(third >= OUT_FIRST, third < FC_FIRST)
+        member = jnp.where(valid, third - OUT_FIRST, 0)
+        group = member % 4
+        target = p.target(
+            x=member % 2, near=member // 2 % 2, core=member // 4, y=group // 2, far=group % 2
+        )
+        rows_moves.append(
+            Move(
+                p, rows_in.at[part], out.at[member],
+                rows_sem.at[0, part], rows_sem.at[1, 1], target, valid,
+            )
+        )
+    gather_x.last_hop()
+    for near in range(2):
+        spreads[near].middle()
+    arrived(back_all.at[p.me], move_sem.at[1, 3])
+    gather_back = Gather(p, back_all, back_sem)
+    gather_back.begin()
+    for near in range(2):
+        for slot in range(4):
+            arrived(fc.at[p.far, near, p.y, slot], fc_recv.at[4 * near + slot])
+        item = Spread(p, lambda far, y, near=near: fc.at[far, near, y], spread_sem, 6 + 3 * near)
+        item.begin()
+        spreads.append(item)
+    root_y, root_far = p.me % 4 // 2, p.me % 2
+    same_y, same_far = p.y == root_y, p.far == root_far
+    mine = out.at[p.me]
+    to_far, to_y = p.target(far=1 - p.far), p.target(y=1 - p.y)
+    root = jnp.logical_and(same_y, same_far)
+    beside = jnp.logical_and(same_y, jnp.logical_not(same_far))
+    opposite = jnp.logical_not(same_y)
+    over_far = remote(mine, mine, tree_sem, 0, to_far)
+    over_y = remote(mine, mine, tree_sem, 1, to_y)
+
+    @pl.when(root)
+    def _():
+        arrived(mine, rows_sem.at[1, 1])
+        over_far.start()
+        over_y.start()
+
+    arrived(proj.at[p.y, p.far], rows_sem.at[1, 0])
+    item = Spread(p, lambda far, y: proj.at[y, far], spread_sem, 12)
+    item.begin()
+    spreads.append(item)
+    gather_back.second_hop()
+    gather_back.third_hop()
+    gather_back.last_hop()
+    for item in spreads[2:4]:
+        item.middle()
+
+    @pl.when(beside)
+    def _():
+        over_far.wait_recv()
+        over_y.start()
+
+    @pl.when(opposite)
+    def _():
+        over_y.wait_recv()
+
+    gather_out = Gather(p, out, out_sem)
+    gather_out.begin()
+    spreads[4].middle()
+    gather_out.second_hop()
+    gather_out.third_hop()
+    gather_out.last_hop()
+    for item in (gather_x, gather_back, gather_out):
+        item.finish()
+    for item in spreads:
+        item.finish()
+
+    @pl.when(root)
+    def _():
+        over_far.wait_send()
+
+    @pl.when(same_y)
+    def _():
+        over_y.wait_send()
+
+    for item in [x_move, order_move, back_move] + qkv_moves + fc_moves + rows_moves:
+        item.sent()
+    arrived(order, move_sem.at[1, 1])
+    arrived(vec_all, move_sem.at[1, 2])
+    sent = vec_all.at[pl.ds(1, DEVICES - 1)]
+    arrived(sent, move_sem.at[0, 2])
+
+
+def intake(x, back, order, vectors, qkv_pieces, fc_pieces, row_blocks):
+    rows, width = x.shape
+    low = jnp.bfloat16
+    _, four, wide = qkv_pieces.shape
+    _, _, unit, hidden = fc_pieces.shape
+    any_space = pl.BlockSpec(memory_space=pl.ANY)
+
+    def like(*shape, kind=low):
+        return jax.ShapeDtypeStruct(shape, kind)
+
+    return pl.pallas_call(
+        intake_kernel,
+        out_shape=[
+            like(MEMBERS, rows, width),
+            like(MEMBERS, rows, width),
+            like(*order.shape, kind=order.dtype),
+            like(DEVICES, *vectors.shape),
+            like(2, 2, 2, four, wide),
+            like(2, 2, 2, 4, unit, hidden),
+            like(2, 2, four, width),
+            like(MEMBERS, four, width),
+        ],
+        in_specs=[any_space] * 7,
+        out_specs=[any_space] * 8,
+        scratch_shapes=[
+            pltpu.SemaphoreType.DMA((2, 4)),
+            pltpu.SemaphoreType.DMA((2, 8)),
+            pltpu.SemaphoreType.DMA((3, 8)),
+            pltpu.SemaphoreType.DMA((8,)),
+            pltpu.SemaphoreType.DMA((2, 3)),
+            pltpu.SemaphoreType.DMA((2, 7)),
+            pltpu.SemaphoreType.DMA((2, 7)),
+            pltpu.SemaphoreType.DMA((2, 7)),
+            pltpu.SemaphoreType.DMA((2, 15)),
+            pltpu.SemaphoreType.DMA((2, 2)),
+        ],
+        compiler_params=pltpu.CompilerParams(collective_id=1, has_side_effects=True),
+        name="intake",
+    )(x, back, order, vectors, qkv_pieces, fc_pieces, row_blocks)
+
+
+def gather_kernel(own, out, local_sem, sems):
+    p = Place()
+    item = Gather(p, out, sems)
+    greet((item.first, item.second, item.other))
+    for name, index, target in (("a", 0, item.first), ("b", 1, item.second), ("c", 2, item.other)):
+        copy = remote(own, out.at[p.me], sems, index, target)
+        copy.start()
+        item.copies[name] = copy
+    local = pltpu.make_async_copy(own, out.at[p.me], local_sem)
+    local.start()
+    item.second_hop()
+    item.third_hop()
+    item.last_hop()
+    item.finish()
+    local.wait()
+
+
+def group_gather(value, ident):
+    any_space = pl.BlockSpec(memory_space=pl.ANY)
+    return pl.pallas_call(
+        gather_kernel,
+        out_shape=jax.ShapeDtypeStruct((MEMBERS,) + value.shape, value.dtype),
+        in_specs=[any_space],
+        out_specs=any_space,
+        scratch_shapes=[pltpu.SemaphoreType.DMA, pltpu.SemaphoreType.DMA((2, 7))],
+        compiler_params=pltpu.CompilerParams(collective_id=ident, has_side_effects=True),
+        name="group_gather",
+    )(value)
+
+
+def scatter_kernel(part, out, from_core, sums, two, got, last, done, sems):
+    p = Place()
+    route = Gather(p, None, None)
+    greet((route.first, route.second, route.other))
+    copies = []
+    for j in (3, 2, 1, 0):
+        item = remote(part.at[4 * (1 - p.core) + j], from_core.at[j], sems, j, route.other)
+        item.start()
+        copies.append(item)
+    mine = 4 * p.core
+    here, there = p.me - mine, route.of_first - mine
+    beyond, across = route.of_second - mine, route.of_both - mine
+    for item in copies:
+        item.wait_recv()
+
+    def summed(block):
+        return part[mine + block].astype(jnp.float32) + from_core[block].astype(jnp.float32)
+
+    two[0] = summed(across).astype(jnp.bfloat16)
+    send_across = remote(two.at[0], got.at[0], sems, 4, route.second)
+    send_across.start()
+    two[1] = summed(beyond).astype(jnp.bfloat16)
+    send_beyond = remote(two.at[1], got.at[1], sems, 5, route.second)
+    send_beyond.start()
+    sums[...] = summed(there)
+    send_across.wait_recv()
+    last[...] = (sums[...] + got[0].astype(jnp.float32)).astype(jnp.bfloat16)
+    send_last = remote(last, done, sems, 6, route.first)
+    send_last.start()
+    sums[...] = summed(here)
+    send_beyond.wait_recv()
+    sums[...] += got[1].astype(jnp.float32)
+    send_last.wait_recv()
+    out[...] = sums[...] + done[...].astype(jnp.float32)
+    for item in copies + [send_across, send_beyond, send_last]:
+        item.wait_send()
+
+
+def group_scatter(value, ident):
+    rows, width = value.shape
+    rows = rows // MEMBERS
+    low = jnp.bfloat16
+    vmem = pl.BlockSpec(memory_space=pltpu.VMEM)
+    return pl.pallas_call(
+        scatter_kernel,
+        out_shape=jax.ShapeDtypeStruct((rows, width), jnp.float32),
+        in_specs=[vmem],
+        out_specs=vmem,
+        scratch_shapes=[
+            pltpu.VMEM((4, rows, width), low),
+            pltpu.VMEM((rows, width), jnp.float32),
+            pltpu.VMEM((2, rows, width), low),
+            pltpu.VMEM((2, rows, width), low),
+            pltpu.VMEM((rows, width), low),
+            pltpu.VMEM((rows, width), low),
+            pltpu.SemaphoreType.DMA((2, 7)),
+        ],
+        compiler_params=pltpu.CompilerParams(
+            collective_id=ident, has_side_effects=True, vmem_limit_bytes=VMEM_BYTES
+        ),
+        name="group_scatter",
+    )(value.reshape(MEMBERS, rows, width))
+
+
+def wide(value):
+    return value.astype(jnp.float32)
+
+
+def low(value):
+    return value.astype(jnp.bfloat16)
+
+
+class Fold:
+    def __init__(self, place, at, landing, leaving, last, sems, first):
+        p = place
+        self.p, self.at, self.landing, self.leaving, self.last = p, at, landing, leaving, last
+        self.to_far, self.to_y = p.target(far=1 - p.far), p.target(y=1 - p.y)
+        self.sems, self.first = sems, first
+
+    def begin(self):
+        p = self.p
+        other = 1 - p.far
+        self.a = remote(
+            self.at(other, 1 - p.y), self.landing(other), self.sems, self.first, self.to_y
+        )
+        self.b = remote(
+            self.at(p.far, 1 - p.y), self.landing(p.far), self.sems, self.first + 1, self.to_y
+        )
+        self.a.start()
+        self.b.start()
+
+    def middle(self):
+        p = self.p
+        other = 1 - p.far
+        self.a.wait_recv()
+        self.leaving[...] = low(wide(self.at(other, p.y)[...]) + wide(self.landing(other)[...]))
+        self.c = remote(self.leaving, self.last, self.sems, self.first + 2, self.to_far)
+        self.c.start()
+
+    def end(self):
+        p = self.p
+        self.b.wait_recv()
+        partial = wide(self.at(p.far, p.y)[...]) + wide(self.landing(p.far)[...])
+        self.c.wait_recv()
+        return low(partial + wide(self.last[...]))
+
+    def sent(self):
+        for item in (self.a, self.b, self.c):
+            item.wait_send()
+
+
+def yield_kernel(
+    qkv, fc, proj, out, vec,
+    qkv_back, fc_back, rows_back, vec_back,
+    qkv_y, fc_y, proj_y, out_y, qkv_go, fc_go, proj_go, out_go,
+    qkv_far, fc_far, proj_far, out_far, qkv_sum, fc_sum, proj_sum, out_sum, vec_got,
+    fold_sem, tree_sem, vec_sem, qkv_send, qkv_recv, fc_send, fc_recv, rows_send, rows_recv,
+):
+    p = Place()
+    unit = fc_back.shape[2]
+    greet_all(p)
+    folds = [
+        Fold(
+            p, lambda far, y: proj.at[y, far], lambda far: proj_y.at[far],
+            proj_go, proj_far, fold_sem, 0,
+        )
+    ]
+    for near in range(2):
+        folds.append(
+            Fold(
+                p, lambda far, y, near=near: fc.at[far, near, y],
+                lambda far, near=near: fc_y.at[far, near],
+                fc_go.at[near], fc_far.at[near], fold_sem, 3 + 3 * near,
+            )
+        )
+    for near in range(2):
+        folds.append(
+            Fold(
+                p, lambda far, y, near=near: qkv.at[far, near, y],
+                lambda far, near=near: qkv_y.at[far, near],
+                qkv_go.at[near], qkv_far.at[near], fold_sem, 9 + 3 * near,
+            )
+        )
+    for item in folds:
+        item.begin()
+    root_y, root_far = p.me % 4 // 2, p.me % 2
+    same_y, same_far = p.y == root_y, p.far == root_far
+    root = jnp.logical_and(same_y, same_far)
+    beside = jnp.logical_and(same_y, jnp.logical_not(same_far))
+    over_y = remote(out, out_y, tree_sem, 0, p.target(y=1 - p.y))
+    over_far = remote(out_go, out_far, tree_sem, 1, p.target(far=1 - p.far))
+
+    @pl.when(jnp.logical_not(same_y))
+    def _():
+        over_y.start()
+
+    def vec_copy(step):
+        other = (p.linear + step) % DEVICES
+        return pltpu.make_async_remote_copy(
+            src_ref=vec.at[other],
+            dst_ref=vec_got.at[p.linear],
+            send_sem=vec_sem.at[0],
+            recv_sem=vec_sem.at[1],
+            device_id=(other // MEMBERS, other % MEMBERS),
+            device_id_type=MESH,
+        )
+
+    def vec_send(step, carry):
+        vec_copy(step).start()
+        return carry
+
+    lax.fori_loop(1, DEVICES, vec_send, 0)
+    pltpu.make_async_copy(vec.at[p.linear], vec_got.at[p.linear], vec_sem.at[1]).start()
+    for item in folds:
+        item.middle()
+
+    @pl.when(same_y)
+    def _():
+        over_y.wait_recv()
+
+    @pl.when(beside)
+    def _():
+        out_go[...] = low(wide(out[...]) + wide(out_y[...]))
+        over_far.start()
+
+    moves = []
+    proj_sum[...] = folds[0].end()
+    target, part = shard_of(PROJ_FIRST + 4 * p.me + p.group)
+    moves.append(
+        Move(p, proj_sum, rows_back.at[part], rows_send.at[0], rows_recv.at[part], target)
+    )
+    for near in range(2):
+        block = folds[1 + near].end()
+        for slot in range(4):
+            fc_sum[near, slot] = block[slot * unit : (slot + 1) * unit]
+            third = FC_FIRST + 4 * (4 * p.far + 2 * near + p.y) + slot
+            target, part = shard_of(third)
+            moves.append(
+                Move(
+                    p, fc_sum.at[near, slot], fc_back.at[part, p.me],
+                    fc_send.at[near, slot], fc_recv.at[part, p.me], target,
+                )
+            )
+
+    @pl.when(root)
+    def _():
+        over_far.wait_recv()
+        out_sum[...] = low(wide(out[...]) + wide(out_y[...]) + wide(out_far[...]))
+
+    target, part = shard_of(OUT_FIRST + p.me)
+    moves.append(
+        Move(p, out_sum, rows_back.at[part], rows_send.at[1], rows_recv.at[part], target, root)
+    )
+    for near in range(2):
+        qkv_sum[near] = folds[3 + near].end()
+        target = (0 * p.fsdp, 4 * p.far + 2 * near + p.y)
+        moves.append(
+            Move(
+                p, qkv_sum.at[near], qkv_back.at[p.me], qkv_send.at[near], qkv_recv.at[p.me],
+                target,
+            )
+        )
+    @pl.when(p.fsdp == 0)
+    def _():
+        for member in range(MEMBERS):
+            arrived(qkv_back.at[member], qkv_recv.at[member])
+
+    for part in range(3):
+        third = 3 * p.linear + part
+        is_fc = jnp.logical_and(third >= FC_FIRST, third < PROJ_FIRST)
+        is_rows = jnp.logical_and(third >= OUT_FIRST, jnp.logical_not(is_fc))
+
+        @pl.when(is_fc)
+        def _(part=part):
+            for member in range(MEMBERS):
+                arrived(fc_back.at[part, member], fc_recv.at[part, member])
+
+        @pl.when(is_rows)
+        def _(part=part):
+            arrived(rows_back.at[part], rows_recv.at[part])
+
+    arrived(vec_got, vec_sem.at[1])
+    vec_back[...] = jnp.sum(vec_got[...], 0)
+    arrived(vec_got.at[pl.ds(1, DEVICES - 1)], vec_sem.at[0])
+    for item in folds:
+        item.sent()
+
+    @pl.when(jnp.logical_not(same_y))
+    def _():
+        over_y.wait_send()
+
+    @pl.when(beside)
+    def _():
+        over_far.wait_send()
+
+    for item in moves:
+        item.sent()
+
+
+def yield_grads(qkv, fc, proj, out, vec):
+    kind = jnp.bfloat16
+    four, wide_qkv = qkv.shape[-2:]
+    hidden = fc.shape[-1]
+    width = proj.shape[-1]
+    unit = four // 4
+    any_space = pl.BlockSpec(memory_space=pl.ANY)
+    vmem = pl.BlockSpec(memory_space=pltpu.VMEM)
+
+    def buffer(*shape, dtype=kind):
+        return pltpu.VMEM(shape, dtype)
+
+    dma = pltpu.SemaphoreType.DMA
+    return pl.pallas_call(
+        yield_kernel,
+        out_shape=[
+            jax.ShapeDtypeStruct((MEMBERS, four, wide_qkv), kind),
+            jax.ShapeDtypeStruct((3, MEMBERS, unit, hidden), kind),
+            jax.ShapeDtypeStruct((3, four, width), kind),
+            jax.ShapeDtypeStruct(vec.shape[1:], vec.dtype),
+        ],
+        in_specs=[vmem] * 5,
+        out_specs=[any_space, any_space, any_space, vmem],
+        scratch_shapes=[
+            buffer(2, 2, four, wide_qkv),
+            buffer(2, 2, four, hidden),
+            buffer(2, four, width),
+            buffer(four, width),
+            buffer(2, four, wide_qkv),
+            buffer(2, four, hidden),
+            buffer(four, width),
+            buffer(four, width),
+            buffer(2, four, wide_qkv),
+            buffer(2, four, hidden),
+            buffer(four, width),
+            buffer(four, width),
+            buffer(2, four, wide_qkv),
+            buffer(2, 4, unit, hidden),
+            buffer(four, width),
+            buffer(four, width),
+            buffer(*vec.shape, dtype=vec.dtype),
+            dma((2, 15)),
+            dma((2, 2)),
+            dma((2,)),
+            dma((2,)),
+            dma((8,)),
+            dma((2, 4)),
+            dma((3, 8)),
+            dma((2,)),
+            dma((3,)),
+        ],
+        compiler_params=pltpu.CompilerParams(
+            collective_id=2, has_side_effects=True, vmem_limit_bytes=VMEM_BYTES
+        ),
+        name="yield_grads",
+    )(qkv, fc, proj, out, vec)
+
+
+def lane_of(shape):
+    return lax.broadcasted_iota(jnp.int32, shape, 1) // HD
+
+
+def dot_nt(a, b):
+    return lax.dot_general(a, b, (((1,), (1,)), ((), ())), preferred_element_type=jnp.float32)
+
+
+def dot_tn(a, b):
+    return lax.dot_general(a, b, (((0,), (0,)), ((), ())), preferred_element_type=jnp.float32)
+
+
+def probabilities(query, keys, row_pos, col_pos):
+    scores = dot_nt(query, keys) * 0.125
+    scores = jnp.where(col_pos <= row_pos, scores, -1e30)
+    weights = jnp.exp(scores - jnp.max(scores, -1, keepdims=True))
+    return weights / jnp.sum(weights, -1, keepdims=True)
+
+
+def attend_kernel(query, keys, values, row_pos, col_pos, out):
+    lanes = lane_of(query.shape)
+    result = jnp.zeros(query.shape, jnp.float32)
+    for head in range(2):
+        mine = lanes == head
+        own = jnp.where(mine, query[...], jnp.zeros_like(query))
+        probs = probabilities(own, keys[...], row_pos[...], col_pos[...])
+        mixed = jnp.dot(
+            probs.astype(jnp.bfloat16), values[...], preferred_element_type=jnp.float32
+        )
+        result = jnp.where(mine, mixed, result)
+    out[...] = result.astype(jnp.bfloat16)
+
+
+def attend_back_kernel(
+    query, keys, values, grad, row_pos, col_pos, dquery, dkeys, dvalues, key_sum, value_sum
+):
+    step = pl.program_id(1)
+
+    @pl.when(step == 0)
+    def _():
+        key_sum[...] = jnp.zeros_like(key_sum)
+        value_sum[...] = jnp.zeros_like(value_sum)
+
+    lanes = lane_of(query.shape)
+    result = jnp.zeros(query.shape, jnp.float32)
+    add_keys = add_values = 0.0
+    for head in range(2):
+        mine = lanes == head
+        own = jnp.where(mine, query[...], jnp.zeros_like(query))
+        own_grad = jnp.where(mine, grad[...], jnp.zeros_like(grad))
+        probs = probabilities(own, keys[...], row_pos[...], col_pos[...])
+        dprobs = dot_nt(own_grad, values[...])
+        delta = jnp.sum(probs * dprobs, -1, keepdims=True)
+        dscores = (probs * (dprobs - delta)).astype(jnp.bfloat16)
+        mixed = jnp.dot(dscores, keys[...], preferred_element_type=jnp.float32)
+        result = jnp.where(mine, mixed, result)
+        add_keys = add_keys + dot_tn(dscores, own)
+        add_values = add_values + dot_tn(probs.astype(jnp.bfloat16), own_grad)
+    dquery[...] = (result * 0.125).astype(jnp.bfloat16)
+    key_sum[...] += add_keys
+    value_sum[...] += add_values
+
+    @pl.when(step == pl.num_programs(1) - 1)
+    def _():
+        dkeys[...] = (key_sum[...] * 0.125).astype(jnp.bfloat16)
+        dvalues[...] = value_sum[...].astype(jnp.bfloat16)
+
+
+def attend(qkv, row_pos, col_pos, span):
+    length = qkv.shape[0]
+    wide = 2 * HD
+    return pl.pallas_call(
+        attend_kernel,
+        grid=(SLOTS // 2, length // span),
+        in_specs=[
+            pl.BlockSpec((span, wide), lambda h, i: (i, h)),
+            pl.BlockSpec((length, wide), lambda h, i: (0, SLOTS // 2 + h)),
+            pl.BlockSpec((length, wide), lambda h, i: (0, SLOTS + h)),
+            pl.BlockSpec((span, 1), lambda h, i: (i, 0)),
+            pl.BlockSpec((1, length), lambda h, i: (0, 0)),
+        ],
+        out_specs=pl.BlockSpec((span, wide), lambda h, i: (i, h)),
+        out_shape=jax.ShapeDtypeStruct((length, SLOTS * HD), jnp.bfloat16),
+        compiler_params=pltpu.CompilerParams(vmem_limit_bytes=VMEM_BYTES),
+        name="attend",
+    )(qkv, qkv, qkv, row_pos, col_pos)
+
+
+def attend_back(qkv, grad, row_pos, col_pos, span):
+    length = qkv.shape[0]
+    wide = 2 * HD
+    whole = jax.ShapeDtypeStruct((length, SLOTS * HD), jnp.bfloat16)
+    return pl.pallas_call(
+        attend_back_kernel,
+        grid=(SLOTS // 2, length // span),
+        in_specs=[
+            pl.BlockSpec((span, wide), lambda h, i: (i, h)),
+            pl.BlockSpec((length, wide), lambda h, i: (0, SLOTS // 2 + h)),
+            pl.BlockSpec((length, wide), lambda h, i: (0, SLOTS + h)),
+            pl.BlockSpec((span, wide), lambda h, i: (i, h)),
+            pl.BlockSpec((span, 1), lambda h, i: (i, 0)),
+            pl.BlockSpec((1, length), lambda h, i: (0, 0)),
+        ],
+        out_specs=[
+            pl.BlockSpec((span, wide), lambda h, i: (i, h)),
+            pl.BlockSpec((length, wide), lambda h, i: (0, h)),
+            pl.BlockSpec((length, wide), lambda h, i: (0, h)),
+        ],
+        out_shape=[whole, whole, whole],
+        scratch_shapes=[
+            pltpu.VMEM((length, wide), jnp.float32),
+            pltpu.VMEM((length, wide), jnp.float32),
+        ],
+        compiler_params=pltpu.CompilerParams(vmem_limit_bytes=VMEM_BYTES),
+        name="attend_back",
+    )(qkv, qkv, qkv, grad, row_pos, col_pos)
+
+
+def head_columns(rows, width):
+    pieces = []
+    for member in range(MEMBERS):
+        first = head_start(member) * HD
+        pieces.append(
+            jnp.concatenate(
+                [
+                    rows[:, part * width + first : part * width + first + SLOTS * HD]
+                    for part in range(3)
+                ],
+                1,
+            )
+        )
+    return jnp.stack(pieces)
+
+
+def own_heads(member):
+    return (head_start(member + 1) - head_start(member)) * HD
+
+
+def all_heads(pieces):
+    return jnp.concatenate([pieces[m][:, : own_heads(m)] for m in range(MEMBERS)], 1)
+
+
+def to_group(value):
+    pairs = []
+    for f in range(GROUPS):
+        for c in range(MEMBERS):
+            core, near, x = c // 4, c // 2 % 2, c % 2
+            y, far = f // 2, f % 2
+            pairs.append((f * MEMBERS + c, (2 * x + core) * MEMBERS + 4 * far + 2 * near + y))
+    return lax.ppermute(value, ("fsdp", "ctx"), pairs)
+
+
+def per_device_groups(
+    inputs, cotangent, slot_order, weights, vectors, first_w, second_w, first_vec, second_vec
+):
+    seqs, rows, width = inputs.shape
+    kind, high = jnp.bfloat16, jnp.float32
+    fsdp, ctx = lax.axis_index("fsdp"), lax.axis_index("ctx")
+    member = 4 * (fsdp % 2) + 2 * (ctx // 2 % 2) + fsdp // 2
+    length = rows * MEMBERS
+    hidden = FF // MEMBERS
+    local = weights.shape[0]
+    third = local // 3
+    unit = width // DEVICES
+    four = 4 * unit
+    per_part = SLOTS * HD
+
+    qkv_pieces = head_columns(weights.reshape(four, 3 * width), width)
+    fc_pieces = weights.reshape(3, unit, MEMBERS, hidden).transpose(0, 2, 1, 3)
+    row_blocks = weights.reshape(3, four, width)
+    order = jnp.pad(slot_order, ((0, 7), (0, 128 - slot_order.shape[1])))
+    vec_rows, vec_cols = vectors.shape
+    padded = jnp.pad(vectors, ((0, 16 - vec_rows), (0, -vec_cols % 128)))
+    x_all, back_all, order, full_vec, own_qkv, own_fc, own_proj, full_out = intake(
+        inputs.reshape(rows, width), cotangent.reshape(rows, width), order, padded,
+        qkv_pieces, fc_pieces, row_blocks,
+    )
+    x_all, back_all = x_all.reshape(length, width), back_all.reshape(length, width)
+    own_qkv = own_qkv.reshape(width, 3 * per_part)
+    own_fc = own_fc.reshape(width, hidden)
+    own_proj = own_proj.reshape(hidden, width)
+    full_out = full_out.reshape(width, width)
+    order = order[0, : slot_order.shape[1]]
+    block = length // order.shape[0]
+    pos = (order[:, None] * block + jnp.arange(block, dtype=jnp.int32)).reshape(-1)
+    row_pos, col_pos = pos[:, None], pos[None, :]
+    full_vec = full_vec[:, :vec_rows, :vec_cols].reshape(GROUPS, MEMBERS, vec_rows, vec_cols)
+    vec = full_vec.transpose(0, 2, 1, 3).reshape(-1, width).astype(high)
+    head_at = HEADS * member // MEMBERS * HD
+    bias_q = lax.dynamic_slice(vec[2], (head_at,), (per_part,))
+    bias_v = lax.dynamic_slice(vec[3], (head_at,), (per_part,))
+    bias_qkv = jnp.concatenate([bias_q, jnp.zeros_like(bias_q), bias_v])
+    bias_fc = lax.dynamic_slice(vec[8:].reshape(-1), (member * hidden,), (hidden,))
+
+    mine = member * rows
+    h_first = layer_norm(x_all.astype(high), vec[0], vec[1]).astype(kind)
+    qkv = jnp.dot(h_first, own_qkv, preferred_element_type=high) + bias_qkv
+    qkv = qkv.astype(kind)
+    span = min(length, 256)
+    attn = attend(qkv, row_pos, col_pos, span)
+    attn_all = all_heads(group_gather(attn, 3))
+    resid = x_all.astype(high) + jnp.dot(attn_all, full_out, preferred_element_type=high) + vec[4]
+    h_second = layer_norm(resid, vec[5], vec[6]).astype(kind)
+    pre = jnp.dot(h_second, own_fc, preferred_element_type=high) + bias_fc
+    act, pull_gelu = jax.vjp(gelu_tanh, pre)
+    act = act.astype(kind)
+    made = group_scatter(jnp.dot(act, own_proj, preferred_element_type=high).astype(kind), 4)
+    resid_own = lax.dynamic_slice_in_dim(resid, mine, rows, 0)
+    outputs = (resid_own + made + vec[7]).astype(kind)
+
+    back_own = lax.dynamic_slice_in_dim(back_all, mine, rows, 0).astype(high)
+    grad_proj = jnp.einsum("tf,td->fd", act, back_all, preferred_element_type=high).astype(kind)
+    grad_bp = jnp.sum(back_own, 0)
+    dact = jnp.einsum("td,fd->tf", back_all, own_proj, preferred_element_type=high)
+    dpre = pull_gelu(dact)[0].astype(kind)
+    grad_fc = jnp.einsum("td,tf->df", h_second, dpre, preferred_element_type=high).astype(kind)
+    grad_bf = jnp.sum(dpre, 0, dtype=high)
+    dh_second = group_scatter(
+        jnp.einsum("tf,df->td", dpre, own_fc, preferred_element_type=high).astype(kind), 4
+    )
+    _, pull_second = jax.vjp(layer_norm, resid_own, vec[5], vec[6])
+    dres_ln, grad_g2, grad_b2 = pull_second(dh_second)
+    dresid = back_own + dres_ln
+    dbranch = dresid.astype(kind)
+    grad_bo = jnp.sum(dbranch, 0, dtype=high)
+    dbranch_all = group_gather(dbranch, 5).reshape(length, width)
+    out_heads = lax.dynamic_slice_in_dim(full_out, head_at, per_part, 0)
+    dattn = jnp.einsum("te,de->td", dbranch_all, out_heads, preferred_element_type=high)
+    dattn = dattn.astype(kind)
+    attn_cols = lax.dynamic_slice_in_dim(attn_all, member * four, four, 1)
+    grad_out = jnp.einsum("td,te->de", attn_cols, dbranch_all, preferred_element_type=high)
+    dqkv = jnp.concatenate(attend_back(qkv, dattn, row_pos, col_pos, span), 1)
+    lane = jnp.arange(per_part)
+    keep = lane < jnp.where(member == MEMBERS - 1, per_part, (SLOTS - 1) * HD)
+    dqkv = jnp.where(jnp.tile(keep, 3), dqkv, jnp.zeros_like(dqkv))
+    grad_qkv = jnp.einsum("td,te->de", h_first, dqkv, preferred_element_type=high).astype(kind)
+    bias_sums = jnp.sum(dqkv, 0, dtype=high)
+    dh_first = group_scatter(
+        jnp.einsum("te,de->td", dqkv, own_qkv, preferred_element_type=high).astype(kind), 4
+    )
+    x_own = lax.dynamic_slice_in_dim(x_all, mine, rows, 0).astype(high)
+    _, pull_first = jax.vjp(layer_norm, x_own, vec[0], vec[1])
+    dx_ln, grad_g1, grad_b1 = pull_first(dh_first)
+    input_grad = (dresid + dx_ln).astype(kind)
+    results = to_group(jnp.concatenate([outputs, input_grad], 1))
+    outputs = results[:, :width].reshape(seqs, rows, width)
+    input_grad = results[:, width:].reshape(seqs, rows, width)
+
+    zero_row = jnp.zeros((width,), high)
+    row_q = lax.dynamic_update_slice(zero_row, bias_sums[:per_part], (head_at,))
+    row_v = lax.dynamic_update_slice(zero_row, bias_sums[2 * per_part :], (head_at,))
+    row_f = lax.dynamic_update_slice(jnp.zeros((FF,), high), grad_bf, (member * hidden,))
+    grad_vec = jnp.concatenate(
+        [
+            jnp.stack([grad_g1, grad_b1, row_q, row_v, grad_bo, grad_g2, grad_b2, grad_bp]),
+            row_f.reshape(-1, width),
+        ],
+        0,
+    )
+    grad_vec = grad_vec.reshape(GROUPS, vec_rows, MEMBERS, vec_cols).transpose(0, 2, 1, 3)
+    grad_vec = grad_vec.reshape(DEVICES, vec_rows, vec_cols)
+    grad_vec = jnp.pad(grad_vec, ((0, 0), (0, 8 - vec_rows), (0, -vec_cols % 128)))
+    qkv_back, fc_back, rows_back, vec_back = yield_grads(
+        grad_qkv.reshape(2, 2, 2, four, 3 * per_part),
+        grad_fc.reshape(2, 2, 2, four, hidden),
+        grad_proj.reshape(2, 2, four, width),
+        grad_out.astype(kind),
+        grad_vec,
+    )
+    qkv_flat = jnp.concatenate(
+        [all_heads(qkv_back[:, :, p * per_part : (p + 1) * per_part]) for p in range(3)], 1
+    ).reshape(local, 128)
+    fc_flat = fc_back.transpose(0, 2, 1, 3).reshape(3, third, 128)
+    rows_flat = rows_back.reshape(3, third, 128)
+    thirds = 3 * (fsdp * MEMBERS + ctx) + jnp.arange(3)
+    is_fc = jnp.logical_and(thirds >= FC_FIRST, thirds < PROJ_FIRST)
+    others = jnp.where(is_fc[:, None, None], fc_flat, rows_flat).reshape(local, 128)
+    owned = jnp.where(fsdp == 0, qkv_flat, others).astype(high)
+    new_w = adamw(weights, owned, first_w, second_w, rate_matrix, weight_decay)
+    owned_vec = vec_back[:vec_rows, :vec_cols]
+    new_vec = adamw(vectors, owned_vec, first_vec, second_vec, rate_vector, 0.0)
+    return (outputs, input_grad, new_w[0], new_w[1], new_w[2], new_vec[0], new_vec[1], new_vec[2])
+
+
 def solution(mesh):
     in_specs = (
         P("fsdp", "ctx", None),
@@ -288,6 +1322,7 @@
         P("fsdp", "ctx"),
         P("fsdp", "ctx"),
     )
+    per_device = per_device_groups if mesh.shape["ctx"] == MEMBERS else per_device_ring
     return jax.shard_map(
         per_device, mesh=mesh, in_specs=in_specs, out_specs=out_specs, check_vma=False
     )

time: 3250 us -> 826 us (0.25)
  the two profiles are of different devices: /device:TPU:0 before, /device:TPU:29 now
where the time goes in v1:
time: 826 us; the launch traced here: 815 us
  Pallas kernels  596 us (72%)
  local copies, waits for them, and re-layouts  109 us (13%)
  matrix products  66.7 us (8%)
  other arithmetic  39 us (5%)
    pallas_call x1, Pallas kernels, intake(): pl.pallas_call(intake_kernel, out_shape=[like(MEMBERS, rows, width), like...  250 us
    pallas_call x1, Pallas kernels, yield_grads(): pl.pallas_call(yield_kernel, out_shape=[jax.ShapeDtypeStruct((MEMBERS, fo...  191 us
    pallas_call x3, Pallas kernels, group_scatter(): pl.pallas_call(scatter_kernel, out_shape=jax.ShapeDtypeStruct((rows, widt...  70.1 us
    pallas_call x2, Pallas kernels, group_gather(): pl.pallas_call(gather_kernel, out_shape=jax.ShapeDtypeStruct((MEMBERS,) +...  49.3 us
    pallas_call x1, Pallas kernels, attend_back(): pl.pallas_call(attend_back_kernel, grid=(SLOTS // 2, length // span), in_...  21.4 us
  transfers between devices with their start and end apart: 1, of which 0 were waited for; matrix products, arithmetic and copies ran while one was open for 9% of the time, Pallas kernels for 23%

profile of v1, /device:TPU:29, one launch (start us, length us, event | category | flops | bytes accessed | tf_op | source)
XLA Modules:
  0.0 814.7 jit_solution(513027264543255933)
XLA Ops:
  27.2 250.4 %intake.1 = (bf16[8,128,1600]{2,1,0:T(8,128)(2,1)}, bf16[8,128,1600]{2,1,0:T(8,128)(2,1)}, s32[8,128]{1,0:T(8,128)}, bf16[32,16,256]{2,1,0:T(8,128)(2,1)}, bf16[...) custom-call(bf16[128,1600]{1,0:T(8,128)(2,1)} %bitcast.209, ...), custom_call_target="tpu_custom_call" | custom-call | tf_op jit(solution)/shard_map/intake/pallas_call | solution.py:641
  299.8 13.7 %attend.1.own = bf16[1024,256]{1,0:T(8,128)(2,1)} custom-call(bf16[1024,768]{1,0:T(8,128)(2,1)} %add_convert_fusion.1.query.keys.values, bf16[1024,768]{1,0:T(8,128)(2,1)} %add_convert_fusion.1.query.keys.values, bf16[1024,768]{1,0:T(8,128)(2,1)} %add_convert_fusion.1.query.keys.values, s32[1024,1]{1,0:T(8,128)} %add.289.row_pos, s32[1,1024]{1,0:T(1,128)} %add.250.col_pos), custom_call_target="tpu_custom_call" | custom-call | tf_op jit(solution)/shard_map/attend/pallas_call | solution.py:1090
  313.5 27.9 %group_gather.2 = bf16[8,1024,256]{2,1,0:T(8,128)(2,1)} custom-call(bf16[1024,256]{1,0:T(8,128)(2,1)} %attend.1.own), custom_call_target="tpu_custom_call" | custom-call | tf_op jit(solution)/shard_map/group_gather/pallas_call | solution.py:691
  345.6 7.0 concatenate.51
  352.5 10.4 %fusion.70 = (f32[1024]{0:T(1024)S(1)}, f32[1024,1600]{1,0:T(8,128)S(1)}) fusion(f32[1600]{0:T(1024)S(1)} %get-tuple-element.145, bf16[1024,1600]{1,0:T(8,128)(2,1)} %concatenate.51, bf16[1600,1600]{1,0:T(8,128)(2,1)} %bitcast.244, bf16[1024,1600]{1,0:T(8,128)(2,1)S(1)} %bitcast.186), kind=kOutput, calls=%fused_computation.175 | convolution fusion | flops 5249432576 | bytes 18237696 | tf_op jit(solution)/shard_map/dot_general | solution.py:1220
  373.4 5.7 convolution_convert_fusion.2
  384.8 4.9 convolution_convert_fusion
  389.7 5.4 copy.33
  395.1 23.6 %group_scatter.4 = f32[128,1600]{1,0:T(8,128)} custom-call(bf16[8,128,1600]{2,1,0:T(8,128)(2,1)} %bitcast.191), custom_call_target="tpu_custom_call" | custom-call | tf_op jit(solution)/shard_map/group_scatter/pallas_call | solution.py:745
  420.6 5.6 copy.32
  426.1 23.4 %group_scatter.3 = f32[128,1600]{1,0:T(8,128)} custom-call(bf16[8,128,1600]{2,1,0:T(8,128)(2,1)} %bitcast.192), custom_call_target="tpu_custom_call" | custom-call | tf_op jit(solution)/shard_map/group_scatter/pallas_call | solution.py:745
  455.2 21.4 %group_gather.3 = bf16[8,128,1600]{2,1,0:T(8,128)(2,1)} custom-call(bf16[128,1600]{1,0:T(8,128)(2,1)} %get-tuple-element.77.own), custom_call_target="tpu_custom_call" | custom-call | tf_op jit(solution)/shard_map/group_gather/pallas_call | solution.py:691
  480.8 21.4 %attend_back.1 = (bf16[1024,256]{1,0:T(8,128)(2,1)}, bf16[1024,256]{1,0:T(8,128)(2,1)}, bf16[1024,256]{1,0:T(8,128)(2,1)}) custom-call(bf16[1024,768]{1,0:T(8,128)(2,1)} %add_convert_fusion.1.query.keys.values, bf16[1024,768]{1,0:T(8,128)(2,1)} %add_convert_fusion.1.query.keys.values, bf16[1024,768]{1,0:T(8,128)(2,1)} %add_convert_fusion.1.query.keys.values, ...), custom_call_target="tpu_custom_call" | custom-call | tf_op jit(solution)/shard_map/attend_back/pallas_call | solution.py:1111
  502.1 6.7 convolution_convert_fusion.1
  508.8 5.4 copy.35
  514.2 23.1 %group_scatter.5 = f32[128,1600]{1,0:T(8,128)} custom-call(bf16[8,128,1600]{2,1,0:T(8,128)(2,1)} %bitcast.193), custom_call_target="tpu_custom_call" | custom-call | tf_op jit(solution)/shard_map/group_scatter/pallas_call | solution.py:745
  545.7 7.3 convolution_convert_fusion.3
  553.0 5.5 convolution_convert_fusion.4
  559.3 5.2 copy.36
  576.9 6.1 fusion.21
  583.7 190.8 %yield_grads.1 = (bf16[8,200,768]{2,1,0:T(8,128)(2,1)}, bf16[3,8,50,800]{3,2,1,0:T(8,128)(2,1)}, bf16[3,200,1600]{2,1,0:T(8,128)(2,1)}, f32[8,256]{1,0:T(8,128)}) custom-call(bf16[2,2,2,200,768]{4,3,2,1,0:T(8,128)(2,1)} %bitcast.200, bf16[2,2,2,200,800]{4,3,2,1,0:T(8,128)(2,1)} %bitcast.194, bf16[2,2,200,1600]{3,2,1,0:T(8,128)(2,1)} %bitcast.199, ...), custom_call_target="tpu_custom_call" | custom-call | tf_op jit(solution)/shard_map/yield_grads/pallas_call | solution.py:974
  789.4 4.9 reshape.340
  794.3 5.0 reshape.342
  799.3 11.0 %convert_subtract_fusion.2 = (f32[7500,128]{1,0:T(8,128)}, f32[7500,128]{1,0:T(8,128)}, f32[7500,128]{1,0:T(8,128)}) fusion(bf16[7500,128]{1,0:T(8,128)(2,1)S(1)} %copy-done.3, f32[7500,128]{1,0:T(8,128)} %param.15, f32[7500,128]{1,0:T(8,128)} %param.14, bf16[7500,128]{1,0:T(8,128)(2,1)} %reshape.340, bf16[7500,128]{1,0:T(8,128)(2,1)} %reshape.341, ...), kind=kLoop, calls=%fused_computation.18 | loop fusion | flops 18240000 | bytes 26887500 | tf_op jit(solution)/shard_map/sub | solution.py:99
  (188 shorter events, 121.1 us)
Async XLA Ops:
  10.4 7.2 copy-start.37
  10.4 7.8 copy-start.12
  13.2 6.0 copy-start.13
  17.6 6.2 copy-start.32
  20.2 5.3 copy-start.16
  20.3 5.3 copy-start.17
  20.3 5.3 copy-start.18
  20.3 5.4 copy-start.14
  20.3 5.4 copy-start.15
  277.6 9.0 %copy-start.1 = (bf16[8,128,1600]{2,1,0:T(8,128)(2,1)S(1)}, bf16[8,128,1600]{2,1,0:T(8,128)(2,1)}, u32[]{:S(2)}) copy-start(bf16[8,128,1600]{2,1,0:T(8,128)(2,1)} %get-tuple-element.23) | copy-start | bytes 9830404
  280.8 13.1 %copy-start.30 = (f32[1600]{0:T(1024)}, f32[1600]{0:T(1024)S(1)}, u32[]{:S(2)}) copy-start(f32[1600]{0:T(1024)S(1)} %get-tuple-element.144) | copy-start | bytes 19204
  373.4 5.7 copy-start.40
  373.4 5.7 copy-start.28
  480.8 21.4 %copy-start.35 = (pred[768]{0:T(1024)(128)(4,1)S(1)}, pred[768]{0:T(1024)(128)(4,1)}, u32[]{:S(2)}) copy-start(pred[768]{0:T(1024)(128)(4,1)} %tile.10) | copy-start | bytes 2308
  543.7 267.3 %collective-permute-start = (bf16[128,3200]{1,0:T(8,128)(2,1)}, bf16[128,3200]{1,0:T(8,128)(2,1)}, u32[]{:S(2)}, u32[]{:S(2)}) collective-permute-start(bf16[128,3200]{1,0:T(8,128)(2,1)} %pad_maximum_fusion), channel_id=1, source_target_pairs={{0,0},{1,16},{2,2},{3,18},{4,8},{5,24},{6,10},{7,26},{8,4},{9,20},... | collective-permute-start | bytes 2457608 | tf_op jit(solution)/shard_map/ppermute | solution.py:1168
  545.7 7.3 copy-start.29
  545.7 7.3 copy-start.41
  553.0 5.6 copy-start.9
  553.0 5.6 copy-start.10
  553.0 5.5 copy-start.11
  789.4 9.9 %copy-start.3 = (bf16[7500,128]{1,0:T(8,128)(2,1)S(1)}, bf16[7500,128]{1,0:T(8,128)(2,1)}, u32[]{:S(2)}) copy-start(bf16[7500,128]{1,0:T(8,128)(2,1)} %param.12) | copy-start | bytes 5760004
  799.3 11.1 %copy-start.33 = (f32[3,200]{1,0:T(4,128)S(1)}, f32[3,200]{1,0:T(4,128)}, u32[]{:S(2)}) copy-start(f32[3,200]{1,0:T(4,128)} %param.17) | copy-start | bytes 7204
  799.3 11.1 %copy-start.34 = (f32[3,200]{1,0:T(4,128)S(1)}, f32[3,200]{1,0:T(4,128)}, u32[]{:S(2)}) copy-start(f32[3,200]{1,0:T(4,128)} %param.16) | copy-start | bytes 7204
  799.3 11.1 %copy-start.36 = (f32[8,256]{1,0:T(8,128)S(1)}, f32[8,256]{1,0:T(8,128)}, u32[]{:S(2)}) copy-start(f32[8,256]{1,0:T(8,128)} %get-tuple-element.37) | copy-start | bytes 24580
  (21 other events, 79.6 us)

commit v2 on v1

--- a/solution.py
+++ b/solution.py
@@ -272,6 +272,7 @@
 GROUPS = 4
 DEVICES = MEMBERS * GROUPS
 MESH = pl.DeviceIdType.MESH
+BLOCK = 64
 SLOTS = 4
 VMEM_BYTES = 60 * 1024 * 1024
 OUT_FIRST = 24
@@ -451,81 +452,226 @@
     return (shard // MEMBERS, shard % MEMBERS), third % 3
 
 
-def intake_kernel(
-    x_in, back_in, order_in, vec_in, qkv_in, fc_in, rows_in,
-    x_all, back_all, order, vec_all, qkv, fc, proj, out,
-    move_sem, qkv_sem, fc_send, fc_recv, rows_sem, x_sem, back_sem, out_sem, spread_sem, tree_sem,
+def lookup(table, index):
+    result = 0
+    for place, entry in enumerate(table):
+        if entry:
+            result = result + jnp.where(index == place, entry, 0)
+    return result
+
+
+FC_OF_GROUP = (
+    (0, 1, 16, 17, 18, 22, 23, 24),
+    (2, 3, 19, 20, 21, 25, 26, 27),
+    (4, 5, 6, 10, 11, 12, 28, 29),
+    (7, 8, 9, 13, 14, 15, 30, 31),
+)
+FC_SLOT = [0] * 32
+FC_Y = [0] * 32
+for _group, _units in enumerate(FC_OF_GROUP):
+    for _slot, _unit in enumerate(_units):
+        FC_SLOT[_unit] = _slot
+        FC_Y[_unit] = _group % 2
+
+
+def fc_unit(far, y, slot):
+    return lookup([units[slot] for units in FC_OF_GROUP], 2 * far + y)
+
+
+def fc_home(place, unit):
+    return lookup(FC_SLOT, unit), lookup(FC_Y, unit)
+
+
+def out_root(member):
+    return jnp.where(member // 3 == 1, 1, 0)
+
+
+def half_tile(flat, first, count, stride, half):
+    at = half // 2
+    tile = flat[pl.ds(first + at, count, stride=stride), :]
+    if half % 2 == 0:
+        return tile
+    after = flat[pl.ds(first + at + 1, count, stride=stride), :]
+    lane = lax.broadcasted_iota(jnp.int32, tile.shape, 1)
+    return pltpu.roll(jnp.where(lane < HD, after, tile), HD, 1)
+
+
+def lay_qkv(flat, rows, pieces, member):
+    count = rows.shape[1] // 2
+    halves = 3 * HEADS
+    for part in range(3):
+        for odd in range(2):
+            for tile in range(SLOTS // 2):
+                half = halves * odd + HEADS * part + head_start(member) + 2 * tile
+                rows[SLOTS // 2 * part + tile, pl.ds(odd, count, stride=2), :] = half_tile(
+                    flat, 0, count, halves, half
+                )
+    for tile in range(3 * SLOTS // 2):
+        pieces[member, :, 128 * tile : 128 * tile + 128] = rows[tile].astype(jnp.bfloat16)
+
+
+def lay_fc(flat, first, pieces, part):
+    count, hidden = pieces.shape[-2:]
+    stride = FF // 128
+    for member in range(MEMBERS):
+        start, shift = divmod(member * hidden, 128)
+        for tile in range(-(-hidden // 128)):
+            value = flat[pl.ds(first + start + tile, count, stride=stride), :]
+            size = min(128, hidden - 128 * tile)
+            if shift:
+                if shift + size > 128:
+                    after = flat[pl.ds(first + start + tile + 1, count, stride=stride), :]
+                    lane = lax.broadcasted_iota(jnp.int32, value.shape, 1)
+                    value = jnp.where(lane < shift, after, value)
+                value = pltpu.roll(value, 128 - shift, 1)
+            pieces[part, member, :, 128 * tile : 128 * tile + size] = value[:, :size].astype(
+                jnp.bfloat16
+            )
+
+
+def lay_rows(flat, first, rows, blocks, part):
+    count = rows.shape[1] // 2
+    width = blocks.shape[-1]
+    halves = width // HD
+    for odd in range(2):
+        for tile in range(-(-width // 128)):
+            half = halves * odd + 2 * tile
+            size = min(128, width - 128 * tile)
+            if size == 128 or half % 2 == 0:
+                value = half_tile(flat, first, count, halves, half)
+            else:
+                value = pltpu.roll(
+                    flat[pl.ds(first + half // 2, count, stride=halves), :], HD, 1
+                )
+            rows[tile, pl.ds(odd, count, stride=2), :] = value
+    for tile in range(-(-width // 128)):
+        size = min(128, width - 128 * tile)
+        blocks[part, :, 128 * tile : 128 * tile + size] = rows[tile, :, :size].astype(
+            jnp.bfloat16
+        )
+
+
+def norm_rows(value, gain, shift):
+    center = value - jnp.mean(value, -1, keepdims=True)
+    spread = jnp.mean(center * center, -1, keepdims=True)
+    return center * lax.rsqrt(spread + epsilon_norm) * gain + shift
+
+
+def member_lanes(row, member, count):
+    result = jnp.zeros((row.shape[0], count), row.dtype)
+    for other in range(MEMBERS):
+        first = head_start(other) * HD
+        result = result + jnp.where(member == other, row[:, first : first + count], 0.0)
+    return result
+
+
+def attend_block(query, keys, values, row_pos, col_pos):
+    lanes = lane_of(query.shape)
+    result = jnp.zeros(query.shape, jnp.float32)
+    for head in range(2):
+        mine = lanes == head
+        own = jnp.where(mine, query, jnp.zeros_like(query))
+        probs = probabilities(own, keys, row_pos, col_pos)
+        mixed = jnp.dot(probs.astype(jnp.bfloat16), values, preferred_element_type=jnp.float32)
+        result = jnp.where(mine, mixed, result)
+    return result.astype(jnp.bfloat16)
+
+
+def forward_kernel(
+    x_in, back_in, order_in, vec_in, weights,
+    x_all, back_all, vecs, row_pos, col_pos, w_qkv, h_first, qkv, attn_all, fc, proj, out,
+    flat, rows, qkv_pieces, fc_pieces, blocks, order, vec_all, qkv_land, attn,
+    fc_part, proj_part, out_part,
+    move_sem, qkv_sem, fc_send, fc_recv, rows_sem, x_sem, back_sem, spread_sem,
+    own_sem, fc_sem, proj_sem, tree_sem, out_sem, attn_sem,
 ):
     p = Place()
-    greet_all(p)
+    third_rows = weights.shape[0] // 3
+    count, width = x_in.shape
+    length = MEMBERS * count
+    pairs = SLOTS // 2
+    barrier = pltpu.get_barrier_semaphore()
+
+    def signal(step, carry):
+        other = (p.linear + step) % DEVICES
+        pl.semaphore_signal(
+            barrier, inc=1, device_id=(other // MEMBERS, other % MEMBERS), device_id_type=MESH
+        )
+        return carry
+
+    lax.fori_loop(1, DEVICES, signal, 0)
+    flat[...] = weights[...].astype(jnp.float32)
+    pl.semaphore_wait(barrier, DEVICES - 1)
     home = p.target(
         x=p.ctx % 2, near=p.ctx // 2 % 2, core=p.ctx // 4, y=p.fsdp // 2, far=p.fsdp % 2
     )
-    home_member = p.ctx
-    x_move = Move(
-        p, x_in, x_all.at[home_member], move_sem.at[0, 0], move_sem.at[1, 0], home
-    )
+    x_move = Move(p, x_in, x_all.at[p.ctx], move_sem.at[0, 0], move_sem.at[1, 0], home)
     order_move = Move(p, order_in, order, move_sem.at[0, 1], move_sem.at[1, 1], home)
     owner = p.fsdp == 0
     qkv_moves = []
-    for member in (1, 0, 3, 2, 5, 4, 7, 6):
+    for member in (7, 6, 3, 2, 5, 4, 1, 0):
+
+        @pl.when(owner)
+        def _(member=member):
+            lay_qkv(flat, rows, qkv_pieces, member)
+
         target = p.target(x=member % 2, near=member // 2 % 2, core=member // 4)
         qkv_moves.append(
             Move(
-                p, qkv_in.at[member], qkv.at[p.far, p.near, p.y],
+                p, qkv_pieces.at[member], qkv_land.at[p.far, p.near, p.y],
                 qkv_sem.at[0, member], qkv_sem.at[1, p.near], target, owner,
             )
         )
-    def vec_copy(step):
+
+    def vec_send(step, carry):
         other = (p.linear + step) % DEVICES
-        return pltpu.make_async_remote_copy(
+        pltpu.make_async_remote_copy(
             src_ref=vec_in,
             dst_ref=vec_all.at[p.linear],
             send_sem=move_sem.at[0, 2],
             recv_sem=move_sem.at[1, 2],
             device_id=(other // MEMBERS, other % MEMBERS),
             device_id_type=MESH,
-        )
-
-    def vec_send(step, carry):
-        vec_copy(step).start()
+        ).start()
         return carry
 
     lax.fori_loop(1, DEVICES, vec_send, 0)
     pltpu.make_async_copy(vec_in, vec_all.at[p.linear], move_sem.at[1, 2]).start()
+    for part in range(3):
+        third = 3 * p.linear + part
+        is_fc = jnp.logical_and(third >= FC_FIRST, third < PROJ_FIRST)
+        is_rows = jnp.logical_and(third >= OUT_FIRST, jnp.logical_not(is_fc))
+
+        @pl.when(is_fc)
+        def _(part=part):
+            lay_fc(flat, part * third_rows, fc_pieces, part)
+
+        @pl.when(is_rows)
+        def _(part=part):
+            lay_rows(flat, part * third_rows, rows, blocks, part)
 
     arrived(x_all.at[p.me], move_sem.at[1, 0])
     gather_x = Gather(p, x_all, x_sem)
     gather_x.begin()
-    back_move = Move(
-        p, back_in, back_all.at[home_member], move_sem.at[0, 3], move_sem.at[1, 3], home
-    )
     spreads = []
     for near in range(2):
-        spreads.append(
-            Spread(p, lambda far, y, near=near: qkv.at[far, near, y], spread_sem, 3 * near)
-        )
-    for near in range(2):
-        arrived(qkv.at[p.far, near, p.y], qkv_sem.at[1, near])
-        spreads[near].begin()
+        arrived(qkv_land.at[p.far, near, p.y], qkv_sem.at[1, near])
+        item = Spread(p, lambda far, y, near=near: qkv_land.at[far, near, y], spread_sem, 3 * near)
+        item.begin()
+        spreads.append(item)
     gather_x.second_hop()
     gather_x.third_hop()
     fc_moves, rows_moves = [], []
     for part in range(3):
         third = 3 * p.linear + part
-        unit = third - FC_FIRST
-        valid = jnp.logical_and(unit >= 0, third < PROJ_FIRST)
-        unit = jnp.where(valid, unit, 0)
-        ctx, slot = unit // 4, unit % 4
-        far, near, y = ctx // 4, ctx // 2 % 2, ctx % 2
-        for member in (1, 0, 3, 2, 5, 4, 7, 6):
-            target = p.target(
-                x=member % 2, near=member // 2 % 2, core=member // 4, far=far, y=y
-            )
+        valid = jnp.logical_and(third >= FC_FIRST, third < PROJ_FIRST)
+        slot, y = fc_home(p, jnp.where(valid, third - FC_FIRST, 0))
+        for member in (7, 6, 3, 2, 5, 4, 1, 0):
+            target = p.target(x=member % 2, near=member // 2 % 2, core=member // 4, y=y)
             fc_moves.append(
                 Move(
-                    p, fc_in.at[part, member], fc.at[far, near, y, slot],
-                    fc_send.at[part, member], fc_recv.at[4 * near + slot], target, valid,
+                    p, fc_pieces.at[part, member], fc_part.at[slot],
+                    fc_send.at[part, member], fc_recv.at[slot], target, valid,
                 )
             )
     for part in range(3):
@@ -538,135 +684,290 @@
         )
         rows_moves.append(
             Move(
-                p, rows_in.at[part], proj.at[group // 2, group % 2],
+                p, blocks.at[part], proj_part,
                 rows_sem.at[0, part], rows_sem.at[1, 0], target, valid,
             )
         )
         valid = jnp.logical_and(third >= OUT_FIRST, third < FC_FIRST)
         member = jnp.where(valid, third - OUT_FIRST, 0)
-        group = member % 4
         target = p.target(
-            x=member % 2, near=member // 2 % 2, core=member // 4, y=group // 2, far=group % 2
+            x=member % 2, near=member // 2 % 2, core=member // 4, y=out_root(member), far=0
         )
         rows_moves.append(
             Move(
-                p, rows_in.at[part], out.at[member],
+                p, blocks.at[part], out_part,
                 rows_sem.at[0, part], rows_sem.at[1, 1], target, valid,
             )
         )
     gather_x.last_hop()
-    for near in range(2):
-        spreads[near].middle()
+    back_move = Move(p, back_in, back_all.at[p.ctx], move_sem.at[0, 3], move_sem.at[1, 3], home)
+    arrived(vec_all, move_sem.at[1, 2])
+    cols = vec_in.shape[-1]
+    used = width // MEMBERS
+    total = jnp.zeros(vecs.shape, jnp.float32)
+    for ctx in range(MEMBERS):
+        block = jnp.concatenate([vec_all[MEMBERS * f + ctx] for f in range(GROUPS)], 0)
+        lane = lax.broadcasted_iota(jnp.int32, (cols, width), 0)
+        at = lax.broadcasted_iota(jnp.int32, (cols, width), 1) - used * ctx
+        spot = jnp.where(jnp.logical_and(lane == at, lane < used), 1.0, 0.0)
+        total = total + jnp.dot(
+            block, spot.astype(jnp.bfloat16), preferred_element_type=jnp.float32
+        )
+    vecs[...] = total
+    arrived(order, move_sem.at[1, 1])
+    slots = order[0:1, :].astype(jnp.float32)
+    lane = lax.broadcasted_iota(jnp.int32, (length, 128), 1)
+    row = lax.broadcasted_iota(jnp.int32, (length, 128), 0)
+    spot = jnp.where(lane == row // BLOCK, slots, 0.0)
+    inner = lax.broadcasted_iota(jnp.int32, (length, 1), 0) % BLOCK
+    row_pos[...] = jnp.sum(spot, 1, keepdims=True) * BLOCK + inner.astype(jnp.float32)
+    lane = lax.broadcasted_iota(jnp.int32, (128, length), 1)
+    row = lax.broadcasted_iota(jnp.int32, (128, length), 0)
+    spot = jnp.where(row == lane // BLOCK, 1.0, 0.0)
+    inner = lax.broadcasted_iota(jnp.int32, (1, length), 1) % BLOCK
+    found = jnp.dot(
+        order[...].astype(jnp.bfloat16), spot.astype(jnp.bfloat16),
+        preferred_element_type=jnp.float32,
+    )
+    col_pos[...] = found[0:1, :] * BLOCK + inner.astype(jnp.float32)
+    for item in spreads:
+        item.middle()
     arrived(back_all.at[p.me], move_sem.at[1, 3])
     gather_back = Gather(p, back_all, back_sem)
     gather_back.begin()
-    for near in range(2):
-        for slot in range(4):
-            arrived(fc.at[p.far, near, p.y, slot], fc_recv.at[4 * near + slot])
-        item = Spread(p, lambda far, y, near=near: fc.at[far, near, y], spread_sem, 6 + 3 * near)
-        item.begin()
-        spreads.append(item)
-    root_y, root_far = p.me % 4 // 2, p.me % 2
-    same_y, same_far = p.y == root_y, p.far == root_far
+    gather_x.finish()
+
+    def norm_block(step, carry):
+        value = norm_rows(x_all[step].astype(jnp.float32), vecs[0:1, :], vecs[1:2, :])
+        h_first[pl.ds(pl.multiple_of(step * count, count), count), :] = value.astype(jnp.bfloat16)
+        return carry
+
+    lax.fori_loop(0, MEMBERS, norm_block, 0)
+    to_far, to_y = p.target(far=1 - p.far), p.target(y=1 - p.y)
+    fc_far, fc_y, fc_later, own_copies = [], [], [], []
+    for slot in range(8):
+        arrived(fc_part.at[slot], fc_recv.at[slot])
+        landing = fc.at[fc_unit(p.far, p.y, slot)]
+        fc_far.append(remote(fc_part.at[slot], landing, fc_sem, slot, to_far))
+        fc_far[slot].start()
+        fc_y.append(remote(fc_part.at[slot], landing, fc_sem, 8 + slot, to_y))
+        fc_y[slot].start()
+        own_copies.append(pltpu.make_async_copy(fc_part.at[slot], landing, own_sem.at[slot]))
+        own_copies[slot].start()
+    gather_back.second_hop()
+    gather_back.third_hop()
+    root_y = out_root(p.me)
+    same_y = p.y == root_y
+    root = jnp.logical_and(same_y, p.far == 0)
+    beside = jnp.logical_and(same_y, p.far == 1)
     mine = out.at[p.me]
-    to_far, to_y = p.target(far=1 - p.far), p.target(y=1 - p.y)
-    root = jnp.logical_and(same_y, same_far)
-    beside = jnp.logical_and(same_y, jnp.logical_not(same_far))
-    opposite = jnp.logical_not(same_y)
-    over_far = remote(mine, mine, tree_sem, 0, to_far)
-    over_y = remote(mine, mine, tree_sem, 1, to_y)
+    out_far = remote(out_part, mine, tree_sem, 0, to_far)
+    out_y = remote(out_part, mine, tree_sem, 1, to_y)
+    out_later = remote(mine, mine, tree_sem, 2, to_y)
+    out_own = pltpu.make_async_copy(out_part, mine, own_sem.at[8])
 
     @pl.when(root)
     def _():
-        arrived(mine, rows_sem.at[1, 1])
-        over_far.start()
-        over_y.start()
-
-    arrived(proj.at[p.y, p.far], rows_sem.at[1, 0])
-    item = Spread(p, lambda far, y: proj.at[y, far], spread_sem, 12)
-    item.begin()
-    spreads.append(item)
-    gather_back.second_hop()
-    gather_back.third_hop()
+        arrived(out_part, rows_sem.at[1, 1])
+        out_far.start()
+        out_y.start()
+        out_own.start()
+
+    arrived(proj_part, rows_sem.at[1, 0])
+    my_proj, far_proj = proj.at[p.y, p.far], proj.at[p.y, 1 - p.far]
+    proj_far = remote(proj_part, my_proj, proj_sem, 0, to_far)
+    proj_y = remote(proj_part, my_proj, proj_sem, 1, to_y)
+    proj_far.start()
+    proj_y.start()
+    proj_own = pltpu.make_async_copy(proj_part, my_proj, own_sem.at[9])
+    proj_own.start()
+    for item in spreads:
+        item.finish()
+    four = qkv_land.shape[3]
+    for far in range(2):
+        for near in range(2):
+            for y in range(2):
+                first = four * (4 * far + 2 * near + y)
+                w_qkv[first : first + four, :] = qkv_land[far, near, y]
+    per_part = SLOTS * HD
+    bias = jnp.concatenate(
+        [
+            member_lanes(vecs[2:3, :], p.me, per_part),
+            jnp.zeros((1, per_part), jnp.float32),
+            member_lanes(vecs[16:17, :], p.me, per_part),
+        ],
+        1,
+    )
+
+    def qkv_block(step, carry):
+        at = pl.ds(pl.multiple_of(step * 2 * count, 2 * count), 2 * count)
+        value = jnp.dot(h_first[at, :], w_qkv[...], preferred_element_type=jnp.float32)
+        qkv[at, :] = (value + bias).astype(jnp.bfloat16)
+        return carry
+
+    lax.fori_loop(0, MEMBERS // 2, qkv_block, 0)
     gather_back.last_hop()
-    for item in spreads[2:4]:
-        item.middle()
+    span = 2 * count
+
+    def one_pair(pair):
+        def one_block(step, carry):
+            at = pl.ds(pl.multiple_of(step * span, span), span)
+            attn[pair, at, :] = attend_block(
+                qkv[at, 128 * pair : 128 * pair + 128],
+                qkv[:, 128 * (pairs + pair) : 128 * (pairs + pair) + 128],
+                qkv[:, 128 * (2 * pairs + pair) : 128 * (2 * pairs + pair) + 128],
+                row_pos[at, :],
+                col_pos[...],
+            )
+            return carry
+
+        lax.fori_loop(0, length // span, one_block, 0)
+
+    def share(pair):
+        item = Gather(p, attn_all.at[pair], attn_sem.at[pair])
+        for name, index, target in (
+            ("a", 0, item.first), ("b", 1, item.second), ("c", 2, item.other),
+        ):
+            copy = remote(attn.at[pair], attn_all.at[pair, p.me], attn_sem.at[pair], index, target)
+            copy.start()
+            item.copies[name] = copy
+        copy = pltpu.make_async_copy(
+            attn.at[pair], attn_all.at[pair, p.me], own_sem.at[10 + pair]
+        )
+        copy.start()
+        own_copies.append(copy)
+        return item
+
+    one_pair(0)
+    gathers = [share(0)]
+    for slot in range(8):
+        fc_far[slot].wait_recv()
+        landing = fc.at[fc_unit(1 - p.far, p.y, slot)]
+        copy = remote(landing, landing, fc_sem, 16 + slot, to_y)
+        copy.start()
+        fc_later.append(copy)
 
     @pl.when(beside)
     def _():
-        over_far.wait_recv()
-        over_y.start()
-
-    @pl.when(opposite)
+        out_far.wait_recv()
+        out_later.start()
+
+    gathers[0].second_hop()
+    gathers[0].third_hop()
+    gathers[0].last_hop()
+    one_pair(1)
+    gathers.append(share(1))
+    proj_far.wait_recv()
+    proj_later = remote(far_proj, far_proj, proj_sem, 2, to_y)
+    proj_later.start()
+    gathers[1].second_hop()
+    gathers[1].third_hop()
+    gathers[1].last_hop()
+
+    @pl.when(root)
     def _():
-        over_y.wait_recv()
+        out_own.wait()
+
+    @pl.when(jnp.logical_and(jnp.logical_not(same_y), p.far == 0))
+    def _():
+        out_y.wait_recv()
+
+    @pl.when(jnp.logical_and(jnp.logical_not(same_y), p.far == 1))
+    def _():
+        out_later.wait_recv()
 
     gather_out = Gather(p, out, out_sem)
     gather_out.begin()
-    spreads[4].middle()
     gather_out.second_hop()
     gather_out.third_hop()
     gather_out.last_hop()
-    for item in (gather_x, gather_back, gather_out):
+    for item in gathers + [gather_out, gather_back]:
         item.finish()
-    for item in spreads:
-        item.finish()
+    for item in fc_y + fc_later + [proj_y, proj_later]:
+        item.wait_recv()
+    for item in fc_far + fc_y + fc_later + [proj_far, proj_y, proj_later]:
+        item.wait_send()
 
     @pl.when(root)
     def _():
-        over_far.wait_send()
-
-    @pl.when(same_y)
+        out_far.wait_send()
+        out_y.wait_send()
+
+    @pl.when(beside)
     def _():
-        over_y.wait_send()
-
+        out_later.wait_send()
+
+    for item in own_copies + [proj_own]:
+        item.wait()
     for item in [x_move, order_move, back_move] + qkv_moves + fc_moves + rows_moves:
         item.sent()
-    arrived(order, move_sem.at[1, 1])
-    arrived(vec_all, move_sem.at[1, 2])
-    sent = vec_all.at[pl.ds(1, DEVICES - 1)]
-    arrived(sent, move_sem.at[0, 2])
-
-
-def intake(x, back, order, vectors, qkv_pieces, fc_pieces, row_blocks):
+    arrived(vec_all.at[pl.ds(1, DEVICES - 1)], move_sem.at[0, 2])
+
+
+def forward(x, back, order, vectors, weights):
     rows, width = x.shape
-    low = jnp.bfloat16
-    _, four, wide = qkv_pieces.shape
-    _, _, unit, hidden = fc_pieces.shape
+    kind, high = jnp.bfloat16, jnp.float32
+    unit, hidden = width // DEVICES, FF // MEMBERS
+    four, cols = 4 * unit, 3 * SLOTS * HD
+    length, pairs = MEMBERS * rows, SLOTS // 2
     any_space = pl.BlockSpec(memory_space=pl.ANY)
-
-    def like(*shape, kind=low):
-        return jax.ShapeDtypeStruct(shape, kind)
+    vmem = pl.BlockSpec(memory_space=pltpu.VMEM)
+    dma = pltpu.SemaphoreType.DMA
+
+    def like(*shape, dtype=kind):
+        return jax.ShapeDtypeStruct(shape, dtype)
 
     return pl.pallas_call(
-        intake_kernel,
+        forward_kernel,
         out_shape=[
             like(MEMBERS, rows, width),
             like(MEMBERS, rows, width),
-            like(*order.shape, kind=order.dtype),
-            like(DEVICES, *vectors.shape),
-            like(2, 2, 2, four, wide),
-            like(2, 2, 2, 4, unit, hidden),
+            like(GROUPS * vectors.shape[0], width, dtype=high),
+            like(length, 1, dtype=high),
+            like(1, length, dtype=high),
+            like(width, cols),
+            like(length, width),
+            like(length, cols),
+            like(pairs, MEMBERS, length, 2 * HD),
+            like(DEVICES, unit, hidden),
             like(2, 2, four, width),
             like(MEMBERS, four, width),
         ],
-        in_specs=[any_space] * 7,
-        out_specs=[any_space] * 8,
+        in_specs=[any_space] * 4 + [vmem],
+        out_specs=[vmem, any_space] + [vmem] * 6 + [any_space] * 4,
         scratch_shapes=[
-            pltpu.SemaphoreType.DMA((2, 4)),
-            pltpu.SemaphoreType.DMA((2, 8)),
-            pltpu.SemaphoreType.DMA((3, 8)),
-            pltpu.SemaphoreType.DMA((8,)),
-            pltpu.SemaphoreType.DMA((2, 3)),
-            pltpu.SemaphoreType.DMA((2, 7)),
-            pltpu.SemaphoreType.DMA((2, 7)),
-            pltpu.SemaphoreType.DMA((2, 7)),
-            pltpu.SemaphoreType.DMA((2, 15)),
-            pltpu.SemaphoreType.DMA((2, 2)),
+            pltpu.VMEM(weights.shape, high),
+            pltpu.VMEM((-(-width // 128), four, 128), high),
+            pltpu.VMEM((MEMBERS, four, cols), kind),
+            pltpu.VMEM((3, MEMBERS, unit, hidden), kind),
+            pltpu.VMEM((3, four, width), kind),
+            pltpu.VMEM(order.shape, order.dtype),
+            pltpu.VMEM((DEVICES,) + vectors.shape, kind),
+            pltpu.VMEM((2, 2, 2, four, cols), kind),
+            pltpu.VMEM((pairs, length, 2 * HD), kind),
+            pltpu.VMEM((8, unit, hidden), kind),
+            pltpu.VMEM((four, width), kind),
+            pltpu.VMEM((four, width), kind),
+            dma((2, 4)),
+            dma((2, 8)),
+            dma((3, 8)),
+            dma((8,)),
+            dma((2, 3)),
+            dma((2, 7)),
+            dma((2, 7)),
+            dma((2, 6)),
+            dma((12,)),
+            dma((2, 24)),
+            dma((2, 3)),
+            dma((2, 3)),
+            dma((2, 7)),
+            dma((pairs, 2, 7)),
         ],
-        compiler_params=pltpu.CompilerParams(collective_id=1, has_side_effects=True),
-        name="intake",
-    )(x, back, order, vectors, qkv_pieces, fc_pieces, row_blocks)
+        compiler_params=pltpu.CompilerParams(
+            collective_id=1, has_side_effects=True, vmem_limit_bytes=VMEM_BYTES
+        ),
+        name="forward",
+    )(x, back, order, vectors, weights)
 
 
 def gather_kernel(own, out, local_sem, sems):
@@ -1035,20 +1336,6 @@
     return weights / jnp.sum(weights, -1, keepdims=True)
 
 
-def attend_kernel(query, keys, values, row_pos, col_pos, out):
-    lanes = lane_of(query.shape)
-    result = jnp.zeros(query.shape, jnp.float32)
-    for head in range(2):
-        mine = lanes == head
-        own = jnp.where(mine, query[...], jnp.zeros_like(query))
-        probs = probabilities(own, keys[...], row_pos[...], col_pos[...])
-        mixed = jnp.dot(
-            probs.astype(jnp.bfloat16), values[...], preferred_element_type=jnp.float32
-        )
-        result = jnp.where(mine, mixed, result)
-    out[...] = result.astype(jnp.bfloat16)
-
-
 def attend_back_kernel(
     query, keys, values, grad, row_pos, col_pos, dquery, dkeys, dvalues, key_sum, value_sum
 ):
@@ -1082,26 +1369,6 @@
     def _():
         dkeys[...] = (key_sum[...] * 0.125).astype(jnp.bfloat16)
         dvalues[...] = value_sum[...].astype(jnp.bfloat16)
-
-
-def attend(qkv, row_pos, col_pos, span):
-    length = qkv.shape[0]
-    wide = 2 * HD
-    return pl.pallas_call(
-        attend_kernel,
-        grid=(SLOTS // 2, length // span),
-        in_specs=[
-            pl.BlockSpec((span, wide), lambda h, i: (i, h)),
-            pl.BlockSpec((length, wide), lambda h, i: (0, SLOTS // 2 + h)),
-            pl.BlockSpec((length, wide), lambda h, i: (0, SLOTS + h)),
-            pl.BlockSpec((span, 1), lambda h, i: (i, 0)),
-            pl.BlockSpec((1, length), lambda h, i: (0, 0)),
-        ],
-        out_specs=pl.BlockSpec((span, wide), lambda h, i: (i, h)),
-        out_shape=jax.ShapeDtypeStruct((length, SLOTS * HD), jnp.bfloat16),
-        compiler_params=pltpu.CompilerParams(vmem_limit_bytes=VMEM_BYTES),
-        name="attend",
-    )(qkv, qkv, qkv, row_pos, col_pos)
 
 
 def attend_back(qkv, grad, row_pos, col_pos, span):
@@ -1134,22 +1401,6 @@
     )(qkv, qkv, qkv, grad, row_pos, col_pos)
 
 
-def head_columns(rows, width):
-    pieces = []
-    for member in range(MEMBERS):
-        first = head_start(member) * HD
-        pieces.append(
-            jnp.concatenate(
-                [
-                    rows[:, part * width + first : part * width + first + SLOTS * HD]
-                    for part in range(3)
-                ],
-                1,
-            )
-        )
-    return jnp.stack(pieces)
-
-
 def own_heads(member):
     return (head_start(member + 1) - head_start(member)) * HD
 
@@ -1183,40 +1434,25 @@
     four = 4 * unit
     per_part = SLOTS * HD
 
-    qkv_pieces = head_columns(weights.reshape(four, 3 * width), width)
-    fc_pieces = weights.reshape(3, unit, MEMBERS, hidden).transpose(0, 2, 1, 3)
-    row_blocks = weights.reshape(3, four, width)
-    order = jnp.pad(slot_order, ((0, 7), (0, 128 - slot_order.shape[1])))
+    order = jnp.pad(slot_order, ((0, 127), (0, 128 - slot_order.shape[1])))
     vec_rows, vec_cols = vectors.shape
     padded = jnp.pad(vectors, ((0, 16 - vec_rows), (0, -vec_cols % 128)))
-    x_all, back_all, order, full_vec, own_qkv, own_fc, own_proj, full_out = intake(
-        inputs.reshape(rows, width), cotangent.reshape(rows, width), order, padded,
-        qkv_pieces, fc_pieces, row_blocks,
+    (
+        x_all, back_all, vec, row_pos, col_pos, own_qkv, h_first, qkv, attn_all,
+        own_fc, own_proj, full_out,
+    ) = forward(
+        inputs.reshape(rows, width), cotangent.reshape(rows, width), order, padded, weights
     )
     x_all, back_all = x_all.reshape(length, width), back_all.reshape(length, width)
-    own_qkv = own_qkv.reshape(width, 3 * per_part)
     own_fc = own_fc.reshape(width, hidden)
     own_proj = own_proj.reshape(hidden, width)
     full_out = full_out.reshape(width, width)
-    order = order[0, : slot_order.shape[1]]
-    block = length // order.shape[0]
-    pos = (order[:, None] * block + jnp.arange(block, dtype=jnp.int32)).reshape(-1)
-    row_pos, col_pos = pos[:, None], pos[None, :]
-    full_vec = full_vec[:, :vec_rows, :vec_cols].reshape(GROUPS, MEMBERS, vec_rows, vec_cols)
-    vec = full_vec.transpose(0, 2, 1, 3).reshape(-1, width).astype(high)
+    attn_all = all_heads(jnp.concatenate([attn_all[0], attn_all[1]], 2))
+    vec = vec.reshape(GROUPS, -1, width)[:, :vec_rows].reshape(-1, width)
     head_at = HEADS * member // MEMBERS * HD
-    bias_q = lax.dynamic_slice(vec[2], (head_at,), (per_part,))
-    bias_v = lax.dynamic_slice(vec[3], (head_at,), (per_part,))
-    bias_qkv = jnp.concatenate([bias_q, jnp.zeros_like(bias_q), bias_v])
     bias_fc = lax.dynamic_slice(vec[8:].reshape(-1), (member * hidden,), (hidden,))
-
     mine = member * rows
-    h_first = layer_norm(x_all.astype(high), vec[0], vec[1]).astype(kind)
-    qkv = jnp.dot(h_first, own_qkv, preferred_element_type=high) + bias_qkv
-    qkv = qkv.astype(kind)
     span = min(length, 256)
-    attn = attend(qkv, row_pos, col_pos, span)
-    attn_all = all_heads(group_gather(attn, 3))
     resid = x_all.astype(high) + jnp.dot(attn_all, full_out, preferred_element_type=high) + vec[4]
     h_second = layer_norm(resid, vec[5], vec[6]).astype(kind)
     pre = jnp.dot(h_second, own_fc, preferred_element_type=high) + bias_fc

time: 826 us -> 708 us (0.86)
  the two profiles are of different devices: /device:TPU:29 before, /device:TPU:20 now
where the time goes in v2:
time: 708 us; the launch traced here: 702 us
  Pallas kernels  528 us (75%)
  local copies, waits for them, and re-layouts  68.1 us (10%)
  matrix products  63.2 us (9%)
  other arithmetic  37.2 us (5%)
    pallas_call x1, Pallas kernels, forward(): pl.pallas_call(forward_kernel, out_shape=[like(MEMBERS, rows, width), lik...  213 us
    pallas_call x1, Pallas kernels, yield_grads(): pl.pallas_call(yield_kernel, out_shape=[jax.ShapeDtypeStruct((MEMBERS, fo...  202 us
    pallas_call x3, Pallas kernels, group_scatter(): pl.pallas_call(scatter_kernel, out_shape=jax.ShapeDtypeStruct((rows, widt...  70.3 us
    pallas_call x1, Pallas kernels, group_gather(): pl.pallas_call(gather_kernel, out_shape=jax.ShapeDtypeStruct((MEMBERS,) +...  22 us
    pallas_call x1, Pallas kernels, attend_back(): pl.pallas_call(attend_back_kernel, grid=(SLOTS // 2, length // span), in_...  21.4 us
  transfers between devices with their start and end apart: 1, of which 0 were waited for; matrix products, arithmetic and copies ran while one was open for 9% of the time, Pallas kernels for 29%

profile of v2, /device:TPU:20, one launch (start us, length us, event | category | flops | bytes accessed | tf_op | source)
XLA Modules:
  0.0 701.9 jit_solution(6415010489109026492)
XLA Ops:
  7.2 212.7 %forward.1 = (bf16[8,128,1600]{2,1,0:T(8,128)(2,1)}, bf16[8,128,1600]{2,1,0:T(8,128)(2,1)}, f32[64,1600]{1,0:T(8,128)}, f32[1024,1]{1,0:T(8,128)}, f32[1,1024]{1...) custom-call(bf16[128,1600]{1,0:T(8,128)(2,1)} %bitcast.153, ...), custom_call_target="tpu_custom_call" | custom-call | tf_op jit(solution)/shard_map/forward/pallas_call | solution.py:920
  221.1 4.7 reshape.197
  230.5 5.4 concatenate.19
  235.9 13.1 %fusion.52 = (f32[1024]{0:T(1024)S(1)}, f32[1024,1600]{1,0:T(8,128)}) fusion(f32[1600]{0:T(1024)S(1)} %get-tuple-element.74, bf16[1024,1600]{1,0:T(8,128)(2,1)S(1)} %concatenate.19, bf16[1600,1600]{1,0:T(8,128)(2,1)} %bitcast.190, bf16[1024,1600]{1,0:T(8,128)(2,1)} %bitcast.155), kind=kOutput, calls=%fused_computation.148 | convolution fusion | flops 5249432576 | bytes 18237696 | tf_op jit(solution)/shard_map/dot_general | solution.py:1456
  255.5 4.2 add_convert_fusion
  263.1 4.5 convolution_convert_fusion.2
  267.7 4.5 convert_reduce_fusion
  273.4 4.9 convolution_convert_fusion
  278.3 5.4 copy.30
  283.7 23.3 %group_scatter.4 = f32[128,1600]{1,0:T(8,128)} custom-call(bf16[8,128,1600]{2,1,0:T(8,128)(2,1)} %bitcast.137), custom_call_target="tpu_custom_call" | custom-call | tf_op jit(solution)/shard_map/group_scatter/pallas_call | solution.py:1046
  312.6 23.5 %group_scatter.3 = f32[128,1600]{1,0:T(8,128)} custom-call(bf16[8,128,1600]{2,1,0:T(8,128)(2,1)} %bitcast.138), custom_call_target="tpu_custom_call" | custom-call | tf_op jit(solution)/shard_map/group_scatter/pallas_call | solution.py:1046
  340.0 22.0 %group_gather.1 = bf16[8,128,1600]{2,1,0:T(8,128)(2,1)} custom-call(bf16[128,1600]{1,0:T(8,128)(2,1)} %get-tuple-element.84.own), custom_call_target="tpu_custom_call" | custom-call | tf_op jit(solution)/shard_map/group_gather/pallas_call | solution.py:992
  361.9 4.1 convolution_convert_fusion.7.grad
  366.1 21.4 %attend_back.1 = (bf16[1024,256]{1,0:T(8,128)(2,1)}, bf16[1024,256]{1,0:T(8,128)(2,1)}, bf16[1024,256]{1,0:T(8,128)(2,1)}) custom-call(bf16[1024,768]{1,0:T(8,128)(2,1)} %get-tuple-element.34.query.keys.values, bf16[1024,768]{1,0:T(8,128)(2,1)} %get-tuple-element.34.query.keys.values, bf16[1024,768]{1,0:T(8,128)(2,1)} %get-tuple-element.34.query.keys.values, ...), custom_call_target="tpu_custom_call" | custom-call | tf_op jit(solution)/shard_map/attend_back/pallas_call | solution.py:1378
  387.4 6.6 convolution_convert_fusion.1
  394.1 5.4 copy.31
  399.5 23.5 %group_scatter.5 = f32[128,1600]{1,0:T(8,128)} custom-call(bf16[8,128,1600]{2,1,0:T(8,128)(2,1)} %bitcast.139), custom_call_target="tpu_custom_call" | custom-call | tf_op jit(solution)/shard_map/group_scatter/pallas_call | solution.py:1046
  433.2 7.2 %convolution_convert_fusion.3 = bf16[1600,800]{0,1:T(8,128)(2,1)} fusion(bf16[1024,800]{0,1:T(8,128)(2,1)} %copy-done.20, bf16[1024,1600]{1,0:T(8,128)(2,1)} %copy-done.2), kind=kOutput, calls=%fused_computation.30 | convolution fusion | flops 2622720000 | bytes 7475200 | tf_op jit(solution)/shard_map/td,tf->df/dot_general | solution.py:1470
  440.5 5.5 convolution_convert_fusion.4
  446.8 5.5 copy.32
  455.5 6.2 convolution_convert_fusion.5
  463.1 201.6 %yield_grads.1 = (bf16[8,200,768]{2,1,0:T(8,128)(2,1)}, bf16[3,8,50,800]{3,2,1,0:T(8,128)(2,1)}, bf16[3,200,1600]{2,1,0:T(8,128)(2,1)}, f32[8,256]{1,0:T(8,128)}) custom-call(bf16[2,2,2,200,768]{4,3,2,1,0:T(8,128)(2,1)} %bitcast.144, bf16[2,2,2,200,800]{4,3,2,1,0:T(8,128)(2,1)} %bitcast.140, bf16[2,2,200,1600]{3,2,1,0:T(8,128)(2,1)} %bitcast.143, ...), custom_call_target="tpu_custom_call" | custom-call | tf_op jit(solution)/shard_map/yield_grads/pallas_call | solution.py:1275
  670.6 4.7 reshape.218
  686.3 11.3 %convert_subtract_fusion = (f32[7500,128]{1,0:T(8,128)}, f32[7500,128]{1,0:T(8,128)}, f32[7500,128]{1,0:T(8,128)}) fusion(bf16[7500,128]{1,0:T(8,128)(2,1)} %weights.1, f32[7500,128]{1,0:T(8,128)} %param.15, f32[7500,128]{1,0:T(8,128)} %param.14, bf16[7500,128]{1,0:T(8,128)(2,1)} %reshape.217, bf16[7500,128]{1,0:T(8,128)(2,1)} %reshape.218, ...), kind=kLoop, calls=%fused_computation.18 | loop fusion | flops 18240000 | bytes 26887500 | tf_op jit(solution)/shard_map/sub | solution.py:99
  (113 shorter events, 68.8 us)
Async XLA Ops:
  235.9 13.1 %copy-start.1 = (bf16[1024,1600]{1,0:T(8,128)(2,1)}, bf16[1024,1600]{1,0:T(8,128)(2,1)S(1)}, u32[]{:S(2)}) copy-start(bf16[1024,1600]{1,0:T(8,128)(2,1)S(1)} %concatenate.19) | copy-start | bytes 9830404
  255.5 4.3 copy-start.4
  259.8 3.3 copy-start.2
  259.8 3.3 copy-start.17
  263.1 4.6 copy-start.18
  263.1 4.6 copy-start.11
  272.2 1.2 copy-start.20
  312.6 23.5 %copy-start = (f32[128,1600]{1,0:T(8,128)S(1)}, f32[128,1600]{1,0:T(8,128)}, u32[]{:S(2)}) copy-start(f32[128,1600]{1,0:T(8,128)} %group_scatter.4) | copy-start | bytes 2457604
  429.4 268.9 %collective-permute-start = (bf16[128,3200]{1,0:T(8,128)(2,1)}, bf16[128,3200]{1,0:T(8,128)(2,1)}, u32[]{:S(2)}, u32[]{:S(2)}) collective-permute-start(bf16[128,3200]{1,0:T(8,128)(2,1)} %pad_maximum_fusion), channel_id=1, source_target_pairs={{0,0},{1,16},{2,2},{3,18},{4,8},{5,24},{6,10},{7,26},{8,4},{9,20},... | collective-permute-start | bytes 2457608 | tf_op jit(solution)/shard_map/ppermute | solution.py:1419
  433.2 7.3 %copy-start.12 = (bf16[8,128,1600]{2,1,0:T(8,128)(2,1)S(1)}, bf16[8,128,1600]{2,1,0:T(8,128)(2,1)}, u32[]{:S(2)}) copy-start(bf16[8,128,1600]{2,1,0:T(8,128)(2,1)} %get-tuple-element.33) | copy-start | bytes 9830404
  433.2 7.2 %copy-start.19 = (f32[1024,800]{0,1:T(8,128)S(1)}, f32[1024,800]{0,1:T(8,128)}, u32[]{:S(2)}) copy-start(f32[1024,800]{0,1:T(8,128)} %copy-done.18) | copy-start | bytes 9830404
  440.4 5.6 copy-start.5
  440.4 5.6 copy-start.7
  440.5 5.5 copy-start.9
  446.0 6.3 copy-start.3
  452.3 3.2 copy-start.6
  452.3 3.2 copy-start.8
  452.3 3.2 copy-start.10
  686.2 11.4 %copy-start.13 = (bf16[3,200]{1,0:T(4,128)(2,1)S(1)}, bf16[3,200]{1,0:T(4,128)(2,1)}, u32[]{:S(2)}) copy-start(bf16[3,200]{1,0:T(4,128)(2,1)} %param.13) | copy-start | bytes 3604
  686.2 11.4 %copy-start.14 = (f32[3,200]{1,0:T(4,128)S(1)}, f32[3,200]{1,0:T(4,128)}, u32[]{:S(2)}) copy-start(f32[3,200]{1,0:T(4,128)} %param.17) | copy-start | bytes 7204
  686.2 11.4 %copy-start.15 = (f32[3,200]{1,0:T(4,128)S(1)}, f32[3,200]{1,0:T(4,128)}, u32[]{:S(2)}) copy-start(f32[3,200]{1,0:T(4,128)} %param.16) | copy-start | bytes 7204
  686.2 11.3 %copy-start.16 = (f32[8,256]{1,0:T(8,128)S(1)}, f32[8,256]{1,0:T(8,128)}, u32[]{:S(2)}) copy-start(f32[8,256]{1,0:T(8,128)} %get-tuple-element.45) | copy-start | bytes 24580

commit v3 on v2

--- a/solution.py
+++ b/solution.py
@@ -579,9 +579,10 @@
 
 def forward_kernel(
     x_in, back_in, order_in, vec_in, weights,
-    x_all, back_all, vecs, row_pos, col_pos, w_qkv, h_first, qkv, attn_all, fc, proj, out,
-    flat, rows, qkv_pieces, fc_pieces, blocks, order, vec_all, qkv_land, attn,
-    fc_part, proj_part, out_part,
+    x_all, back_all, vecs, row_pos, col_pos, w_qkv, h_first, qkv, attn_all, attn,
+    w_fc, w_proj, w_out,
+    flat, rows, qkv_pieces, fc_pieces, blocks, order, vec_all, qkv_land,
+    fc, proj, out, fc_part, proj_part, out_part,
     move_sem, qkv_sem, fc_send, fc_recv, rows_sem, x_sem, back_sem, spread_sem,
     own_sem, fc_sem, proj_sem, tree_sem, out_sem, attn_sem,
 ):
@@ -879,12 +880,24 @@
     gather_out = Gather(p, out, out_sem)
     gather_out.begin()
     gather_out.second_hop()
+    for item in fc_y + fc_later:
+        item.wait_recv()
+    for item in own_copies[:8]:
+        item.wait()
     gather_out.third_hop()
+    unit = fc.shape[1]
+    for block in range(DEVICES):
+        w_fc[unit * block : unit * block + unit, :] = fc[block]
     gather_out.last_hop()
+    proj_y.wait_recv()
+    proj_later.wait_recv()
+    proj_own.wait()
+    for group in range(GROUPS):
+        w_proj[four * group : four * group + four, :] = proj[group // 2, group % 2]
     for item in gathers + [gather_out, gather_back]:
         item.finish()
-    for item in fc_y + fc_later + [proj_y, proj_later]:
-        item.wait_recv()
+    for block in range(MEMBERS):
+        w_out[four * block : four * block + four, :] = out[block]
     for item in fc_far + fc_y + fc_later + [proj_far, proj_y, proj_later]:
         item.wait_send()
 
@@ -897,7 +910,7 @@
     def _():
         out_later.wait_send()
 
-    for item in own_copies + [proj_own]:
+    for item in own_copies[8:]:
         item.wait()
     for item in [x_move, order_move, back_move] + qkv_moves + fc_moves + rows_moves:
         item.sent()
@@ -929,12 +942,13 @@
             like(length, width),
             like(length, cols),
             like(pairs, MEMBERS, length, 2 * HD),
-            like(DEVICES, unit, hidden),
-            like(2, 2, four, width),
-            like(MEMBERS, four, width),
+            like(pairs, length, 2 * HD),
+            like(width, hidden),
+            like(hidden, width),
+            like(width, width),
         ],
         in_specs=[any_space] * 4 + [vmem],
-        out_specs=[vmem, any_space] + [vmem] * 6 + [any_space] * 4,
+        out_specs=[vmem, any_space] + [vmem] * 6 + [any_space] + [vmem] * 4,
         scratch_shapes=[
             pltpu.VMEM(weights.shape, high),
             pltpu.VMEM((-(-width // 128), four, 128), high),
@@ -944,7 +958,9 @@
             pltpu.VMEM(order.shape, order.dtype),
             pltpu.VMEM((DEVICES,) + vectors.shape, kind),
             pltpu.VMEM((2, 2, 2, four, cols), kind),
-            pltpu.VMEM((pairs, length, 2 * HD), kind),
+            pltpu.VMEM((DEVICES, unit, hidden), kind),
+            pltpu.VMEM((2, 2, four, width), kind),
+            pltpu.VMEM((MEMBERS, four, width), kind),
             pltpu.VMEM((8, unit, hidden), kind),
             pltpu.VMEM((four, width), kind),
             pltpu.VMEM((four, width), kind),
@@ -970,100 +986,6 @@
     )(x, back, order, vectors, weights)
 
 
-def gather_kernel(own, out, local_sem, sems):
-    p = Place()
-    item = Gather(p, out, sems)
-    greet((item.first, item.second, item.other))
-    for name, index, target in (("a", 0, item.first), ("b", 1, item.second), ("c", 2, item.other)):
-        copy = remote(own, out.at[p.me], sems, index, target)
-        copy.start()
-        item.copies[name] = copy
-    local = pltpu.make_async_copy(own, out.at[p.me], local_sem)
-    local.start()
-    item.second_hop()
-    item.third_hop()
-    item.last_hop()
-    item.finish()
-    local.wait()
-
-
-def group_gather(value, ident):
-    any_space = pl.BlockSpec(memory_space=pl.ANY)
-    return pl.pallas_call(
-        gather_kernel,
-        out_shape=jax.ShapeDtypeStruct((MEMBERS,) + value.shape, value.dtype),
-        in_specs=[any_space],
-        out_specs=any_space,
-        scratch_shapes=[pltpu.SemaphoreType.DMA, pltpu.SemaphoreType.DMA((2, 7))],
-        compiler_params=pltpu.CompilerParams(collective_id=ident, has_side_effects=True),
-        name="group_gather",
-    )(value)
-
-
-def scatter_kernel(part, out, from_core, sums, two, got, last, done, sems):
-    p = Place()
-    route = Gather(p, None, None)
-    greet((route.first, route.second, route.other))
-    copies = []
-    for j in (3, 2, 1, 0):
-        item = remote(part.at[4 * (1 - p.core) + j], from_core.at[j], sems, j, route.other)
-        item.start()
-        copies.append(item)
-    mine = 4 * p.core
-    here, there = p.me - mine, route.of_first - mine
-    beyond, across = route.of_second - mine, route.of_both - mine
-    for item in copies:
-        item.wait_recv()
-
-    def summed(block):
-        return part[mine + block].astype(jnp.float32) + from_core[block].astype(jnp.float32)
-
-    two[0] = summed(across).astype(jnp.bfloat16)
-    send_across = remote(two.at[0], got.at[0], sems, 4, route.second)
-    send_across.start()
-    two[1] = summed(beyond).astype(jnp.bfloat16)
-    send_beyond = remote(two.at[1], got.at[1], sems, 5, route.second)
-    send_beyond.start()
-    sums[...] = summed(there)
-    send_across.wait_recv()
-    last[...] = (sums[...] + got[0].astype(jnp.float32)).astype(jnp.bfloat16)
-    send_last = remote(last, done, sems, 6, route.first)
-    send_last.start()
-    sums[...] = summed(here)
-    send_beyond.wait_recv()
-    sums[...] += got[1].astype(jnp.float32)
-    send_last.wait_recv()
-    out[...] = sums[...] + done[...].astype(jnp.float32)
-    for item in copies + [send_across, send_beyond, send_last]:
-        item.wait_send()
-
-
-def group_scatter(value, ident):
-    rows, width = value.shape
-    rows = rows // MEMBERS
-    low = jnp.bfloat16
-    vmem = pl.BlockSpec(memory_space=pltpu.VMEM)
-    return pl.pallas_call(
-        scatter_kernel,
-        out_shape=jax.ShapeDtypeStruct((rows, width), jnp.float32),
-        in_specs=[vmem],
-        out_specs=vmem,
-        scratch_shapes=[
-            pltpu.VMEM((4, rows, width), low),
-            pltpu.VMEM((rows, width), jnp.float32),
-            pltpu.VMEM((2, rows, width), low),
-            pltpu.VMEM((2, rows, width), low),
-            pltpu.VMEM((rows, width), low),
-            pltpu.VMEM((rows, width), low),
-            pltpu.SemaphoreType.DMA((2, 7)),
-        ],
-        compiler_params=pltpu.CompilerParams(
-            collective_id=ident, has_side_effects=True, vmem_limit_bytes=VMEM_BYTES
-        ),
-        name="group_scatter",
-    )(value.reshape(MEMBERS, rows, width))
-
-
 def wide(value):
     return value.astype(jnp.float32)
 
@@ -1072,37 +994,295 @@
     return value.astype(jnp.bfloat16)
 
 
+GELU_SCALE = 0.7978845608028654
+GELU_CUBE = 0.044715
+
+
+class Reduce:
+    def __init__(self, place, part, from_core, two, got, last, done, sems):
+        self.p, self.part, self.from_core = place, part, from_core
+        self.two, self.got, self.last, self.done, self.sems = two, got, last, done, sems
+        self.route = Gather(place, None, None)
+        self.copies = []
+
+    def _go(self, source, landing, index, target):
+        item = remote(source, landing, self.sems, index, target)
+        item.start()
+        self.copies.append(item)
+        return item
+
+    def begin(self):
+        p = self.p
+        for j in (3, 2, 1, 0):
+            self._go(
+                self.part.at[4 * (1 - p.core) + j], self.from_core.at[j], j, self.route.other
+            )
+
+    def _summed(self, member):
+        block = member - 4 * self.p.core
+        return wide(self.part[member]) + wide(self.from_core[block])
+
+    def second(self):
+        for item in self.copies[:4]:
+            item.wait_recv()
+        self.two[0] = low(self._summed(self.route.of_both))
+        self.across = self._go(self.two.at[0], self.got.at[0], 4, self.route.second)
+        self.two[1] = low(self._summed(self.route.of_second))
+        self.beyond = self._go(self.two.at[1], self.got.at[1], 5, self.route.second)
+
+    def third(self):
+        self.across.wait_recv()
+        self.last[...] = low(self._summed(self.route.of_first) + wide(self.got[0]))
+        self.final = self._go(self.last, self.done, 6, self.route.first)
+
+    def result(self):
+        self.beyond.wait_recv()
+        value = self._summed(self.p.me) + wide(self.got[1])
+        self.final.wait_recv()
+        return value + wide(self.done[...])
+
+    def sent(self):
+        for item in self.copies:
+            item.wait_send()
+
+
+def reduce_buffers(rows, width):
+    kind = jnp.bfloat16
+    return [
+        pltpu.VMEM((4, rows, width), kind),
+        pltpu.VMEM((2, rows, width), kind),
+        pltpu.VMEM((2, rows, width), kind),
+        pltpu.VMEM((rows, width), kind),
+        pltpu.VMEM((rows, width), kind),
+        pltpu.SemaphoreType.DMA((2, 7)),
+    ]
+
+
+def store_rows(target, first, value, lanes=slice(None)):
+    size = target.shape[1]
+    row = 0
+    while row < value.shape[0]:
+        block, at = divmod(first + row, size)
+        count = min(size - at, value.shape[0] - row)
+        target[block, at : at + count, lanes] = low(value[row : row + count])
+        row += count
+
+
+def middle_kernel(
+    x_all, attn_all, back_all, vecs, w_out_in, w_fc_in, w_proj_in,
+    grad_fc, grad_proj, made, resid_own, dresid, dbranch, sums, fc_sums,
+    h_second, attn, back, w_out, w_fc, w_proj, act, dpre, dh_part, made_part, g_fc, g_proj,
+    resid, from_core, two, got, last, done, reduce_sem, load_sem, store_sem,
+):
+    p = Place()
+    length, width = h_second.shape
+    count = length // MEMBERS
+    hidden = act.shape[1]
+    pairs = attn.shape[0]
+    loads = []
+    for index, (source, target) in enumerate(
+        (
+            (attn_all, attn), (w_out_in, w_out), (x_all, h_second),
+            (w_fc_in, w_fc), (back_all, back), (w_proj_in, w_proj),
+        )
+    ):
+        copy = pltpu.make_async_copy(source, target, load_sem.at[index])
+        copy.start()
+        loads.append(copy)
+    reduce = Reduce(p, dh_part, from_core, two, got, last, done, reduce_sem)
+    route = reduce.route
+    greet((route.first, route.second, route.other))
+    bias_fc = jnp.zeros((1, hidden), jnp.float32)
+    for member in range(MEMBERS):
+        row = (34, 48, 49, 50)[member // 2]
+        first = hidden * (member % 2)
+        bias_fc = bias_fc + jnp.where(
+            p.me == member, vecs[row : row + 1, first : first + hidden], 0.0
+        )
+    fc_sums[...] = jnp.zeros_like(fc_sums)
+    for copy in loads:
+        copy.wait()
+    span = 2 * count
+
+    def one_block(step, carry):
+        at = pl.ds(pl.multiple_of(step * span, span), span)
+        total = wide(h_second[at, :]) + vecs[17:18, :]
+        for member in range(MEMBERS):
+            first = head_start(member) * HD
+            used = (head_start(member + 1) - head_start(member)) * HD
+            heads = jnp.concatenate([attn[pair, member, at, :] for pair in range(pairs)], 1)
+            if used < SLOTS * HD:
+                lane = lax.broadcasted_iota(jnp.int32, heads.shape, 1)
+                heads = jnp.where(lane < used, heads, jnp.zeros_like(heads))
+            total = total + jnp.dot(
+                heads, w_out[first : first + SLOTS * HD, :], preferred_element_type=jnp.float32
+            )
+        resid[...] = total
+
+        @pl.when(step == p.me // 2)
+        def _():
+            resid_own[...] = resid[pl.ds(pl.multiple_of(p.me % 2 * count, count), count), :]
+
+        normed = low(norm_rows(total, vecs[18:19, :], vecs[32:33, :]))
+        h_second[at, :] = normed
+        pre = jnp.dot(normed, w_fc[...], preferred_element_type=jnp.float32) + bias_fc
+        square = pre * pre
+        slope = jnp.tanh(GELU_SCALE * (pre + GELU_CUBE * pre * square))
+        act[at, :] = low(0.5 * pre * (1.0 + slope))
+        tilt = 0.5 * (1.0 + slope) + 0.5 * pre * (1.0 - slope * slope) * GELU_SCALE * (
+            1.0 + 3.0 * GELU_CUBE * square
+        )
+        dpre_block = low(dot_nt(back[at, :], w_proj[...]) * tilt)
+        dpre[at, :] = dpre_block
+        fc_sums[...] += jnp.sum(wide(dpre_block), 0, keepdims=True)
+        value = low(dot_nt(dpre_block, w_fc[...]))
+        dh_part[2 * step] = value[:count]
+        dh_part[2 * step + 1] = value[count:]
+        return carry
+
+    lax.fori_loop(0, MEMBERS // 2, one_block, 0)
+    reduce.begin()
+    chunk = 256
+
+    def one_proj(step, carry):
+        lanes = pl.ds(pl.multiple_of(step * chunk, chunk), chunk)
+        store_rows(g_proj, 0, dot_tn(act[...], back[:, lanes]), lanes)
+        return carry
+
+    lax.fori_loop(0, 3, one_proj, 0)
+    reduce.second()
+    lax.fori_loop(3, width // chunk, one_proj, 0)
+    tail = slice(width // chunk * chunk, width)
+    if width % chunk:
+        store_rows(g_proj, 0, dot_tn(act[...], back[:, tail]), tail)
+    stores = [pltpu.make_async_copy(g_proj, grad_proj, store_sem.at[0])]
+    stores[0].start()
+    for first in range(0, width, chunk):
+        size = min(chunk, width - first)
+        store_rows(g_fc, first, dot_tn(h_second[:, first : first + size], dpre[...]))
+        if first + size == 4 * chunk:
+            reduce.third()
+    stores.append(pltpu.make_async_copy(g_fc, grad_fc, store_sem.at[1]))
+    stores[1].start()
+
+    def one_made(step, carry):
+        at = pl.ds(pl.multiple_of(step * span, span), span)
+        value = low(jnp.dot(act[at, :], w_proj[...], preferred_element_type=jnp.float32))
+        made_part[2 * step] = value[:count]
+        made_part[2 * step + 1] = value[count:]
+        return carry
+
+    lax.fori_loop(0, MEMBERS // 2, one_made, 0)
+    stores.append(pltpu.make_async_copy(made_part, made, store_sem.at[2]))
+    stores[2].start()
+    dh = reduce.result()
+    center = resid_own[...] - jnp.mean(resid_own[...], -1, keepdims=True)
+    scale = lax.rsqrt(jnp.mean(center * center, -1, keepdims=True) + epsilon_norm)
+    hat = center * scale
+    back_own = wide(back[pl.ds(pl.multiple_of(p.me * count, count), count), :])
+    scaled = dh * vecs[18:19, :]
+    inner = jnp.mean(scaled * hat, -1, keepdims=True)
+    value = back_own + (scaled - jnp.mean(scaled, -1, keepdims=True) - hat * inner) * scale
+    dresid[...] = value
+    branch = low(value)
+    dbranch[...] = branch
+    sums[0:1, :] = jnp.sum(dh * hat, 0, keepdims=True)
+    sums[1:2, :] = jnp.sum(dh, 0, keepdims=True)
+    sums[2:3, :] = jnp.sum(wide(branch), 0, keepdims=True)
+    sums[3:4, :] = jnp.sum(back_own, 0, keepdims=True)
+    sums[4:8, :] = jnp.zeros((4, width), jnp.float32)
+    reduce.sent()
+    for copy in stores:
+        copy.wait()
+
+
+def middle(x_all, attn_all, back_all, vecs, w_out, w_fc, w_proj):
+    kind, high = jnp.bfloat16, jnp.float32
+    length, width = x_all.shape
+    rows = length // MEMBERS
+    hidden = w_proj.shape[0]
+    four = width // MEMBERS
+    any_space = pl.BlockSpec(memory_space=pl.ANY)
+    vmem = pl.BlockSpec(memory_space=pltpu.VMEM)
+    dma = pltpu.SemaphoreType.DMA
+
+    def like(*shape, dtype=kind):
+        return jax.ShapeDtypeStruct(shape, dtype)
+
+    def buffer(*shape, dtype=kind):
+        return pltpu.VMEM(shape, dtype)
+
+    return pl.pallas_call(
+        middle_kernel,
+        out_shape=[
+            like(MEMBERS, four, hidden),
+            like(GROUPS, four, width),
+            like(MEMBERS, rows, width),
+            like(rows, width, dtype=high),
+            like(rows, width, dtype=high),
+            like(rows, width),
+            like(8, width, dtype=high),
+            like(1, hidden, dtype=high),
+        ],
+        in_specs=[any_space] * 3 + [vmem] + [any_space] * 3,
+        out_specs=[any_space] * 3 + [vmem] * 5,
+        scratch_shapes=[
+            buffer(*x_all.shape),
+            buffer(*attn_all.shape),
+            buffer(*back_all.shape),
+            buffer(*w_out.shape),
+            buffer(*w_fc.shape),
+            buffer(*w_proj.shape),
+            buffer(length, hidden),
+            buffer(length, hidden),
+            buffer(MEMBERS, rows, width),
+            buffer(MEMBERS, rows, width),
+            buffer(MEMBERS, four, hidden),
+            buffer(GROUPS, four, width),
+            buffer(2 * rows, width, dtype=high),
+        ]
+        + reduce_buffers(rows, width)
+        + [dma((6,)), dma((3,))],
+        compiler_params=pltpu.CompilerParams(
+            collective_id=3, has_side_effects=True, vmem_limit_bytes=VMEM_BYTES
+        ),
+        name="middle",
+    )(x_all, attn_all, back_all, vecs, w_out, w_fc, w_proj)
+
+
 class Fold:
-    def __init__(self, place, at, landing, leaving, last, sems, first):
+    def __init__(self, place, away, kept, landing, leaving, last, sems, first):
         p = place
-        self.p, self.at, self.landing, self.leaving, self.last = p, at, landing, leaving, last
+        self.p, self.away, self.kept, self.landing = p, away, kept, landing
+        self.leaving, self.last = leaving, last
         self.to_far, self.to_y = p.target(far=1 - p.far), p.target(y=1 - p.y)
         self.sems, self.first = sems, first
 
     def begin(self):
-        p = self.p
-        other = 1 - p.far
+        other = 1 - self.p.far
         self.a = remote(
-            self.at(other, 1 - p.y), self.landing(other), self.sems, self.first, self.to_y
-        )
+            self.away(other), self.landing(other), self.sems, self.first, self.to_y
+        )
+        self.a.start()
+
+    def rest(self):
+        far = self.p.far
         self.b = remote(
-            self.at(p.far, 1 - p.y), self.landing(p.far), self.sems, self.first + 1, self.to_y
-        )
-        self.a.start()
+            self.away(far), self.landing(far), self.sems, self.first + 1, self.to_y
+        )
         self.b.start()
 
     def middle(self):
-        p = self.p
-        other = 1 - p.far
+        other = 1 - self.p.far
         self.a.wait_recv()
-        self.leaving[...] = low(wide(self.at(other, p.y)[...]) + wide(self.landing(other)[...]))
+        self.leaving[...] = low(wide(self.kept(other)[...]) + wide(self.landing(other)[...]))
         self.c = remote(self.leaving, self.last, self.sems, self.first + 2, self.to_far)
         self.c.start()
 
     def end(self):
-        p = self.p
+        far = self.p.far
         self.b.wait_recv()
-        partial = wide(self.at(p.far, p.y)[...]) + wide(self.landing(p.far)[...])
+        partial = wide(self.kept(far)[...]) + wide(self.landing(far)[...])
         self.c.wait_recv()
         return low(partial + wide(self.last[...]))
 
@@ -1111,88 +1291,267 @@
             item.wait_send()
 
 
-def yield_kernel(
-    qkv, fc, proj, out, vec,
-    qkv_back, fc_back, rows_back, vec_back,
-    qkv_y, fc_y, proj_y, out_y, qkv_go, fc_go, proj_go, out_go,
-    qkv_far, fc_far, proj_far, out_far, qkv_sum, fc_sum, proj_sum, out_sum, vec_got,
-    fold_sem, tree_sem, vec_sem, qkv_send, qkv_recv, fc_send, fc_recv, rows_send, rows_recv,
+def backward_kernel(
+    dbranch, made_in, grad_fc, grad_proj, attn, qkv, row_pos, col_pos, w_out, w_qkv_in,
+    h_in, x_all, resid_own, dresid, vecs, sums, fc_sums,
+    out_home, grad_home, qkv_back, fc_back, rows_back, vec_back,
+    branch_all, dattn, dqkv, key_sum, value_sum, w_heads, w_qkv, h_first, x_own, made, dh_part,
+    fc_own, proj_own, g_qkv, g_heads, g_out, result, input_grad, vec_rows, vec_go, vec_got,
+    fc_y, proj_y, qkv_y, out_y, fc_go, proj_go, qkv_go, out_go,
+    fc_far, proj_far, qkv_far, out_far, fc_sum, proj_sum, qkv_sum, out_sum,
+    core_a, two_a, got_a, last_a, done_a, sem_a, core_b, two_b, got_b, last_b, done_b, sem_b,
+    load_sem, branch_sem, fold_sem, tree_sem, vec_sem, home_sem,
+    qkv_send, qkv_recv, fc_send, fc_recv, rows_send, rows_recv,
 ):
     p = Place()
-    unit = fc_back.shape[2]
+    count, width = dbranch.shape
+    length = MEMBERS * count
+    four, unit = grad_proj.shape[1], fc_back.shape[2]
+    pairs = SLOTS // 2
+    per_part = SLOTS * HD
+    first_head = HEADS * p.me // MEMBERS * HD
+    loads = []
+
+    def load(source, target):
+        copy = pltpu.make_async_copy(source, target, load_sem.at[len(loads)])
+        copy.start()
+        loads.append(copy)
+
+    load(w_out.at[pl.ds(pl.multiple_of(first_head, HD), per_part)], w_heads)
+    load(x_all.at[p.me], x_own)
+    for far in range(2):
+        load(grad_proj.at[2 * p.y + far], proj_own.at[far])
+        for near in range(2):
+            load(grad_fc.at[4 * far + 2 * near + p.y], fc_own.at[far, near])
+    load(made_in, made)
+    load(w_qkv_in, w_qkv)
+    load(h_in, h_first)
     greet_all(p)
-    folds = [
+    gather = Gather(p, branch_all, branch_sem)
+    for name, index, target in (
+        ("a", 0, gather.first), ("b", 1, gather.second), ("c", 2, gather.other),
+    ):
+        copy = remote(dbranch, branch_all.at[p.me], branch_sem, index, target)
+        copy.start()
+        gather.copies[name] = copy
+    load(dbranch, branch_all.at[p.me])
+    proj_fold = Fold(
+        p, lambda far: grad_proj.at[2 * (1 - p.y) + far], lambda far: proj_own.at[far],
+        lambda far: proj_y.at[far], proj_go, proj_far, fold_sem, 0,
+    )
+    fc_folds = [
         Fold(
-            p, lambda far, y: proj.at[y, far], lambda far: proj_y.at[far],
-            proj_go, proj_far, fold_sem, 0,
-        )
+            p, lambda far, near=near: grad_fc.at[4 * far + 2 * near + 1 - p.y],
+            lambda far, near=near: fc_own.at[far, near],
+            lambda far, near=near: fc_y.at[far, near],
+            fc_go.at[near], fc_far.at[near], fold_sem, 3 + 3 * near,
+        )
+        for near in range(2)
     ]
-    for near in range(2):
-        folds.append(
-            Fold(
-                p, lambda far, y, near=near: fc.at[far, near, y],
-                lambda far, near=near: fc_y.at[far, near],
-                fc_go.at[near], fc_far.at[near], fold_sem, 3 + 3 * near,
-            )
-        )
-    for near in range(2):
-        folds.append(
-            Fold(
-                p, lambda far, y, near=near: qkv.at[far, near, y],
-                lambda far, near=near: qkv_y.at[far, near],
-                qkv_go.at[near], qkv_far.at[near], fold_sem, 9 + 3 * near,
-            )
-        )
-    for item in folds:
+    qkv_folds = [
+        Fold(
+            p, lambda far, near=near: g_qkv.at[4 * far + 2 * near + 1 - p.y],
+            lambda far, near=near: g_qkv.at[4 * far + 2 * near + p.y],
+            lambda far, near=near: qkv_y.at[far, near],
+            qkv_go.at[near], qkv_far.at[near], fold_sem, 9 + 3 * near,
+        )
+        for near in range(2)
+    ]
+    proj_fold.begin()
+    for item in fc_folds:
         item.begin()
-    root_y, root_far = p.me % 4 // 2, p.me % 2
-    same_y, same_far = p.y == root_y, p.far == root_far
-    root = jnp.logical_and(same_y, same_far)
-    beside = jnp.logical_and(same_y, jnp.logical_not(same_far))
-    over_y = remote(out, out_y, tree_sem, 0, p.target(y=1 - p.y))
+    gather.second_hop()
+    gather.third_hop()
+    gather.last_hop()
+    for copy in loads:
+        copy.wait()
+    proj_fold.middle()
+    gather.finish()
+    span = 2 * count
+
+    def one_dattn(step, carry):
+        at = pl.ds(pl.multiple_of(step * span, span), span)
+        grad = jnp.concatenate([branch_all[2 * step], branch_all[2 * step + 1]], 0)
+        value = low(dot_nt(grad, w_heads[...]))
+        for pair in range(pairs):
+            dattn[pair, at, :] = value[:, 128 * pair : 128 * pair + 128]
+        return carry
+
+    lax.fori_loop(0, length // span, one_dattn, 0)
+    reduce_made = Reduce(p, made, core_a, two_a, got_a, last_a, done_a, sem_a)
+    reduce_made.begin()
+    proj_fold.rest()
+
+    def one_pair(pair):
+        key_sum[...] = jnp.zeros_like(key_sum)
+        value_sum[...] = jnp.zeros_like(value_sum)
+
+        def columns(part):
+            return slice(128 * (pairs * part + pair), 128 * (pairs * part + pair) + 128)
+
+        def one_block(step, carry):
+            at = pl.ds(pl.multiple_of(step * span, span), span)
+            query, grad = qkv[at, columns(0)], dattn[pair, at, :]
+            keys, values = qkv[:, columns(1)], qkv[:, columns(2)]
+            lanes = lane_of(query.shape)
+            total = jnp.zeros(query.shape, jnp.float32)
+            add_keys = add_values = 0.0
+            for head in range(2):
+                mine = lanes == head
+                own = jnp.where(mine, query, jnp.zeros_like(query))
+                own_grad = jnp.where(mine, grad, jnp.zeros_like(grad))
+                probs = probabilities(own, keys, row_pos[at, :], col_pos[...])
+                dprobs = dot_nt(own_grad, values)
+                delta = jnp.sum(probs * dprobs, -1, keepdims=True)
+                dscores = low(probs * (dprobs - delta))
+                mixed = jnp.dot(dscores, keys, preferred_element_type=jnp.float32)
+                total = jnp.where(mine, mixed, total)
+                add_keys = add_keys + dot_tn(dscores, own)
+                add_values = add_values + dot_tn(low(probs), own_grad)
+            dqkv[at, columns(0)] = low(total * 0.125)
+            key_sum[...] += add_keys
+            value_sum[...] += add_values
+            return carry
+
+        lax.fori_loop(0, length // span, one_block, 0)
+        dqkv[:, columns(1)] = low(key_sum[...] * 0.125)
+        dqkv[:, columns(2)] = low(value_sum[...])
+
+    one_pair(0)
+    for item in fc_folds:
+        item.middle()
+    for item in fc_folds:
+        item.rest()
+    reduce_made.second()
+    one_pair(1)
+    reduce_made.third()
+    for part in range(3):
+        last = 128 * (pairs * part + pairs - 1)
+        value = dqkv[:, last : last + 128]
+        keep = jnp.logical_or(lane_of(value.shape) == 0, p.me == MEMBERS - 1)
+        dqkv[:, last : last + 128] = jnp.where(keep, value, jnp.zeros_like(value))
+
+    def one_part(step, carry):
+        at = pl.ds(pl.multiple_of(step * span, span), span)
+        value = low(dot_nt(dqkv[at, :], w_qkv[...]))
+        dh_part[2 * step] = value[:count]
+        dh_part[2 * step + 1] = value[count:]
+        return carry
+
+    lax.fori_loop(0, length // span, one_part, 0)
+    reduce_dh = Reduce(p, dh_part, core_b, two_b, got_b, last_b, done_b, sem_b)
+    reduce_dh.begin()
+    chunk = 256
+    for first in range(0, width, chunk):
+        size = min(chunk, width - first)
+        store_rows(g_qkv, first, dot_tn(h_first[:, first : first + size], dqkv[...]))
+    for item in qkv_folds:
+        item.begin()
+    for item in qkv_folds:
+        item.rest()
+    reduce_dh.second()
+    for pair in range(pairs):
+        total = 0.0
+        for block in range(MEMBERS):
+            at = slice(block * count, block * count + count)
+            total = total + dot_tn(attn[pair, at, :], branch_all[block])
+        g_heads[128 * pair : 128 * pair + 128, :] = total
+    g_out[...] = low(g_heads[pl.ds(pl.multiple_of(four * p.me - first_head, 8), four), :])
+    root_y = out_root(p.me)
+    same_y = p.y == root_y
+    root = jnp.logical_and(same_y, p.far == 0)
+    beside = jnp.logical_and(same_y, p.far == 1)
+    over_y = remote(g_out, out_y, tree_sem, 0, p.target(y=1 - p.y))
     over_far = remote(out_go, out_far, tree_sem, 1, p.target(far=1 - p.far))
 
     @pl.when(jnp.logical_not(same_y))
     def _():
         over_y.start()
 
-    def vec_copy(step):
+    reduce_dh.third()
+    result[...] = low(resid_own[...] + reduce_made.result() + vecs[33:34, :])
+    home = p.target(
+        x=p.ctx % 2, near=p.ctx // 2 % 2, core=p.ctx // 4, y=p.fsdp // 2, far=p.fsdp % 2
+    )
+    moves = [Move(p, result, out_home, home_sem.at[0, 0], home_sem.at[1, 0], home)]
+
+    @pl.when(same_y)
+    def _():
+        over_y.wait_recv()
+
+    @pl.when(beside)
+    def _():
+        out_go[...] = low(wide(g_out[...]) + wide(out_y[...]))
+        over_far.start()
+
+    dh = reduce_dh.result()
+    x = wide(x_own[...])
+    center = x - jnp.mean(x, -1, keepdims=True)
+    scale = lax.rsqrt(jnp.mean(center * center, -1, keepdims=True) + epsilon_norm)
+    hat = center * scale
+    scaled = dh * vecs[0:1, :]
+    inner = jnp.mean(scaled * hat, -1, keepdims=True)
+    value = (scaled - jnp.mean(scaled, -1, keepdims=True) - hat * inner) * scale
+    input_grad[...] = low(dresid[...] + value)
+    moves.append(Move(p, input_grad, grad_home, home_sem.at[0, 1], home_sem.at[1, 1], home))
+    bias_sums = jnp.sum(wide(dqkv[...]), 0, keepdims=True)
+
+    def placed(value, starts, me):
+        total = jnp.zeros((1, width), jnp.float32)
+        for index, start in enumerate(starts):
+            parts = [value]
+            if start:
+                parts.insert(0, jnp.zeros((1, start), jnp.float32))
+            after = width - start - value.shape[1]
+            if after:
+                parts.append(jnp.zeros((1, after), jnp.float32))
+            row = jnp.concatenate(parts, 1) if len(parts) > 1 else value
+            total = total + jnp.where(me == index, row, 0.0)
+        return total
+
+    heads = [head_start(member) * HD for member in range(MEMBERS)]
+    vec_rows[0:1, :] = jnp.sum(dh * hat, 0, keepdims=True)
+    vec_rows[1:2, :] = jnp.sum(dh, 0, keepdims=True)
+    vec_rows[2:3, :] = placed(bias_sums[:, :per_part], heads, p.me)
+    vec_rows[3:4, :] = placed(bias_sums[:, 2 * per_part :], heads, p.me)
+    vec_rows[4:5, :] = sums[2:3, :]
+    vec_rows[5:7, :] = sums[0:2, :]
+    vec_rows[7:8, :] = sums[3:4, :]
+    hidden = fc_sums.shape[1]
+    fc_row = placed(fc_sums[...], (0, hidden), p.me % 2)
+    for row in range(GROUPS):
+        vec_rows[8 + row : 9 + row, :] = jnp.where(p.me // 2 == row, fc_row, 0.0)
+    used = width // MEMBERS
+    vec_go[...] = jnp.zeros_like(vec_go)
+    for f in range(GROUPS):
+        for c in range(MEMBERS):
+            vec_go[MEMBERS * f + c, 0:3, 0:used] = vec_rows[
+                3 * f : 3 * f + 3, used * c : used * c + used
+            ]
+
+    def vec_send(step, carry):
         other = (p.linear + step) % DEVICES
-        return pltpu.make_async_remote_copy(
-            src_ref=vec.at[other],
+        pltpu.make_async_remote_copy(
+            src_ref=vec_go.at[other],
             dst_ref=vec_got.at[p.linear],
             send_sem=vec_sem.at[0],
             recv_sem=vec_sem.at[1],
             device_id=(other // MEMBERS, other % MEMBERS),
             device_id_type=MESH,
-        )
-
-    def vec_send(step, carry):
-        vec_copy(step).start()
+        ).start()
         return carry
 
     lax.fori_loop(1, DEVICES, vec_send, 0)
-    pltpu.make_async_copy(vec.at[p.linear], vec_got.at[p.linear], vec_sem.at[1]).start()
-    for item in folds:
+    pltpu.make_async_copy(vec_go.at[p.linear], vec_got.at[p.linear], vec_sem.at[1]).start()
+    for item in qkv_folds:
         item.middle()
-
-    @pl.when(same_y)
-    def _():
-        over_y.wait_recv()
-
-    @pl.when(beside)
-    def _():
-        out_go[...] = low(wide(out[...]) + wide(out_y[...]))
-        over_far.start()
-
-    moves = []
-    proj_sum[...] = folds[0].end()
+    proj_sum[...] = proj_fold.end()
     target, part = shard_of(PROJ_FIRST + 4 * p.me + p.group)
     moves.append(
         Move(p, proj_sum, rows_back.at[part], rows_send.at[0], rows_recv.at[part], target)
     )
     for near in range(2):
-        block = folds[1 + near].end()
+        block = fc_folds[near].end()
         for slot in range(4):
             fc_sum[near, slot] = block[slot * unit : (slot + 1) * unit]
             third = FC_FIRST + 4 * (4 * p.far + 2 * near + p.y) + slot
@@ -1207,14 +1566,14 @@
     @pl.when(root)
     def _():
         over_far.wait_recv()
-        out_sum[...] = low(wide(out[...]) + wide(out_y[...]) + wide(out_far[...]))
+        out_sum[...] = low(wide(g_out[...]) + wide(out_y[...]) + wide(out_far[...]))
 
     target, part = shard_of(OUT_FIRST + p.me)
     moves.append(
         Move(p, out_sum, rows_back.at[part], rows_send.at[1], rows_recv.at[part], target, root)
     )
     for near in range(2):
-        qkv_sum[near] = folds[3 + near].end()
+        qkv_sum[near] = qkv_folds[near].end()
         target = (0 * p.fsdp, 4 * p.far + 2 * near + p.y)
         moves.append(
             Move(
@@ -1222,6 +1581,9 @@
                 target,
             )
         )
+    arrived(vec_got, vec_sem.at[1])
+    vec_back[...] = jnp.sum(vec_got[...], 0)
+
     @pl.when(p.fsdp == 0)
     def _():
         for member in range(MEMBERS):
@@ -1241,10 +1603,10 @@
         def _(part=part):
             arrived(rows_back.at[part], rows_recv.at[part])
 
-    arrived(vec_got, vec_sem.at[1])
-    vec_back[...] = jnp.sum(vec_got[...], 0)
+    arrived(out_home, home_sem.at[1, 0])
+    arrived(grad_home, home_sem.at[1, 1])
     arrived(vec_got.at[pl.ds(1, DEVICES - 1)], vec_sem.at[0])
-    for item in folds:
+    for item in [proj_fold, reduce_made, reduce_dh] + fc_folds + qkv_folds + moves:
         item.sent()
 
     @pl.when(jnp.logical_not(same_y))
@@ -1255,54 +1617,85 @@
     def _():
         over_far.wait_send()
 
-    for item in moves:
-        item.sent()
-
-
-def yield_grads(qkv, fc, proj, out, vec):
-    kind = jnp.bfloat16
-    four, wide_qkv = qkv.shape[-2:]
-    hidden = fc.shape[-1]
-    width = proj.shape[-1]
-    unit = four // 4
+
+def backward(
+    dbranch, made, grad_fc, grad_proj, attn, qkv, row_pos, col_pos, w_out, w_qkv,
+    h_first, x_all, resid_own, dresid, vecs, sums, fc_sums,
+):
+    kind, high = jnp.bfloat16, jnp.float32
+    rows, width = dbranch.shape
+    length = MEMBERS * rows
+    four, cols = width // MEMBERS, qkv.shape[1]
+    unit, hidden = four // 4, fc_sums.shape[1]
+    per_part = SLOTS * HD
     any_space = pl.BlockSpec(memory_space=pl.ANY)
     vmem = pl.BlockSpec(memory_space=pltpu.VMEM)
+    dma = pltpu.SemaphoreType.DMA
+
+    def like(*shape, dtype=kind):
+        return jax.ShapeDtypeStruct(shape, dtype)
 
     def buffer(*shape, dtype=kind):
         return pltpu.VMEM(shape, dtype)
 
-    dma = pltpu.SemaphoreType.DMA
+    used = -(-width // MEMBERS // 128) * 128
     return pl.pallas_call(
-        yield_kernel,
+        backward_kernel,
         out_shape=[
-            jax.ShapeDtypeStruct((MEMBERS, four, wide_qkv), kind),
-            jax.ShapeDtypeStruct((3, MEMBERS, unit, hidden), kind),
-            jax.ShapeDtypeStruct((3, four, width), kind),
-            jax.ShapeDtypeStruct(vec.shape[1:], vec.dtype),
+            like(rows, width),
+            like(rows, width),
+            like(MEMBERS, four, cols),
+            like(3, MEMBERS, unit, hidden),
+            like(3, four, width),
+            like(8, used, dtype=high),
         ],
-        in_specs=[vmem] * 5,
-        out_specs=[any_space, any_space, any_space, vmem],
+        in_specs=[vmem] + [any_space] * 3 + [vmem] * 4 + [any_space] * 4 + [vmem] * 5,
+        out_specs=[any_space] * 5 + [vmem],
         scratch_shapes=[
-            buffer(2, 2, four, wide_qkv),
+            buffer(MEMBERS, rows, width),
+            buffer(SLOTS // 2, length, 2 * HD),
+            buffer(length, cols),
+            buffer(length, 2 * HD, dtype=high),
+            buffer(length, 2 * HD, dtype=high),
+            buffer(per_part, width),
+            buffer(*w_qkv.shape),
+            buffer(*h_first.shape),
+            buffer(rows, width),
+            buffer(MEMBERS, rows, width),
+            buffer(MEMBERS, rows, width),
             buffer(2, 2, four, hidden),
             buffer(2, four, width),
+            buffer(MEMBERS, four, cols),
+            buffer(per_part, width, dtype=high),
             buffer(four, width),
-            buffer(2, four, wide_qkv),
-            buffer(2, four, hidden),
+            buffer(rows, width),
+            buffer(rows, width),
+            buffer(16, width, dtype=high),
+            buffer(DEVICES, 8, used, dtype=high),
+            buffer(DEVICES, 8, used, dtype=high),
+        ]
+        + [
+            buffer(2, 2, four, hidden), buffer(2, four, width), buffer(2, 2, four, cols),
             buffer(four, width),
+        ]
+        + [
+            buffer(2, four, hidden), buffer(four, width), buffer(2, four, cols),
             buffer(four, width),
-            buffer(2, four, wide_qkv),
-            buffer(2, four, hidden),
+        ]
+        * 2
+        + [
+            buffer(2, 4, unit, hidden), buffer(four, width), buffer(2, four, cols),
             buffer(four, width),
-            buffer(four, width),
-            buffer(2, four, wide_qkv),
-            buffer(2, 4, unit, hidden),
-            buffer(four, width),
-            buffer(four, width),
-            buffer(*vec.shape, dtype=vec.dtype),
+        ]
+        + reduce_buffers(rows, width)
+        + reduce_buffers(rows, width)
+        + [
+            dma((12,)),
+            dma((2, 7)),
             dma((2, 15)),
             dma((2, 2)),
             dma((2,)),
+            dma((2, 2)),
             dma((2,)),
             dma((8,)),
             dma((2, 4)),
@@ -1313,8 +1706,11 @@
         compiler_params=pltpu.CompilerParams(
             collective_id=2, has_side_effects=True, vmem_limit_bytes=VMEM_BYTES
         ),
-        name="yield_grads",
-    )(qkv, fc, proj, out, vec)
+        name="backward",
+    )(
+        dbranch, made, grad_fc, grad_proj, attn, qkv, row_pos, col_pos, w_out, w_qkv,
+        h_first, x_all, resid_own, dresid, vecs, sums, fc_sums,
+    )
 
 
 def lane_of(shape):
@@ -1336,87 +1732,12 @@
     return weights / jnp.sum(weights, -1, keepdims=True)
 
 
-def attend_back_kernel(
-    query, keys, values, grad, row_pos, col_pos, dquery, dkeys, dvalues, key_sum, value_sum
-):
-    step = pl.program_id(1)
-
-    @pl.when(step == 0)
-    def _():
-        key_sum[...] = jnp.zeros_like(key_sum)
-        value_sum[...] = jnp.zeros_like(value_sum)
-
-    lanes = lane_of(query.shape)
-    result = jnp.zeros(query.shape, jnp.float32)
-    add_keys = add_values = 0.0
-    for head in range(2):
-        mine = lanes == head
-        own = jnp.where(mine, query[...], jnp.zeros_like(query))
-        own_grad = jnp.where(mine, grad[...], jnp.zeros_like(grad))
-        probs = probabilities(own, keys[...], row_pos[...], col_pos[...])
-        dprobs = dot_nt(own_grad, values[...])
-        delta = jnp.sum(probs * dprobs, -1, keepdims=True)
-        dscores = (probs * (dprobs - delta)).astype(jnp.bfloat16)
-        mixed = jnp.dot(dscores, keys[...], preferred_element_type=jnp.float32)
-        result = jnp.where(mine, mixed, result)
-        add_keys = add_keys + dot_tn(dscores, own)
-        add_values = add_values + dot_tn(probs.astype(jnp.bfloat16), own_grad)
-    dquery[...] = (result * 0.125).astype(jnp.bfloat16)
-    key_sum[...] += add_keys
-    value_sum[...] += add_values
-
-    @pl.when(step == pl.num_programs(1) - 1)
-    def _():
-        dkeys[...] = (key_sum[...] * 0.125).astype(jnp.bfloat16)
-        dvalues[...] = value_sum[...].astype(jnp.bfloat16)
-
-
-def attend_back(qkv, grad, row_pos, col_pos, span):
-    length = qkv.shape[0]
-    wide = 2 * HD
-    whole = jax.ShapeDtypeStruct((length, SLOTS * HD), jnp.bfloat16)
-    return pl.pallas_call(
-        attend_back_kernel,
-        grid=(SLOTS // 2, length // span),
-        in_specs=[
-            pl.BlockSpec((span, wide), lambda h, i: (i, h)),
-            pl.BlockSpec((length, wide), lambda h, i: (0, SLOTS // 2 + h)),
-            pl.BlockSpec((length, wide), lambda h, i: (0, SLOTS + h)),
-            pl.BlockSpec((span, wide), lambda h, i: (i, h)),
-            pl.BlockSpec((span, 1), lambda h, i: (i, 0)),
-            pl.BlockSpec((1, length), lambda h, i: (0, 0)),
-        ],
-        out_specs=[
-            pl.BlockSpec((span, wide), lambda h, i: (i, h)),
-            pl.BlockSpec((length, wide), lambda h, i: (0, h)),
-            pl.BlockSpec((length, wide), lambda h, i: (0, h)),
-        ],
-        out_shape=[whole, whole, whole],
-        scratch_shapes=[
-            pltpu.VMEM((length, wide), jnp.float32),
-            pltpu.VMEM((length, wide), jnp.float32),
-        ],
-        compiler_params=pltpu.CompilerParams(vmem_limit_bytes=VMEM_BYTES),
-        name="attend_back",
-    )(qkv, qkv, qkv, grad, row_pos, col_pos)
-
-
 def own_heads(member):
     return (head_start(member + 1) - head_start(member)) * HD
 
 
 def all_heads(pieces):
     return jnp.concatenate([pieces[m][:, : own_heads(m)] for m in range(MEMBERS)], 1)
-
-
-def to_group(value):
-    pairs = []
-    for f in range(GROUPS):
-        for c in range(MEMBERS):
-            core, near, x = c // 4, c // 2 % 2, c % 2
-            y, far = f // 2, f % 2
-            pairs.append((f * MEMBERS + c, (2 * x + core) * MEMBERS + 4 * far + 2 * near + y))
-    return lax.ppermute(value, ("fsdp", "ctx"), pairs)
 
 
 def per_device_groups(
@@ -1438,89 +1759,21 @@
     vec_rows, vec_cols = vectors.shape
     padded = jnp.pad(vectors, ((0, 16 - vec_rows), (0, -vec_cols % 128)))
     (
-        x_all, back_all, vec, row_pos, col_pos, own_qkv, h_first, qkv, attn_all,
+        x_all, back_all, vecs, row_pos, col_pos, own_qkv, h_first, qkv, attn_all, attn,
         own_fc, own_proj, full_out,
     ) = forward(
         inputs.reshape(rows, width), cotangent.reshape(rows, width), order, padded, weights
     )
-    x_all, back_all = x_all.reshape(length, width), back_all.reshape(length, width)
-    own_fc = own_fc.reshape(width, hidden)
-    own_proj = own_proj.reshape(hidden, width)
-    full_out = full_out.reshape(width, width)
-    attn_all = all_heads(jnp.concatenate([attn_all[0], attn_all[1]], 2))
-    vec = vec.reshape(GROUPS, -1, width)[:, :vec_rows].reshape(-1, width)
-    head_at = HEADS * member // MEMBERS * HD
-    bias_fc = lax.dynamic_slice(vec[8:].reshape(-1), (member * hidden,), (hidden,))
-    mine = member * rows
-    span = min(length, 256)
-    resid = x_all.astype(high) + jnp.dot(attn_all, full_out, preferred_element_type=high) + vec[4]
-    h_second = layer_norm(resid, vec[5], vec[6]).astype(kind)
-    pre = jnp.dot(h_second, own_fc, preferred_element_type=high) + bias_fc
-    act, pull_gelu = jax.vjp(gelu_tanh, pre)
-    act = act.astype(kind)
-    made = group_scatter(jnp.dot(act, own_proj, preferred_element_type=high).astype(kind), 4)
-    resid_own = lax.dynamic_slice_in_dim(resid, mine, rows, 0)
-    outputs = (resid_own + made + vec[7]).astype(kind)
-
-    back_own = lax.dynamic_slice_in_dim(back_all, mine, rows, 0).astype(high)
-    grad_proj = jnp.einsum("tf,td->fd", act, back_all, preferred_element_type=high).astype(kind)
-    grad_bp = jnp.sum(back_own, 0)
-    dact = jnp.einsum("td,fd->tf", back_all, own_proj, preferred_element_type=high)
-    dpre = pull_gelu(dact)[0].astype(kind)
-    grad_fc = jnp.einsum("td,tf->df", h_second, dpre, preferred_element_type=high).astype(kind)
-    grad_bf = jnp.sum(dpre, 0, dtype=high)
-    dh_second = group_scatter(
-        jnp.einsum("tf,df->td", dpre, own_fc, preferred_element_type=high).astype(kind), 4
-    )
-    _, pull_second = jax.vjp(layer_norm, resid_own, vec[5], vec[6])
-    dres_ln, grad_g2, grad_b2 = pull_second(dh_second)
-    dresid = back_own + dres_ln
-    dbranch = dresid.astype(kind)
-    grad_bo = jnp.sum(dbranch, 0, dtype=high)
-    dbranch_all = group_gather(dbranch, 5).reshape(length, width)
-    out_heads = lax.dynamic_slice_in_dim(full_out, head_at, per_part, 0)
-    dattn = jnp.einsum("te,de->td", dbranch_all, out_heads, preferred_element_type=high)
-    dattn = dattn.astype(kind)
-    attn_cols = lax.dynamic_slice_in_dim(attn_all, member * four, four, 1)
-    grad_out = jnp.einsum("td,te->de", attn_cols, dbranch_all, preferred_element_type=high)
-    dqkv = jnp.concatenate(attend_back(qkv, dattn, row_pos, col_pos, span), 1)
-    lane = jnp.arange(per_part)
-    keep = lane < jnp.where(member == MEMBERS - 1, per_part, (SLOTS - 1) * HD)
-    dqkv = jnp.where(jnp.tile(keep, 3), dqkv, jnp.zeros_like(dqkv))
-    grad_qkv = jnp.einsum("td,te->de", h_first, dqkv, preferred_element_type=high).astype(kind)
-    bias_sums = jnp.sum(dqkv, 0, dtype=high)
-    dh_first = group_scatter(
-        jnp.einsum("te,de->td", dqkv, own_qkv, preferred_element_type=high).astype(kind), 4
-    )
-    x_own = lax.dynamic_slice_in_dim(x_all, mine, rows, 0).astype(high)
-    _, pull_first = jax.vjp(layer_norm, x_own, vec[0], vec[1])
-    dx_ln, grad_g1, grad_b1 = pull_first(dh_first)
-    input_grad = (dresid + dx_ln).astype(kind)
-    results = to_group(jnp.concatenate([outputs, input_grad], 1))
-    outputs = results[:, :width].reshape(seqs, rows, width)
-    input_grad = results[:, width:].reshape(seqs, rows, width)
-
-    zero_row = jnp.zeros((width,), high)
-    row_q = lax.dynamic_update_slice(zero_row, bias_sums[:per_part], (head_at,))
-    row_v = lax.dynamic_update_slice(zero_row, bias_sums[2 * per_part :], (head_at,))
-    row_f = lax.dynamic_update_slice(jnp.zeros((FF,), high), grad_bf, (member * hidden,))
-    grad_vec = jnp.concatenate(
-        [
-            jnp.stack([grad_g1, grad_b1, row_q, row_v, grad_bo, grad_g2, grad_b2, grad_bp]),
-            row_f.reshape(-1, width),
-        ],
-        0,
-    )
-    grad_vec = grad_vec.reshape(GROUPS, vec_rows, MEMBERS, vec_cols).transpose(0, 2, 1, 3)
-    grad_vec = grad_vec.reshape(DEVICES, vec_rows, vec_cols)
-    grad_vec = jnp.pad(grad_vec, ((0, 0), (0, 8 - vec_rows), (0, -vec_cols % 128)))
-    qkv_back, fc_back, rows_back, vec_back = yield_grads(
-        grad_qkv.reshape(2, 2, 2, four, 3 * per_part),
-        grad_fc.reshape(2, 2, 2, four, hidden),
-        grad_proj.reshape(2, 2, four, width),
-        grad_out.astype(kind),
-        grad_vec,
-    )
+    grad_fc, grad_proj, made, resid_own, dresid, dbranch, sums, grad_bf = middle(
+        x_all.reshape(length, width), attn_all, back_all.reshape(length, width), vecs,
+        full_out, own_fc, own_proj,
+    )
+    outputs, input_grad, qkv_back, fc_back, rows_back, vec_back = backward(
+        dbranch, made, grad_fc, grad_proj, attn, qkv, row_pos, col_pos, full_out, own_qkv,
+        h_first, x_all, resid_own, dresid, vecs, sums, grad_bf,
+    )
+    outputs = outputs.reshape(seqs, rows, width)
+    input_grad = input_grad.reshape(seqs, rows, width)
     qkv_flat = jnp.concatenate(
         [all_heads(qkv_back[:, :, p * per_part : (p + 1) * per_part]) for p in range(3)], 1
     ).reshape(local, 128)

time: 708 us -> 543 us (0.77)
  the two profiles are of different devices: /device:TPU:20 before, /device:TPU:0 now
where the time goes in v3:
time: 543 us; the launch traced here: 538 us
  Pallas kernels  494 us (91%)
  local copies, waits for them, and re-layouts  30.5 us (6%)
  other arithmetic  12 us (2%)
    pallas_call x1, Pallas kernels, backward(): pl.pallas_call(backward_kernel, out_shape=[like(rows, width), like(rows,...  223 us
    pallas_call x1, Pallas kernels, forward(): pl.pallas_call(forward_kernel, out_shape=[like(MEMBERS, rows, width), lik...  219 us
    pallas_call x1, Pallas kernels, middle(): pl.pallas_call(middle_kernel, out_shape=[like(MEMBERS, four, hidden), lik...  53.1 us
    sub x2, other arithmetic, adamw(): weight - rate * (first_hat / (jnp.sqrt(second_hat) + epsilon_adam) + deca...  12 us

profile of v3, /device:TPU:0, one launch (start us, length us, event | category | flops | bytes accessed | tf_op | source)
XLA Modules:
  0.0 538.2 jit_solution(15500661924967343936)
XLA Ops:
  0.6 2.0 copy.21
  2.6 2.0 copy.22
  4.6 1.3 pad.8.order_in
  5.8 1.3 pad.9.vec_in
  7.1 218.5 %forward.1 = (bf16[8,128,1600]{2,1,0:T(8,128)(2,1)}, bf16[8,128,1600]{2,1,0:T(8,128)(2,1)}, f32[64,1600]{1,0:T(8,128)}, f32[1024,1]{1,0:T(8,128)}, f32[1,1024]{1...) custom-call(bf16[128,1600]{1,0:T(8,128)(2,1)} %bitcast.81, ...), custom_call_target="tpu_custom_call" | custom-call | tf_op jit(solution)/shard_map/forward/pallas_call | solution.py:933
  225.7 53.1 %middle.1 = (bf16[8,200,800]{2,1,0:T(8,128)(2,1)}, bf16[4,200,1600]{2,1,0:T(8,128)(2,1)}, bf16[8,128,1600]{2,1,0:T(8,128)(2,1)}, f32[128,1600]{1,0:T(8,128)}, f3...) custom-call(bf16[1024,1600]{1,0:T(8,128)(2,1)} %bitcast.78, ...), custom_call_target="tpu_custom_call" | custom-call | tf_op jit(solution)/shard_map/middle/pallas_call | solution.py:1215
  278.8 222.8 %backward.1 = (bf16[128,1600]{1,0:T(8,128)(2,1)}, bf16[128,1600]{1,0:T(8,128)(2,1)}, bf16[8,200,768]{2,1,0:T(8,128)(2,1)}, bf16[3,8,50,800]{3,2,1,0:T(8,128)(2,1...) custom-call(bf16[128,1600]{1,0:T(8,128)(2,1)} %get-tuple-element.42.dbranch, ...), custom_call_target="tpu_custom_call" | custom-call | tf_op jit(solution)/shard_map/backward/pallas_call | solution.py:1642
  501.6 2.5 slice_bitcast_fusion
  504.1 1.9 slice_bitcast_fusion.19
  506.0 3.2 concatenate.3
  509.2 3.6 reshape.60
  512.8 1.9 copy.23
  514.7 4.7 reshape.61
  519.5 4.0 reshape.62
  523.5 0.1 broadcast_in_dim.13
  523.6 0.1 broadcast_in_dim.14
  523.7 0.0 copy-start.2
  523.8 0.0 copy-start.3
  523.8 0.0 copy-start.4
  523.8 0.0 copy-start.5
  523.8 11.4 %convert_subtract_fusion = (f32[7500,128]{1,0:T(8,128)}, f32[7500,128]{1,0:T(8,128)}, f32[7500,128]{1,0:T(8,128)}) fusion(bf16[7500,128]{1,0:T(8,128)(2,1)} %weights.1, f32[7500,128]{1,0:T(8,128)} %param.15, f32[7500,128]{1,0:T(8,128)} %param.14, bf16[7500,128]{1,0:T(8,128)(2,1)} %reshape.60, bf16[7500,128]{1,0:T(8,128)(2,1)} %reshape.61, ...), kind=kLoop, calls=%fused_computation.1 | loop fusion | flops 18240000 | bytes 26887500 | tf_op jit(solution)/shard_map/sub | solution.py:99
  535.2 1.0 copy.24
  536.1 1.0 copy.25
  537.1 0.6 convert_subtract_fusion.1
  (9 shorter events, 0.0 us)
Async XLA Ops:
  523.7 11.4 %copy-start.1 = (bf16[128,1600]{1,0:T(8,128)(2,1)S(1)}, bf16[128,1600]{1,0:T(8,128)(2,1)}, u32[]{:S(2)}) copy-start(bf16[128,1600]{1,0:T(8,128)(2,1)} %get-tuple-element.56) | copy-start | bytes 1228804
  523.7 12.4 %copy-start = (bf16[128,1600]{1,0:T(8,128)(2,1)S(1)}, bf16[128,1600]{1,0:T(8,128)(2,1)}, u32[]{:S(2)}) copy-start(bf16[128,1600]{1,0:T(8,128)(2,1)} %get-tuple-element.57) | copy-start | bytes 1228804
  523.7 13.3 %copy-start.2 = (bf16[3,200]{1,0:T(4,128)(2,1)S(1)}, bf16[3,200]{1,0:T(4,128)(2,1)}, u32[]{:S(2)}) copy-start(bf16[3,200]{1,0:T(4,128)(2,1)} %param.13) | copy-start | bytes 3604
  523.8 13.3 %copy-start.3 = (f32[3,200]{1,0:T(4,128)S(1)}, f32[3,200]{1,0:T(4,128)}, u32[]{:S(2)}) copy-start(f32[3,200]{1,0:T(4,128)} %param.17) | copy-start | bytes 7204
  523.8 13.3 %copy-start.4 = (f32[3,200]{1,0:T(4,128)S(1)}, f32[3,200]{1,0:T(4,128)}, u32[]{:S(2)}) copy-start(f32[3,200]{1,0:T(4,128)} %param.16) | copy-start | bytes 7204
  523.8 13.3 %copy-start.5 = (f32[8,256]{1,0:T(8,128)S(1)}, f32[8,256]{1,0:T(8,128)}, u32[]{:S(2)}) copy-start(f32[8,256]{1,0:T(8,128)} %get-tuple-element.61) | copy-start | bytes 24580

commit v4 on v3

--- a/solution.py
+++ b/solution.py
@@ -482,6 +482,58 @@
     return lookup(FC_SLOT, unit), lookup(FC_Y, unit)
 
 
+PROJ_OF_CTX = (
+    (8, 9, 10, 20),
+    (11, 12, 13, 0),
+    (14, 15, 16, 2),
+    (17, 18, 19, 5),
+    (21, 22, 3, 4),
+    (1, 23, 24, 25),
+    (26, 27, 28, 6),
+    (7, 29, 30, 31),
+)
+
+
+def hidden_of(member):
+    core, near, x = member // 4, member // 2 % 2, member % 2
+    return [
+        PROJ_OF_CTX[4 * far + 2 * near + y][2 * core + x] for y in range(2) for far in range(2)
+    ]
+
+
+HIDDEN = [hidden_of(_member) for _member in range(8)]
+HOLDER = {unit: (m, i) for m, units in enumerate(HIDDEN) for i, unit in enumerate(units)}
+PROJ_FSDP, PROJ_CTX = [0] * 32, [0] * 32
+PROJ_UNIT = [0] * 32
+for _ctx, _units in enumerate(PROJ_OF_CTX):
+    for _place, _unit in enumerate(_units):
+        _fsdp = 2 * (_place % 2) + _place // 2
+        PROJ_FSDP[_unit], PROJ_CTX[_unit] = _fsdp, _ctx
+        PROJ_UNIT[8 * _fsdp + _ctx] = _unit
+FC_POSITION = [0] * 32
+for _group, _units in enumerate(FC_OF_GROUP):
+    for _slot, _unit in enumerate(_units):
+        FC_POSITION[_unit] = 8 * _group + _slot
+
+
+def piece(tile_of, col, lane, size):
+    start = col % 128
+    value = tile_of(col // 128)
+    if start + size > 128:
+        lanes = lax.broadcasted_iota(jnp.int32, value.shape, 1)
+        value = jnp.where(lanes < start, tile_of(col // 128 + 1), value)
+    shift = (lane - start) % 128
+    return pltpu.roll(value, shift, 1) if shift else value
+
+
+def join(parts):
+    result = parts[0][1]
+    for lane, value in parts[1:]:
+        lanes = lax.broadcasted_iota(jnp.int32, value.shape, 1)
+        result = jnp.where(lanes < lane, result, value)
+    return result
+
+
 def out_root(member):
     return jnp.where(member // 3 == 1, 1, 0)
 
@@ -513,20 +565,24 @@
 def lay_fc(flat, first, pieces, part):
     count, hidden = pieces.shape[-2:]
     stride = FF // 128
+    block = hidden // GROUPS
+
+    def tile_of(tile):
+        return flat[pl.ds(first + tile, count, stride=stride), :]
+
     for member in range(MEMBERS):
-        start, shift = divmod(member * hidden, 128)
         for tile in range(-(-hidden // 128)):
-            value = flat[pl.ds(first + start + tile, count, stride=stride), :]
             size = min(128, hidden - 128 * tile)
-            if shift:
-                if shift + size > 128:
-                    after = flat[pl.ds(first + start + tile + 1, count, stride=stride), :]
-                    lane = lax.broadcasted_iota(jnp.int32, value.shape, 1)
-                    value = jnp.where(lane < shift, after, value)
-                value = pltpu.roll(value, 128 - shift, 1)
-            pieces[part, member, :, 128 * tile : 128 * tile + size] = value[:, :size].astype(
-                jnp.bfloat16
-            )
+            parts, at = [], 128 * tile
+            while at < 128 * tile + size:
+                which, inside = divmod(at, block)
+                length = min(block - inside, 128 * tile + size - at)
+                col = block * HIDDEN[member][which] + inside
+                parts.append((at - 128 * tile, piece(tile_of, col, at - 128 * tile, length)))
+                at += length
+            pieces[part, member, :, 128 * tile : 128 * tile + size] = join(parts)[
+                :, :size
+            ].astype(jnp.bfloat16)
 
 
 def lay_rows(flat, first, rows, blocks, part):
@@ -551,10 +607,83 @@
         )
 
 
+def wide(value):
+    return value.astype(jnp.float32)
+
+
+def low(value):
+    return value.astype(jnp.bfloat16)
+
+
+def half_of(blocks, core):
+    return blocks.at[pl.ds(4 * core, 4)]
+
+
+class Reduce:
+    def __init__(self, place, away, kept, from_core, two, got, last, done, sems):
+        self.p, self.away, self.kept, self.from_core = place, away, kept, from_core
+        self.two, self.got, self.last, self.done, self.sems = two, got, last, done, sems
+        self.route = Gather(place, None, None)
+        self.copies = []
+
+    def _go(self, source, landing, index, target):
+        item = remote(source, landing, self.sems, index, target)
+        item.start()
+        self.copies.append(item)
+        return item
+
+    def begin(self):
+        for j in (3, 2, 1, 0):
+            self._go(self.away.at[j], self.from_core.at[j], j, self.route.other)
+
+    def _summed(self, member):
+        block = member - 4 * self.p.core
+        return wide(self.kept[block]) + wide(self.from_core[block])
+
+    def second(self):
+        for item in self.copies[:4]:
+            item.wait_recv()
+        self.two[0] = low(self._summed(self.route.of_both))
+        self.across = self._go(self.two.at[0], self.got.at[0], 4, self.route.second)
+        self.two[1] = low(self._summed(self.route.of_second))
+        self.beyond = self._go(self.two.at[1], self.got.at[1], 5, self.route.second)
+
+    def third(self):
+        self.across.wait_recv()
+        self.last[...] = low(self._summed(self.route.of_first) + wide(self.got[0]))
+        self.final = self._go(self.last, self.done, 6, self.route.first)
+
+    def result(self):
+        self.beyond.wait_recv()
+        value = self._summed(self.p.me) + wide(self.got[1])
+        self.final.wait_recv()
+        return value + wide(self.done[...])
+
+    def sent(self):
+        for item in self.copies:
+            item.wait_send()
+
+
+def reduce_buffers(rows, width):
+    kind = jnp.bfloat16
+    return [
+        pltpu.VMEM((4, rows, width), kind),
+        pltpu.VMEM((2, rows, width), kind),
+        pltpu.VMEM((2, rows, width), kind),
+        pltpu.VMEM((rows, width), kind),
+        pltpu.VMEM((rows, width), kind),
+        pltpu.SemaphoreType.DMA((2, 7)),
+    ]
+
+
 def norm_rows(value, gain, shift):
     center = value - jnp.mean(value, -1, keepdims=True)
     spread = jnp.mean(center * center, -1, keepdims=True)
     return center * lax.rsqrt(spread + epsilon_norm) * gain + shift
+
+
+def head_rows(member):
+    return 8 * member
 
 
 def member_lanes(row, member, count):
@@ -579,12 +708,14 @@
 
 def forward_kernel(
     x_in, back_in, order_in, vec_in, weights,
-    x_all, back_all, vecs, row_pos, col_pos, w_qkv, h_first, qkv, attn_all, attn,
-    w_fc, w_proj, w_out,
+    back_all, vecs, row_pos, col_pos, w_qkv_out, h_first_out, qkv_out, attn, w_fc_out, w_proj_out,
+    w_heads, x_own, resid_own, h_second,
+    x_all, w_qkv, h_first, qkv, w_fc, w_proj,
     flat, rows, qkv_pieces, fc_pieces, blocks, order, vec_all, qkv_land,
-    fc, proj, out, fc_part, proj_part, out_part,
+    fc, proj, out, fc_part, proj_part, out_part, tail, next_tail, window, unit_rows, h_own,
+    branch, from_core, two, got, last, done, reduce_sem,
     move_sem, qkv_sem, fc_send, fc_recv, rows_sem, x_sem, back_sem, spread_sem,
-    own_sem, fc_sem, proj_sem, tree_sem, out_sem, attn_sem,
+    own_sem, fc_sem, proj_sem, tree_sem, h_sem, store_sem,
 ):
     p = Place()
     third_rows = weights.shape[0] // 3
@@ -663,6 +794,19 @@
     gather_x.second_hop()
     gather_x.third_hop()
     fc_moves, rows_moves = [], []
+    for part in range(3):
+        third = 3 * p.linear + part
+        valid = jnp.logical_and(third >= OUT_FIRST, third < FC_FIRST)
+        member = jnp.where(valid, third - OUT_FIRST, 0)
+        target = p.target(
+            x=member % 2, near=member // 2 % 2, core=member // 4, y=out_root(member), far=0
+        )
+        rows_moves.append(
+            Move(
+                p, blocks.at[part], out_part,
+                rows_sem.at[0, part], rows_sem.at[1, 1], target, valid,
+            )
+        )
     for part in range(3):
         third = 3 * p.linear + part
         valid = jnp.logical_and(third >= FC_FIRST, third < PROJ_FIRST)
@@ -679,25 +823,11 @@
         third = 3 * p.linear + part
         valid = third >= PROJ_FIRST
         unit = jnp.where(valid, third - PROJ_FIRST, 0)
-        member, group = unit // 4, unit % 4
-        target = p.target(
-            x=member % 2, near=member // 2 % 2, core=member // 4, y=group // 2, far=group % 2
-        )
+        target = (lookup(PROJ_FSDP, unit), lookup(PROJ_CTX, unit))
         rows_moves.append(
             Move(
                 p, blocks.at[part], proj_part,
                 rows_sem.at[0, part], rows_sem.at[1, 0], target, valid,
-            )
-        )
-        valid = jnp.logical_and(third >= OUT_FIRST, third < FC_FIRST)
-        member = jnp.where(valid, third - OUT_FIRST, 0)
-        target = p.target(
-            x=member % 2, near=member // 2 % 2, core=member // 4, y=out_root(member), far=0
-        )
-        rows_moves.append(
-            Move(
-                p, blocks.at[part], out_part,
-                rows_sem.at[0, part], rows_sem.at[1, 1], target, valid,
             )
         )
     gather_x.last_hop()
@@ -744,7 +874,31 @@
         return carry
 
     lax.fori_loop(0, MEMBERS, norm_block, 0)
+    x_own[...] = x_all[p.me]
+    stores = []
+
+    def store(source, target):
+        copy = pltpu.make_async_copy(source, target, store_sem.at[len(stores)])
+        copy.start()
+        stores.append(copy)
+
+    store(h_first, h_first_out)
     to_far, to_y = p.target(far=1 - p.far), p.target(y=1 - p.y)
+    same_y = p.y == out_root(p.me)
+    root = jnp.logical_and(same_y, p.far == 0)
+    beside = jnp.logical_and(same_y, p.far == 1)
+    out_far = remote(out_part, out, tree_sem, 0, to_far)
+    out_y = remote(out_part, out, tree_sem, 1, to_y)
+    out_later = remote(out, out, tree_sem, 2, to_y)
+    out_own = pltpu.make_async_copy(out_part, out, own_sem.at[8])
+
+    @pl.when(root)
+    def _():
+        arrived(out_part, rows_sem.at[1, 1])
+        out_far.start()
+        out_y.start()
+        out_own.start()
+
     fc_far, fc_y, fc_later, own_copies = [], [], [], []
     for slot in range(8):
         arrived(fc_part.at[slot], fc_recv.at[slot])
@@ -757,23 +911,6 @@
         own_copies[slot].start()
     gather_back.second_hop()
     gather_back.third_hop()
-    root_y = out_root(p.me)
-    same_y = p.y == root_y
-    root = jnp.logical_and(same_y, p.far == 0)
-    beside = jnp.logical_and(same_y, p.far == 1)
-    mine = out.at[p.me]
-    out_far = remote(out_part, mine, tree_sem, 0, to_far)
-    out_y = remote(out_part, mine, tree_sem, 1, to_y)
-    out_later = remote(mine, mine, tree_sem, 2, to_y)
-    out_own = pltpu.make_async_copy(out_part, mine, own_sem.at[8])
-
-    @pl.when(root)
-    def _():
-        arrived(out_part, rows_sem.at[1, 1])
-        out_far.start()
-        out_y.start()
-        out_own.start()
-
     arrived(proj_part, rows_sem.at[1, 0])
     my_proj, far_proj = proj.at[p.y, p.far], proj.at[p.y, 1 - p.far]
     proj_far = remote(proj_part, my_proj, proj_sem, 0, to_far)
@@ -790,6 +927,7 @@
             for y in range(2):
                 first = four * (4 * far + 2 * near + y)
                 w_qkv[first : first + four, :] = qkv_land[far, near, y]
+    store(w_qkv, w_qkv_out)
     per_part = SLOTS * HD
     bias = jnp.concatenate(
         [
@@ -807,6 +945,7 @@
         return carry
 
     lax.fori_loop(0, MEMBERS // 2, qkv_block, 0)
+    store(qkv, qkv_out)
     gather_back.last_hop()
     span = 2 * count
 
@@ -824,82 +963,102 @@
 
         lax.fori_loop(0, length // span, one_block, 0)
 
-    def share(pair):
-        item = Gather(p, attn_all.at[pair], attn_sem.at[pair])
-        for name, index, target in (
-            ("a", 0, item.first), ("b", 1, item.second), ("c", 2, item.other),
-        ):
-            copy = remote(attn.at[pair], attn_all.at[pair, p.me], attn_sem.at[pair], index, target)
-            copy.start()
-            item.copies[name] = copy
-        copy = pltpu.make_async_copy(
-            attn.at[pair], attn_all.at[pair, p.me], own_sem.at[10 + pair]
-        )
-        copy.start()
-        own_copies.append(copy)
-        return item
-
     one_pair(0)
-    gathers = [share(0)]
+
+    @pl.when(beside)
+    def _():
+        out_far.wait_recv()
+        out_later.start()
+
     for slot in range(8):
         fc_far[slot].wait_recv()
         landing = fc.at[fc_unit(1 - p.far, p.y, slot)]
         copy = remote(landing, landing, fc_sem, 16 + slot, to_y)
         copy.start()
         fc_later.append(copy)
-
-    @pl.when(beside)
+    one_pair(1)
+
+    @pl.when(root)
     def _():
-        out_far.wait_recv()
-        out_later.start()
-
-    gathers[0].second_hop()
-    gathers[0].third_hop()
-    gathers[0].last_hop()
-    one_pair(1)
-    gathers.append(share(1))
+        out_own.wait()
+
+    @pl.when(jnp.logical_and(jnp.logical_not(same_y), p.far == 0))
+    def _():
+        out_y.wait_recv()
+
+    @pl.when(jnp.logical_and(jnp.logical_not(same_y), p.far == 1))
+    def _():
+        out_later.wait_recv()
+
+    reach = tail.shape[0]
+    tail[...] = out[four - reach :, :]
+    following, before = (p.me + 1) % MEMBERS, (p.me + MEMBERS - 1) % MEMBERS
+    to_next = p.target(
+        x=following % 2, near=following // 2 % 2, core=following // 4
+    )
+    send_tail = remote(tail, next_tail, tree_sem, 3, to_next)
+    send_tail.start()
+    begin = head_rows(p.me)
+    window[...] = jnp.zeros_like(window)
+    window[reach : reach + four, :] = wide(out[...])
+    span_rows = SLOTS * HD
+    unit_rows[...] = low(window[pl.ds(pl.multiple_of(reach - begin, 8), span_rows), :])
+
+    def one_branch(step, carry):
+        at = pl.ds(pl.multiple_of(step * span, span), span)
+        heads = jnp.concatenate([attn[pair, at, :] for pair in range(pairs)], 1)
+        value = low(jnp.dot(heads, unit_rows[...], preferred_element_type=jnp.float32))
+        branch[2 * step] = value[:count]
+        branch[2 * step + 1] = value[count:]
+        return carry
+
+    lax.fori_loop(0, length // span, one_branch, 0)
+    reduce = Reduce(
+        p, half_of(branch, 1 - p.core), half_of(branch, p.core), from_core, two, got, last, done,
+        reduce_sem,
+    )
+    reduce.begin()
     proj_far.wait_recv()
     proj_later = remote(far_proj, far_proj, proj_sem, 2, to_y)
     proj_later.start()
-    gathers[1].second_hop()
-    gathers[1].third_hop()
-    gathers[1].last_hop()
-
-    @pl.when(root)
-    def _():
-        out_own.wait()
-
-    @pl.when(jnp.logical_and(jnp.logical_not(same_y), p.far == 0))
-    def _():
-        out_y.wait_recv()
-
-    @pl.when(jnp.logical_and(jnp.logical_not(same_y), p.far == 1))
-    def _():
-        out_later.wait_recv()
-
-    gather_out = Gather(p, out, out_sem)
-    gather_out.begin()
-    gather_out.second_hop()
+    reduce.second()
+    reduce.third()
     for item in fc_y + fc_later:
         item.wait_recv()
-    for item in own_copies[:8]:
+    for item in own_copies:
         item.wait()
-    gather_out.third_hop()
+    value = wide(x_own[...]) + reduce.result() + vecs[17:18, :]
+    resid_own[...] = value
+    h_own[...] = low(norm_rows(value, vecs[18:19, :], vecs[32:33, :]))
+    gather_h = Gather(p, h_second, h_sem)
+    for name, index, target in (
+        ("a", 0, gather_h.first), ("b", 1, gather_h.second), ("c", 2, gather_h.other),
+    ):
+        copy = remote(h_own, h_second.at[p.me], h_sem, index, target)
+        copy.start()
+        gather_h.copies[name] = copy
+    store(h_own, h_second.at[p.me])
     unit = fc.shape[1]
     for block in range(DEVICES):
         w_fc[unit * block : unit * block + unit, :] = fc[block]
-    gather_out.last_hop()
+    store(w_fc, w_fc_out)
+    gather_h.second_hop()
+    gather_h.third_hop()
     proj_y.wait_recv()
     proj_later.wait_recv()
     proj_own.wait()
     for group in range(GROUPS):
         w_proj[four * group : four * group + four, :] = proj[group // 2, group % 2]
-    for item in gathers + [gather_out, gather_back]:
+    store(w_proj, w_proj_out)
+    gather_h.last_hop()
+    send_tail.wait_recv()
+    window[:reach, :] = wide(next_tail[...])
+    w_heads[...] = low(window[pl.ds(pl.multiple_of(reach - begin, 8), span_rows), :])
+    for item in (gather_h, gather_back):
         item.finish()
-    for block in range(MEMBERS):
-        w_out[four * block : four * block + four, :] = out[block]
-    for item in fc_far + fc_y + fc_later + [proj_far, proj_y, proj_later]:
+    for item in fc_far + fc_y + fc_later + [proj_far, proj_y, proj_later, send_tail]:
         item.wait_send()
+    reduce.sent()
 
     @pl.when(root)
     def _():
@@ -910,8 +1069,8 @@
     def _():
         out_later.wait_send()
 
-    for item in own_copies[8:]:
-        item.wait()
+    for copy in stores:
+        copy.wait()
     for item in [x_move, order_move, back_move] + qkv_moves + fc_moves + rows_moves:
         item.sent()
     arrived(vec_all.at[pl.ds(1, DEVICES - 1)], move_sem.at[0, 2])
@@ -934,22 +1093,30 @@
         forward_kernel,
         out_shape=[
             like(MEMBERS, rows, width),
-            like(MEMBERS, rows, width),
             like(GROUPS * vectors.shape[0], width, dtype=high),
             like(length, 1, dtype=high),
             like(1, length, dtype=high),
             like(width, cols),
             like(length, width),
             like(length, cols),
-            like(pairs, MEMBERS, length, 2 * HD),
             like(pairs, length, 2 * HD),
             like(width, hidden),
             like(hidden, width),
-            like(width, width),
+            like(SLOTS * HD, width),
+            like(rows, width),
+            like(rows, width, dtype=high),
+            like(MEMBERS, rows, width),
         ],
         in_specs=[any_space] * 4 + [vmem],
-        out_specs=[vmem, any_space] + [vmem] * 6 + [any_space] + [vmem] * 4,
+        out_specs=[any_space] + [vmem] * 3 + [any_space] * 3 + [vmem] + [any_space] * 2
+        + [vmem] * 3 + [any_space],
         scratch_shapes=[
+            pltpu.VMEM((MEMBERS, rows, width), kind),
+            pltpu.VMEM((width, cols), kind),
+            pltpu.VMEM((length, width), kind),
+            pltpu.VMEM((length, cols), kind),
+            pltpu.VMEM((width, hidden), kind),
+            pltpu.VMEM((hidden, width), kind),
             pltpu.VMEM(weights.shape, high),
             pltpu.VMEM((-(-width // 128), four, 128), high),
             pltpu.VMEM((MEMBERS, four, cols), kind),
@@ -960,10 +1127,19 @@
             pltpu.VMEM((2, 2, 2, four, cols), kind),
             pltpu.VMEM((DEVICES, unit, hidden), kind),
             pltpu.VMEM((2, 2, four, width), kind),
-            pltpu.VMEM((MEMBERS, four, width), kind),
+            pltpu.VMEM((four, width), kind),
             pltpu.VMEM((8, unit, hidden), kind),
             pltpu.VMEM((four, width), kind),
             pltpu.VMEM((four, width), kind),
+            pltpu.VMEM((64, width), kind),
+            pltpu.VMEM((64, width), kind),
+            pltpu.VMEM((64 + SLOTS * HD, width), high),
+            pltpu.VMEM((SLOTS * HD, width), kind),
+            pltpu.VMEM((rows, width), kind),
+            pltpu.VMEM((MEMBERS, rows, width), kind),
+        ]
+        + reduce_buffers(rows, width)
+        + [
             dma((2, 4)),
             dma((2, 8)),
             dma((3, 8)),
@@ -972,12 +1148,12 @@
             dma((2, 7)),
             dma((2, 7)),
             dma((2, 6)),
-            dma((12,)),
+            dma((9 + 1,)),
             dma((2, 24)),
             dma((2, 3)),
-            dma((2, 3)),
+            dma((2, 4)),
             dma((2, 7)),
-            dma((pairs, 2, 7)),
+            dma((6,)),
         ],
         compiler_params=pltpu.CompilerParams(
             collective_id=1, has_side_effects=True, vmem_limit_bytes=VMEM_BYTES
@@ -986,119 +1162,53 @@
     )(x, back, order, vectors, weights)
 
 
-def wide(value):
-    return value.astype(jnp.float32)
-
-
-def low(value):
-    return value.astype(jnp.bfloat16)
-
-
 GELU_SCALE = 0.7978845608028654
 GELU_CUBE = 0.044715
 
 
-class Reduce:
-    def __init__(self, place, part, from_core, two, got, last, done, sems):
-        self.p, self.part, self.from_core = place, part, from_core
-        self.two, self.got, self.last, self.done, self.sems = two, got, last, done, sems
-        self.route = Gather(place, None, None)
-        self.copies = []
-
-    def _go(self, source, landing, index, target):
-        item = remote(source, landing, self.sems, index, target)
-        item.start()
-        self.copies.append(item)
-        return item
-
-    def begin(self):
-        p = self.p
-        for j in (3, 2, 1, 0):
-            self._go(
-                self.part.at[4 * (1 - p.core) + j], self.from_core.at[j], j, self.route.other
-            )
-
-    def _summed(self, member):
-        block = member - 4 * self.p.core
-        return wide(self.part[member]) + wide(self.from_core[block])
-
-    def second(self):
-        for item in self.copies[:4]:
-            item.wait_recv()
-        self.two[0] = low(self._summed(self.route.of_both))
-        self.across = self._go(self.two.at[0], self.got.at[0], 4, self.route.second)
-        self.two[1] = low(self._summed(self.route.of_second))
-        self.beyond = self._go(self.two.at[1], self.got.at[1], 5, self.route.second)
-
-    def third(self):
-        self.across.wait_recv()
-        self.last[...] = low(self._summed(self.route.of_first) + wide(self.got[0]))
-        self.final = self._go(self.last, self.done, 6, self.route.first)
-
-    def result(self):
-        self.beyond.wait_recv()
-        value = self._summed(self.p.me) + wide(self.got[1])
-        self.final.wait_recv()
-        return value + wide(self.done[...])
-
-    def sent(self):
-        for item in self.copies:
-            item.wait_send()
-
-
-def reduce_buffers(rows, width):
-    kind = jnp.bfloat16
-    return [
-        pltpu.VMEM((4, rows, width), kind),
-        pltpu.VMEM((2, rows, width), kind),
-        pltpu.VMEM((2, rows, width), kind),
-        pltpu.VMEM((rows, width), kind),
-        pltpu.VMEM((rows, width), kind),
-        pltpu.SemaphoreType.DMA((2, 7)),
-    ]
-
-
-def store_rows(target, first, value, lanes=slice(None)):
+def store_rows(target, first, value, lanes=slice(None), at=None):
+    places = at
     size = target.shape[1]
     row = 0
     while row < value.shape[0]:
         block, at = divmod(first + row, size)
         count = min(size - at, value.shape[0] - row)
+        block = block if places is None else places[block]
         target[block, at : at + count, lanes] = low(value[row : row + count])
         row += count
 
 
 def middle_kernel(
-    x_all, attn_all, back_all, vecs, w_out_in, w_fc_in, w_proj_in,
-    grad_fc, grad_proj, made, resid_own, dresid, dbranch, sums, fc_sums,
-    h_second, attn, back, w_out, w_fc, w_proj, act, dpre, dh_part, made_part, g_fc, g_proj,
-    resid, from_core, two, got, last, done, reduce_sem, load_sem, store_sem,
+    h_in, back_all, vecs, resid_own, w_fc_in, w_proj_in,
+    grad_fc, grad_proj, made, dresid, dbranch, sums, fc_sums,
+    h_second, back, w_fc, w_proj, act, dpre, dh_part, made_part, g_fc, g_proj,
+    from_core, two, got, last, done, reduce_sem, load_sem, store_sem,
 ):
     p = Place()
     length, width = h_second.shape
     count = length // MEMBERS
     hidden = act.shape[1]
-    pairs = attn.shape[0]
     loads = []
     for index, (source, target) in enumerate(
         (
-            (attn_all, attn), (w_out_in, w_out), (x_all, h_second),
-            (w_fc_in, w_fc), (back_all, back), (w_proj_in, w_proj),
+            (h_in, h_second), (w_fc_in, w_fc), (back_all, back), (w_proj_in, w_proj),
         )
     ):
         copy = pltpu.make_async_copy(source, target, load_sem.at[index])
         copy.start()
         loads.append(copy)
-    reduce = Reduce(p, dh_part, from_core, two, got, last, done, reduce_sem)
+    reduce = Reduce(p, half_of(dh_part, 1 - p.core), half_of(dh_part, p.core), from_core, two, got, last, done, reduce_sem)
     route = reduce.route
     greet((route.first, route.second, route.other))
     bias_fc = jnp.zeros((1, hidden), jnp.float32)
+    block = hidden // GROUPS
     for member in range(MEMBERS):
-        row = (34, 48, 49, 50)[member // 2]
-        first = hidden * (member % 2)
-        bias_fc = bias_fc + jnp.where(
-            p.me == member, vecs[row : row + 1, first : first + hidden], 0.0
-        )
+        parts = []
+        for unit in HIDDEN[member]:
+            row, first = divmod(block * unit, width)
+            row = (34, 48, 49, 50)[row]
+            parts.append(vecs[row : row + 1, first : first + block])
+        bias_fc = bias_fc + jnp.where(p.me == member, jnp.concatenate(parts, 1), 0.0)
     fc_sums[...] = jnp.zeros_like(fc_sums)
     for copy in loads:
         copy.wait()
@@ -1106,25 +1216,7 @@
 
     def one_block(step, carry):
         at = pl.ds(pl.multiple_of(step * span, span), span)
-        total = wide(h_second[at, :]) + vecs[17:18, :]
-        for member in range(MEMBERS):
-            first = head_start(member) * HD
-            used = (head_start(member + 1) - head_start(member)) * HD
-            heads = jnp.concatenate([attn[pair, member, at, :] for pair in range(pairs)], 1)
-            if used < SLOTS * HD:
-                lane = lax.broadcasted_iota(jnp.int32, heads.shape, 1)
-                heads = jnp.where(lane < used, heads, jnp.zeros_like(heads))
-            total = total + jnp.dot(
-                heads, w_out[first : first + SLOTS * HD, :], preferred_element_type=jnp.float32
-            )
-        resid[...] = total
-
-        @pl.when(step == p.me // 2)
-        def _():
-            resid_own[...] = resid[pl.ds(pl.multiple_of(p.me % 2 * count, count), count), :]
-
-        normed = low(norm_rows(total, vecs[18:19, :], vecs[32:33, :]))
-        h_second[at, :] = normed
+        normed = h_second[at, :]
         pre = jnp.dot(normed, w_fc[...], preferred_element_type=jnp.float32) + bias_fc
         square = pre * pre
         slope = jnp.tanh(GELU_SCALE * (pre + GELU_CUBE * pre * square))
@@ -1159,7 +1251,9 @@
     stores[0].start()
     for first in range(0, width, chunk):
         size = min(chunk, width - first)
-        store_rows(g_fc, first, dot_tn(h_second[:, first : first + size], dpre[...]))
+        store_rows(
+            g_fc, first, dot_tn(h_second[:, first : first + size], dpre[...]), at=FC_POSITION
+        )
         if first + size == 4 * chunk:
             reduce.third()
     stores.append(pltpu.make_async_copy(g_fc, grad_fc, store_sem.at[1]))
@@ -1196,9 +1290,9 @@
         copy.wait()
 
 
-def middle(x_all, attn_all, back_all, vecs, w_out, w_fc, w_proj):
+def middle(h_second, back_all, vecs, resid_own, w_fc, w_proj):
     kind, high = jnp.bfloat16, jnp.float32
-    length, width = x_all.shape
+    length, width = h_second.shape
     rows = length // MEMBERS
     hidden = w_proj.shape[0]
     four = width // MEMBERS
@@ -1215,39 +1309,35 @@
     return pl.pallas_call(
         middle_kernel,
         out_shape=[
-            like(MEMBERS, four, hidden),
+            like(DEVICES, four // 4, hidden),
             like(GROUPS, four, width),
             like(MEMBERS, rows, width),
-            like(rows, width, dtype=high),
             like(rows, width, dtype=high),
             like(rows, width),
             like(8, width, dtype=high),
             like(1, hidden, dtype=high),
         ],
-        in_specs=[any_space] * 3 + [vmem] + [any_space] * 3,
-        out_specs=[any_space] * 3 + [vmem] * 5,
+        in_specs=[any_space] * 2 + [vmem] * 2 + [any_space] * 2,
+        out_specs=[any_space] * 3 + [vmem] * 4,
         scratch_shapes=[
-            buffer(*x_all.shape),
-            buffer(*attn_all.shape),
+            buffer(*h_second.shape),
             buffer(*back_all.shape),
-            buffer(*w_out.shape),
             buffer(*w_fc.shape),
             buffer(*w_proj.shape),
             buffer(length, hidden),
             buffer(length, hidden),
             buffer(MEMBERS, rows, width),
             buffer(MEMBERS, rows, width),
-            buffer(MEMBERS, four, hidden),
+            buffer(DEVICES, four // 4, hidden),
             buffer(GROUPS, four, width),
-            buffer(2 * rows, width, dtype=high),
         ]
         + reduce_buffers(rows, width)
-        + [dma((6,)), dma((3,))],
+        + [dma((4,)), dma((3,))],
         compiler_params=pltpu.CompilerParams(
             collective_id=3, has_side_effects=True, vmem_limit_bytes=VMEM_BYTES
         ),
         name="middle",
-    )(x_all, attn_all, back_all, vecs, w_out, w_fc, w_proj)
+    )(h_second, back_all, vecs, resid_own, w_fc, w_proj)
 
 
 class Fold:
@@ -1292,10 +1382,10 @@
 
 
 def backward_kernel(
-    dbranch, made_in, grad_fc, grad_proj, attn, qkv, row_pos, col_pos, w_out, w_qkv_in,
-    h_in, x_all, resid_own, dresid, vecs, sums, fc_sums,
+    dbranch, made_in, grad_fc, grad_proj, attn, qkv, row_pos, col_pos, w_heads, w_qkv_in,
+    h_in, x_own, resid_own, dresid, vecs, sums, fc_sums,
     out_home, grad_home, qkv_back, fc_back, rows_back, vec_back,
-    branch_all, dattn, dqkv, key_sum, value_sum, w_heads, w_qkv, h_first, x_own, made, dh_part,
+    branch_all, dattn, dqkv, key_sum, value_sum, w_qkv, h_first, made, dh_part,
     fc_own, proj_own, g_qkv, g_heads, g_out, result, input_grad, vec_rows, vec_go, vec_got,
     fc_y, proj_y, qkv_y, out_y, fc_go, proj_go, qkv_go, out_go,
     fc_far, proj_far, qkv_far, out_far, fc_sum, proj_sum, qkv_sum, out_sum,
@@ -1306,10 +1396,9 @@
     p = Place()
     count, width = dbranch.shape
     length = MEMBERS * count
-    four, unit = grad_proj.shape[1], fc_back.shape[2]
+    four = grad_proj.shape[1]
     pairs = SLOTS // 2
     per_part = SLOTS * HD
-    first_head = HEADS * p.me // MEMBERS * HD
     loads = []
 
     def load(source, target):
@@ -1317,13 +1406,11 @@
         copy.start()
         loads.append(copy)
 
-    load(w_out.at[pl.ds(pl.multiple_of(first_head, HD), per_part)], w_heads)
-    load(x_all.at[p.me], x_own)
     for far in range(2):
         load(grad_proj.at[2 * p.y + far], proj_own.at[far])
         for near in range(2):
-            load(grad_fc.at[4 * far + 2 * near + p.y], fc_own.at[far, near])
-    load(made_in, made)
+            load(grad_fc.at[far, p.y, near], fc_own.at[far, near])
+    load(half_of(made_in, p.core), made)
     load(w_qkv_in, w_qkv)
     load(h_in, h_first)
     greet_all(p)
@@ -1341,7 +1428,7 @@
     )
     fc_folds = [
         Fold(
-            p, lambda far, near=near: grad_fc.at[4 * far + 2 * near + 1 - p.y],
+            p, lambda far, near=near: grad_fc.at[far, 1 - p.y, near],
             lambda far, near=near: fc_own.at[far, near],
             lambda far, near=near: fc_y.at[far, near],
             fc_go.at[near], fc_far.at[near], fold_sem, 3 + 3 * near,
@@ -1378,7 +1465,9 @@
         return carry
 
     lax.fori_loop(0, length // span, one_dattn, 0)
-    reduce_made = Reduce(p, made, core_a, two_a, got_a, last_a, done_a, sem_a)
+    reduce_made = Reduce(
+        p, half_of(made_in, 1 - p.core), made, core_a, two_a, got_a, last_a, done_a, sem_a
+    )
     reduce_made.begin()
     proj_fold.rest()
 
@@ -1439,7 +1528,10 @@
         return carry
 
     lax.fori_loop(0, length // span, one_part, 0)
-    reduce_dh = Reduce(p, dh_part, core_b, two_b, got_b, last_b, done_b, sem_b)
+    reduce_dh = Reduce(
+        p, half_of(dh_part, 1 - p.core), half_of(dh_part, p.core), core_b, two_b, got_b, last_b,
+        done_b, sem_b,
+    )
     reduce_dh.begin()
     chunk = 256
     for first in range(0, width, chunk):
@@ -1450,13 +1542,18 @@
     for item in qkv_folds:
         item.rest()
     reduce_dh.second()
+    proj_sum[...] = proj_fold.end()
+    target, part = shard_of(PROJ_FIRST + lookup(PROJ_UNIT, p.linear))
+    moves = [
+        Move(p, proj_sum, rows_back.at[part], rows_send.at[0], rows_recv.at[part], target)
+    ]
     for pair in range(pairs):
         total = 0.0
         for block in range(MEMBERS):
             at = slice(block * count, block * count + count)
             total = total + dot_tn(attn[pair, at, :], branch_all[block])
         g_heads[128 * pair : 128 * pair + 128, :] = total
-    g_out[...] = low(g_heads[pl.ds(pl.multiple_of(four * p.me - first_head, 8), four), :])
+    g_out[...] = low(g_heads[pl.ds(pl.multiple_of(head_rows(p.me), 8), four), :])
     root_y = out_root(p.me)
     same_y = p.y == root_y
     root = jnp.logical_and(same_y, p.far == 0)
@@ -1473,7 +1570,18 @@
     home = p.target(
         x=p.ctx % 2, near=p.ctx // 2 % 2, core=p.ctx // 4, y=p.fsdp // 2, far=p.fsdp % 2
     )
-    moves = [Move(p, result, out_home, home_sem.at[0, 0], home_sem.at[1, 0], home)]
+    moves.append(Move(p, result, out_home, home_sem.at[0, 0], home_sem.at[1, 0], home))
+
+    for near in range(2):
+        fc_sum[near] = fc_folds[near].end()
+        for slot in range(4):
+            target, part = shard_of(FC_FIRST + fc_unit(p.far, p.y, 4 * near + slot))
+            moves.append(
+                Move(
+                    p, fc_sum.at[near, slot], fc_back.at[part, p.me],
+                    fc_send.at[near, slot], fc_recv.at[part, p.me], target,
+                )
+            )
 
     @pl.when(same_y)
     def _():
@@ -1517,10 +1625,6 @@
     vec_rows[4:5, :] = sums[2:3, :]
     vec_rows[5:7, :] = sums[0:2, :]
     vec_rows[7:8, :] = sums[3:4, :]
-    hidden = fc_sums.shape[1]
-    fc_row = placed(fc_sums[...], (0, hidden), p.me % 2)
-    for row in range(GROUPS):
-        vec_rows[8 + row : 9 + row, :] = jnp.where(p.me // 2 == row, fc_row, 0.0)
     used = width // MEMBERS
     vec_go[...] = jnp.zeros_like(vec_go)
     for f in range(GROUPS):
@@ -1528,6 +1632,12 @@
             vec_go[MEMBERS * f + c, 0:3, 0:used] = vec_rows[
                 3 * f : 3 * f + 3, used * c : used * c + used
             ]
+    for unit, (holder, which) in HOLDER.items():
+        f, row = divmod(8 + unit // MEMBERS, 3)
+        value = fc_sums[:, used * which : used * which + used]
+        vec_go[MEMBERS * f + unit % MEMBERS, row : row + 1, 0:used] = jnp.where(
+            p.me == holder, value, 0.0
+        )
 
     def vec_send(step, carry):
         other = (p.linear + step) % DEVICES
@@ -1545,24 +1655,6 @@
     pltpu.make_async_copy(vec_go.at[p.linear], vec_got.at[p.linear], vec_sem.at[1]).start()
     for item in qkv_folds:
         item.middle()
-    proj_sum[...] = proj_fold.end()
-    target, part = shard_of(PROJ_FIRST + 4 * p.me + p.group)
-    moves.append(
-        Move(p, proj_sum, rows_back.at[part], rows_send.at[0], rows_recv.at[part], target)
-    )
-    for near in range(2):
-        block = fc_folds[near].end()
-        for slot in range(4):
-            fc_sum[near, slot] = block[slot * unit : (slot + 1) * unit]
-            third = FC_FIRST + 4 * (4 * p.far + 2 * near + p.y) + slot
-            target, part = shard_of(third)
-            moves.append(
-                Move(
-                    p, fc_sum.at[near, slot], fc_back.at[part, p.me],
-                    fc_send.at[near, slot], fc_recv.at[part, p.me], target,
-                )
-            )
-
     @pl.when(root)
     def _():
         over_far.wait_recv()
@@ -1619,8 +1711,8 @@
 
 
 def backward(
-    dbranch, made, grad_fc, grad_proj, attn, qkv, row_pos, col_pos, w_out, w_qkv,
-    h_first, x_all, resid_own, dresid, vecs, sums, fc_sums,
+    dbranch, made, grad_fc, grad_proj, attn, qkv, row_pos, col_pos, w_heads, w_qkv,
+    h_first, x_own, resid_own, dresid, vecs, sums, fc_sums,
 ):
     kind, high = jnp.bfloat16, jnp.float32
     rows, width = dbranch.shape
@@ -1649,7 +1741,7 @@
             like(3, four, width),
             like(8, used, dtype=high),
         ],
-        in_specs=[vmem] + [any_space] * 3 + [vmem] * 4 + [any_space] * 4 + [vmem] * 5,
+        in_specs=[vmem] + [any_space] * 3 + [vmem] * 5 + [any_space] * 2 + [vmem] * 6,
         out_specs=[any_space] * 5 + [vmem],
         scratch_shapes=[
             buffer(MEMBERS, rows, width),
@@ -1657,13 +1749,11 @@
             buffer(length, cols),
             buffer(length, 2 * HD, dtype=high),
             buffer(length, 2 * HD, dtype=high),
-            buffer(per_part, width),
             buffer(*w_qkv.shape),
             buffer(*h_first.shape),
-            buffer(rows, width),
+            buffer(MEMBERS // 2, rows, width),
             buffer(MEMBERS, rows, width),
-            buffer(MEMBERS, rows, width),
-            buffer(2, 2, four, hidden),
+            buffer(2, 2, 4, unit, hidden),
             buffer(2, four, width),
             buffer(MEMBERS, four, cols),
             buffer(per_part, width, dtype=high),
@@ -1675,11 +1765,11 @@
             buffer(DEVICES, 8, used, dtype=high),
         ]
         + [
-            buffer(2, 2, four, hidden), buffer(2, four, width), buffer(2, 2, four, cols),
+            buffer(2, 2, 4, unit, hidden), buffer(2, four, width), buffer(2, 2, four, cols),
             buffer(four, width),
         ]
         + [
-            buffer(2, four, hidden), buffer(four, width), buffer(2, four, cols),
+            buffer(2, 4, unit, hidden), buffer(four, width), buffer(2, four, cols),
             buffer(four, width),
         ]
         * 2
@@ -1708,8 +1798,8 @@
         ),
         name="backward",
     )(
-        dbranch, made, grad_fc, grad_proj, attn, qkv, row_pos, col_pos, w_out, w_qkv,
-        h_first, x_all, resid_own, dresid, vecs, sums, fc_sums,
+        dbranch, made, grad_fc, grad_proj, attn, qkv, row_pos, col_pos, w_heads, w_qkv,
+        h_first, x_own, resid_own, dresid, vecs, sums, fc_sums,
     )
 
 
@@ -1732,58 +1822,180 @@
     return weights / jnp.sum(weights, -1, keepdims=True)
 
 
-def own_heads(member):
-    return (head_start(member + 1) - head_start(member)) * HD
-
-
-def all_heads(pieces):
-    return jnp.concatenate([pieces[m][:, : own_heads(m)] for m in range(MEMBERS)], 1)
+def head_place(head):
+    member = max(m for m in range(MEMBERS) if head_start(m) <= head)
+    return member, head - head_start(member)
+
+
+def unlay_qkv(flat, tiles, back):
+    count = back.shape[1] // 2
+    for member in range(MEMBERS):
+        for tile in range(back.shape[2] // 128):
+            tiles[member * (back.shape[2] // 128) + tile] = wide(
+                back[member, :, 128 * tile : 128 * tile + 128]
+            )
+    halves = 3 * HEADS
+
+    def half(index, lane):
+        odd, at = divmod(index, halves)
+        part, head = divmod(at, HEADS)
+        member, slot = head_place(head)
+        col = 64 * (SLOTS * part + slot)
+        tile = member * (back.shape[2] // 128) + col // 128
+        return piece(
+            lambda _: tiles[tile, pl.ds(odd, count, stride=2), :], col % 128, lane, HD
+        )
+
+    for row in range(halves):
+        flat[pl.ds(row, count, stride=halves), :] = join(
+            [(0, half(2 * row, 0)), (HD, half(2 * row + 1, HD))]
+        )
+
+
+def unlay_fc(flat, first, tiles, back, part):
+    count, hidden = back.shape[-2:]
+    each = -(-hidden // 128)
+    for member in range(MEMBERS):
+        for tile in range(each):
+            size = min(128, hidden - 128 * tile)
+            tiles[member * each + tile, :count, :size] = wide(
+                back[part, member, :, 128 * tile : 128 * tile + size]
+            )
+    stride, block = FF // 128, hidden // GROUPS
+    for row in range(stride):
+        parts, col = [], 128 * row
+        while col < 128 * row + 128:
+            unit, inside = divmod(col, block)
+            size = min(block - inside, 128 * row + 128 - col)
+            member, which = HOLDER[unit]
+            lane = col - 128 * row
+            value = piece(
+                lambda t, m=member: tiles[m * each + t, :count, :],
+                block * which + inside, lane, size,
+            )
+            parts.append((lane, value))
+            col += size
+        flat[pl.ds(first + row, count, stride=stride), :] = join(parts)
+
+
+def unlay_rows(flat, first, tiles, back, part):
+    count, width = back.shape[1] // 2, back.shape[2]
+    for tile in range(-(-width // 128)):
+        size = min(128, width - 128 * tile)
+        tiles[tile, :, :size] = wide(back[part, :, 128 * tile : 128 * tile + size])
+    halves = width // HD
+
+    def half(index, lane):
+        odd, at = divmod(index, halves)
+        return piece(
+            lambda t: tiles[t, pl.ds(odd, count, stride=2), :], HD * at, lane, HD
+        )
+
+    for row in range(halves):
+        flat[pl.ds(first + row, count, stride=halves), :] = join(
+            [(0, half(2 * row, 0)), (HD, half(2 * row + 1, HD))]
+        )
+
+
+def update_kernel(
+    qkv_in, fc_in, rows_in, weights, first, second, moment, squares, new,
+    flat, tiles, qkv_back, fc_back, rows_back, sem,
+):
+    step = pl.program_id(0)
+    linear = lax.axis_index("fsdp") * MEMBERS + lax.axis_index("ctx")
+
+    @pl.when(step == 0)
+    def _():
+        @pl.when(linear < MEMBERS)
+        def _():
+            copy = pltpu.make_async_copy(qkv_in, qkv_back, sem.at[0])
+            copy.start()
+            copy.wait()
+            unlay_qkv(flat, tiles, qkv_back)
+
+        @pl.when(linear >= MEMBERS)
+        def _():
+            copies = [
+                pltpu.make_async_copy(fc_in, fc_back, sem.at[0]),
+                pltpu.make_async_copy(rows_in, rows_back, sem.at[1]),
+            ]
+            for copy in copies:
+                copy.start()
+            for copy in copies:
+                copy.wait()
+            third_rows = fc_back.shape[2] * FF // 128
+            for part in range(3):
+                third = 3 * linear + part
+                is_fc = jnp.logical_and(third >= FC_FIRST, third < PROJ_FIRST)
+
+                @pl.when(is_fc)
+                def _(part=part):
+                    unlay_fc(flat, part * third_rows, tiles, fc_back, part)
+
+                @pl.when(jnp.logical_not(is_fc))
+                def _(part=part):
+                    unlay_rows(flat, part * third_rows, tiles, rows_back, part)
+
+    size = weights.shape[0]
+    grad = flat[pl.ds(pl.multiple_of(step * size, 8), size), :]
+    result = adamw(weights[...], grad, first[...], second[...], rate_matrix, weight_decay)
+    moment[...], squares[...], new[...] = result
+
+
+def update(qkv_back, fc_back, rows_back, weights, first, second):
+    high = jnp.float32
+    local = weights.shape[0]
+    steps = 10
+    size = -(-local // (16 * steps)) * 16
+    block = pl.BlockSpec((size, 128), lambda i: (i, 0))
+    any_space = pl.BlockSpec(memory_space=pl.ANY)
+    kind = jax.ShapeDtypeStruct((local, 128), high)
+    tile_count = max(qkv_back.shape[0] * qkv_back.shape[2] // 128, MEMBERS * 7)
+    return pl.pallas_call(
+        update_kernel,
+        grid=(steps,),
+        in_specs=[any_space] * 3 + [block] * 3,
+        out_specs=[block] * 3,
+        out_shape=[kind] * 3,
+        scratch_shapes=[
+            pltpu.VMEM((size * steps, 128), high),
+            pltpu.VMEM((tile_count, qkv_back.shape[1], 128), high),
+            pltpu.VMEM(qkv_back.shape, qkv_back.dtype),
+            pltpu.VMEM(fc_back.shape, fc_back.dtype),
+            pltpu.VMEM(rows_back.shape, rows_back.dtype),
+            pltpu.SemaphoreType.DMA((2,)),
+        ],
+        compiler_params=pltpu.CompilerParams(vmem_limit_bytes=VMEM_BYTES),
+        name="update",
+    )(qkv_back, fc_back, rows_back, weights, first, second)
 
 
 def per_device_groups(
     inputs, cotangent, slot_order, weights, vectors, first_w, second_w, first_vec, second_vec
 ):
     seqs, rows, width = inputs.shape
-    kind, high = jnp.bfloat16, jnp.float32
-    fsdp, ctx = lax.axis_index("fsdp"), lax.axis_index("ctx")
-    member = 4 * (fsdp % 2) + 2 * (ctx // 2 % 2) + fsdp // 2
     length = rows * MEMBERS
-    hidden = FF // MEMBERS
-    local = weights.shape[0]
-    third = local // 3
-    unit = width // DEVICES
-    four = 4 * unit
-    per_part = SLOTS * HD
-
     order = jnp.pad(slot_order, ((0, 127), (0, 128 - slot_order.shape[1])))
     vec_rows, vec_cols = vectors.shape
     padded = jnp.pad(vectors, ((0, 16 - vec_rows), (0, -vec_cols % 128)))
     (
-        x_all, back_all, vecs, row_pos, col_pos, own_qkv, h_first, qkv, attn_all, attn,
-        own_fc, own_proj, full_out,
+        back_all, vecs, row_pos, col_pos, own_qkv, h_first, qkv, attn, own_fc, own_proj, w_heads,
+        x_own, resid_own, h_second,
     ) = forward(
         inputs.reshape(rows, width), cotangent.reshape(rows, width), order, padded, weights
     )
-    grad_fc, grad_proj, made, resid_own, dresid, dbranch, sums, grad_bf = middle(
-        x_all.reshape(length, width), attn_all, back_all.reshape(length, width), vecs,
-        full_out, own_fc, own_proj,
+    grad_fc, grad_proj, made, dresid, dbranch, sums, fc_sums = middle(
+        h_second.reshape(length, width), back_all.reshape(length, width), vecs, resid_own,
+        own_fc, own_proj,
     )
     outputs, input_grad, qkv_back, fc_back, rows_back, vec_back = backward(
-        dbranch, made, grad_fc, grad_proj, attn, qkv, row_pos, col_pos, full_out, own_qkv,
-        h_first, x_all, resid_own, dresid, vecs, sums, grad_bf,
+        dbranch, made, grad_fc.reshape((2, 2, 2, 4) + grad_fc.shape[1:]), grad_proj, attn, qkv,
+        row_pos, col_pos, w_heads, own_qkv, h_first, x_own, resid_own, dresid, vecs, sums,
+        fc_sums,
     )
     outputs = outputs.reshape(seqs, rows, width)
     input_grad = input_grad.reshape(seqs, rows, width)
-    qkv_flat = jnp.concatenate(
-        [all_heads(qkv_back[:, :, p * per_part : (p + 1) * per_part]) for p in range(3)], 1
-    ).reshape(local, 128)
-    fc_flat = fc_back.transpose(0, 2, 1, 3).reshape(3, third, 128)
-    rows_flat = rows_back.reshape(3, third, 128)
-    thirds = 3 * (fsdp * MEMBERS + ctx) + jnp.arange(3)
-    is_fc = jnp.logical_and(thirds >= FC_FIRST, thirds < PROJ_FIRST)
-    others = jnp.where(is_fc[:, None, None], fc_flat, rows_flat).reshape(local, 128)
-    owned = jnp.where(fsdp == 0, qkv_flat, others).astype(high)
-    new_w = adamw(weights, owned, first_w, second_w, rate_matrix, weight_decay)
+    new_w = update(qkv_back, fc_back, rows_back, weights, first_w, second_w)
     owned_vec = vec_back[:vec_rows, :vec_cols]
     new_vec = adamw(vectors, owned_vec, first_vec, second_vec, rate_vector, 0.0)
     return (outputs, input_grad, new_w[0], new_w[1], new_w[2], new_vec[0], new_vec[1], new_vec[2])

time: 543 us -> 465 us (0.86)
  Pallas kernels: 494 us -> 447 us
  local copies, waits for them, and re-layouts: 30.5 us -> 10.4 us
  other arithmetic: 12 us -> 1.32 us
    pallas_call x1, Pallas kernels: 219 us -> 193 us  [forward(): pl.pallas_call(forward_kernel, out_shape=[like(MEMBERS, rows, width), lik...]
    pallas_call x1, Pallas kernels: 223 us -> 198 us  [backward(): pl.pallas_call(backward_kernel, out_shape=[like(rows, width), like(rows,...]
    reshape x3 -> x0, local copies, waits for them, and re-layouts: 12.4 us -> none  [the longest x1 4.74 us: per_device_groups(): fc_flat = fc_back.transpose(0, 2, 1, 3).reshape(3, third, 128)]
    sub x2 -> x1, other arithmetic: 12 us -> 1.32 us  [adamw(): weight - rate * (first_hat / (jnp.sqrt(second_hat) + epsilon_adam) + deca...]
    pallas_call x1 -> x2, Pallas kernels: 53.1 us -> 55.5 us  [the longest x1 39.5 us: middle(): pl.pallas_call(middle_kernel, out_shape=[like(DEVICES, four // 4, hidden)...]
where the time goes in v4:
time: 465 us; the launch traced here: 459 us
  Pallas kernels  447 us (96%)
  local copies, waits for them, and re-layouts  10.4 us (2%)
    pallas_call x1, Pallas kernels, backward(): pl.pallas_call(backward_kernel, out_shape=[like(rows, width), like(rows,...  198 us
    pallas_call x1, Pallas kernels, forward(): pl.pallas_call(forward_kernel, out_shape=[like(MEMBERS, rows, width), lik...  193 us
    pallas_call x1, Pallas kernels, middle(): pl.pallas_call(middle_kernel, out_shape=[like(DEVICES, four // 4, hidden)...  39.5 us
    pallas_call x1, Pallas kernels, update(): pl.pallas_call(update_kernel, grid=(steps,), in_specs=[any_space] * 3 + [...  16 us

profile of v4, /device:TPU:0, one launch (start us, length us, event | category | flops | bytes accessed | tf_op | source)
XLA Modules:
  0.0 459.5 jit_solution(12499661173927661108)
XLA Ops:
  0.6 1.3 pad.9.vec_in
  1.9 1.3 pad.8.order_in
  3.2 2.0 copy.17
  5.2 2.0 copy.18
  7.1 193.2 %forward.1 = (bf16[8,128,1600]{2,1,0:T(8,128)(2,1)}, f32[64,1600]{1,0:T(8,128)}, f32[1024,1]{1,0:T(8,128)}, f32[1,1024]{1,0:T(1,128)}, bf16[1600,768]{1,0:T(8,12...) custom-call(bf16[128,1600]{1,0:T(8,128)(2,1)} %bitcast.10, ...), custom_call_target="tpu_custom_call" | custom-call | tf_op jit(solution)/shard_map/forward/pallas_call | solution.py:1092
  200.3 39.5 %middle.1 = (bf16[32,50,800]{2,1,0:T(8,128)(2,1)}, bf16[4,200,1600]{2,1,0:T(8,128)(2,1)}, bf16[8,128,1600]{2,1,0:T(8,128)(2,1)}, f32[128,1600]{1,0:T(8,128)}, bf...) custom-call(bf16[1024,1600]{1,0:T(8,128)(2,1)} %bitcast.8, bf16[1024,1600]{1,0:T(8,128)(2,1)} %bitcast.7, ...), custom_call_target="tpu_custom_call" | custom-call | tf_op jit(solution)/shard_map/middle/pallas_call | solution.py:1309
  239.8 0.0 copy-start
  239.8 0.0 copy-start.1
  239.8 0.0 copy-start.2
  239.8 198.2 %backward.1 = (bf16[128,1600]{1,0:T(8,128)(2,1)}, bf16[128,1600]{1,0:T(8,128)(2,1)}, bf16[8,200,768]{2,1,0:T(8,128)(2,1)}, bf16[3,8,50,800]{3,2,1,0:T(8,128)(2,1...) custom-call(bf16[128,1600]{1,0:T(8,128)(2,1)} %get-tuple-element.44.dbranch, ...), custom_call_target="tpu_custom_call" | custom-call | tf_op jit(solution)/shard_map/backward/pallas_call | solution.py:1734
  438.0 1.9 copy.19
  440.0 1.9 copy.20
  441.9 0.0 copy-done
  441.9 0.0 copy-done.1
  441.9 0.0 copy-done.2
  441.9 1.3 convert_subtract_fusion
  443.2 16.0 %update.1 = (f32[7500,128]{1,0:T(8,128)}, f32[7500,128]{1,0:T(8,128)}, f32[7500,128]{1,0:T(8,128)}) custom-call(bf16[8,200,768]{2,1,0:T(8,128)(2,1)} %get-tuple-element.61.qkv_in, bf16[3,8,50,800]{3,2,1,0:T(8,128)(2,1)} %get-tuple-element.62.fc_in, bf16[3,200,1600]{2,1,0:T(8,128)(2,1)} %get-tuple-element.63.rows_in, bf16[7500,128]{1,0:T(8,128)(2,1)} %weights.3, ...), custom_call_target="tpu_custom_call" | custom-call | tf_op jit(solution)/shard_map/update/pallas_call | solution.py:1954
Async XLA Ops:
  239.8 202.1 %copy-start = (bf16[3,200]{1,0:T(4,128)(2,1)S(1)}, bf16[3,200]{1,0:T(4,128)(2,1)}, u32[]{:S(2)}) copy-start(bf16[3,200]{1,0:T(4,128)(2,1)} %param.13) | copy-start | bytes 3604
  239.8 202.1 %copy-start.1 = (f32[3,200]{1,0:T(4,128)S(1)}, f32[3,200]{1,0:T(4,128)}, u32[]{:S(2)}) copy-start(f32[3,200]{1,0:T(4,128)} %param.17) | copy-start | bytes 7204
  239.8 202.1 %copy-start.2 = (f32[3,200]{1,0:T(4,128)S(1)}, f32[3,200]{1,0:T(4,128)}, u32[]{:S(2)}) copy-start(f32[3,200]{1,0:T(4,128)} %param.16) | copy-start | bytes 7204

commit v5 on v4

--- a/solution.py
+++ b/solution.py
@@ -378,9 +378,9 @@
 
 
 class Gather:
-    def __init__(self, place, out, sems):
+    def __init__(self, place, out, sems, near_first=False):
         p = place
-        step, turn = 1 - p.core, p.core
+        step, turn = (0, 1) if near_first else (1 - p.core, p.core)
         x1, near1 = p.x + step * (1 - 2 * p.x), p.near + turn * (1 - 2 * p.near)
         x2, near2 = p.x + turn * (1 - 2 * p.x), p.near + step * (1 - 2 * p.near)
         self.out, self.sems, self.me = out, sems, p.me
@@ -483,13 +483,13 @@
 
 
 PROJ_OF_CTX = (
-    (8, 9, 10, 20),
-    (11, 12, 13, 0),
+    (8, 9, 10, 3),
+    (11, 12, 13, 6),
     (14, 15, 16, 2),
     (17, 18, 19, 5),
-    (21, 22, 3, 4),
+    (20, 21, 22, 0),
     (1, 23, 24, 25),
-    (26, 27, 28, 6),
+    (4, 26, 27, 28),
     (7, 29, 30, 31),
 )
 
@@ -548,18 +548,15 @@
     return pltpu.roll(jnp.where(lane < HD, after, tile), HD, 1)
 
 
-def lay_qkv(flat, rows, pieces, member):
+def lay_qkv(flat, rows, pieces, member, pair):
     count = rows.shape[1] // 2
     halves = 3 * HEADS
     for part in range(3):
         for odd in range(2):
-            for tile in range(SLOTS // 2):
-                half = halves * odd + HEADS * part + head_start(member) + 2 * tile
-                rows[SLOTS // 2 * part + tile, pl.ds(odd, count, stride=2), :] = half_tile(
-                    flat, 0, count, halves, half
-                )
-    for tile in range(3 * SLOTS // 2):
-        pieces[member, :, 128 * tile : 128 * tile + 128] = rows[tile].astype(jnp.bfloat16)
+            half = halves * odd + HEADS * part + head_start(member) + 2 * pair
+            rows[part, pl.ds(odd, count, stride=2), :] = half_tile(flat, 0, count, halves, half)
+    for part in range(3):
+        pieces[pair, member, :, 128 * part : 128 * part + 128] = rows[part].astype(jnp.bfloat16)
 
 
 def lay_fc(flat, first, pieces, part):
@@ -615,15 +612,25 @@
     return value.astype(jnp.bfloat16)
 
 
+def turn(value, target):
+    rows, cols = value.shape
+    for first in range(0, rows, 128):
+        for lane in range(0, cols, 128):
+            part = value[first : first + 128, lane : lane + 128]
+            target[lane : lane + 128, first : first + 128] = low(wide(part).T)
+
+
 def half_of(blocks, core):
     return blocks.at[pl.ds(4 * core, 4)]
 
 
 class Reduce:
-    def __init__(self, place, away, kept, from_core, two, got, last, done, sems):
+    def __init__(
+        self, place, away, kept, from_core, two, got, last, done, sems, near_first=False
+    ):
         self.p, self.away, self.kept, self.from_core = place, away, kept, from_core
         self.two, self.got, self.last, self.done, self.sems = two, got, last, done, sems
-        self.route = Gather(place, None, None)
+        self.route = Gather(place, None, None, near_first)
         self.copies = []
 
     def _go(self, source, landing, index, target):
@@ -714,12 +721,12 @@
     flat, rows, qkv_pieces, fc_pieces, blocks, order, vec_all, qkv_land,
     fc, proj, out, fc_part, proj_part, out_part, tail, next_tail, window, unit_rows, h_own,
     branch, from_core, two, got, last, done, reduce_sem,
-    move_sem, qkv_sem, fc_send, fc_recv, rows_sem, x_sem, back_sem, spread_sem,
+    order_pad, vec_pad, x_rows, back_rows, move_sem, qkv_sem, fc_send, fc_recv, rows_sem, x_sem, back_sem, spread_sem,
     own_sem, fc_sem, proj_sem, tree_sem, h_sem, store_sem,
 ):
     p = Place()
     third_rows = weights.shape[0] // 3
-    count, width = x_in.shape
+    width, count = x_in.shape
     length = MEMBERS * count
     pairs = SLOTS // 2
     barrier = pltpu.get_barrier_semaphore()
@@ -733,32 +740,39 @@
 
     lax.fori_loop(1, DEVICES, signal, 0)
     flat[...] = weights[...].astype(jnp.float32)
+    order_pad[...] = jnp.zeros_like(order_pad)
+    order_pad[0:1, : order_in.shape[1]] = order_in[...]
+    vec_pad[...] = jnp.zeros_like(vec_pad)
+    vec_pad[: vec_in.shape[0], : vec_in.shape[1]] = vec_in[...]
     pl.semaphore_wait(barrier, DEVICES - 1)
     home = p.target(
         x=p.ctx % 2, near=p.ctx // 2 % 2, core=p.ctx // 4, y=p.fsdp // 2, far=p.fsdp % 2
     )
-    x_move = Move(p, x_in, x_all.at[p.ctx], move_sem.at[0, 0], move_sem.at[1, 0], home)
-    order_move = Move(p, order_in, order, move_sem.at[0, 1], move_sem.at[1, 1], home)
     owner = p.fsdp == 0
     qkv_moves = []
-    for member in (7, 6, 3, 2, 5, 4, 1, 0):
-
-        @pl.when(owner)
-        def _(member=member):
-            lay_qkv(flat, rows, qkv_pieces, member)
-
-        target = p.target(x=member % 2, near=member // 2 % 2, core=member // 4)
-        qkv_moves.append(
-            Move(
-                p, qkv_pieces.at[member], qkv_land.at[p.far, p.near, p.y],
-                qkv_sem.at[0, member], qkv_sem.at[1, p.near], target, owner,
+    for pair in range(pairs):
+        for member in (7, 6, 3, 2, 5, 4, 1, 0):
+
+            @pl.when(owner)
+            def _(member=member, pair=pair):
+                lay_qkv(flat, rows, qkv_pieces, member, pair)
+
+            target = p.target(x=member % 2, near=member // 2 % 2, core=member // 4)
+            qkv_moves.append(
+                Move(
+                    p, qkv_pieces.at[pair, member], qkv_land.at[pair, p.far, p.near, p.y],
+                    qkv_sem.at[0, pair, member], qkv_sem.at[1, pair, p.near], target, owner,
+                )
             )
-        )
+    turn(x_in[...], x_rows)
+    x_move = Move(p, x_rows, x_all.at[p.ctx], move_sem.at[0, 0], move_sem.at[1, 0], home)
+    order_move = Move(p, order_pad, order, move_sem.at[0, 1], move_sem.at[1, 1], home)
+    turn(back_in[...], back_rows)
 
     def vec_send(step, carry):
         other = (p.linear + step) % DEVICES
         pltpu.make_async_remote_copy(
-            src_ref=vec_in,
+            src_ref=vec_pad,
             dst_ref=vec_all.at[p.linear],
             send_sem=move_sem.at[0, 2],
             recv_sem=move_sem.at[1, 2],
@@ -768,7 +782,7 @@
         return carry
 
     lax.fori_loop(1, DEVICES, vec_send, 0)
-    pltpu.make_async_copy(vec_in, vec_all.at[p.linear], move_sem.at[1, 2]).start()
+    pltpu.make_async_copy(vec_pad, vec_all.at[p.linear], move_sem.at[1, 2]).start()
     for part in range(3):
         third = 3 * p.linear + part
         is_fc = jnp.logical_and(third >= FC_FIRST, third < PROJ_FIRST)
@@ -783,15 +797,23 @@
             lay_rows(flat, part * third_rows, rows, blocks, part)
 
     arrived(x_all.at[p.me], move_sem.at[1, 0])
-    gather_x = Gather(p, x_all, x_sem)
+    gather_x = Gather(p, x_all, x_sem, True)
     gather_x.begin()
     spreads = []
-    for near in range(2):
-        arrived(qkv_land.at[p.far, near, p.y], qkv_sem.at[1, near])
-        item = Spread(p, lambda far, y, near=near: qkv_land.at[far, near, y], spread_sem, 3 * near)
-        item.begin()
-        spreads.append(item)
+
+    def spread(pair):
+        for near in range(2):
+            arrived(qkv_land.at[pair, p.far, near, p.y], qkv_sem.at[1, pair, near])
+            item = Spread(
+                p, lambda far, y, near=near: qkv_land.at[pair, far, near, y],
+                spread_sem, 6 * pair + 3 * near,
+            )
+            item.begin()
+            spreads.append(item)
+
+    spread(0)
     gather_x.second_hop()
+    spread(1)
     gather_x.third_hop()
     fc_moves, rows_moves = [], []
     for part in range(3):
@@ -831,9 +853,9 @@
             )
         )
     gather_x.last_hop()
-    back_move = Move(p, back_in, back_all.at[p.ctx], move_sem.at[0, 3], move_sem.at[1, 3], home)
+    back_move = Move(p, back_rows, back_all.at[p.ctx], move_sem.at[0, 3], move_sem.at[1, 3], home)
     arrived(vec_all, move_sem.at[1, 2])
-    cols = vec_in.shape[-1]
+    cols = vec_pad.shape[-1]
     used = width // MEMBERS
     total = jnp.zeros(vecs.shape, jnp.float32)
     for ctx in range(MEMBERS):
@@ -861,10 +883,10 @@
         preferred_element_type=jnp.float32,
     )
     col_pos[...] = found[0:1, :] * BLOCK + inner.astype(jnp.float32)
-    for item in spreads:
+    for item in spreads[:2]:
         item.middle()
     arrived(back_all.at[p.me], move_sem.at[1, 3])
-    gather_back = Gather(p, back_all, back_sem)
+    gather_back = Gather(p, back_all, back_sem, True)
     gather_back.begin()
     gather_x.finish()
 
@@ -919,33 +941,38 @@
     proj_y.start()
     proj_own = pltpu.make_async_copy(proj_part, my_proj, own_sem.at[9])
     proj_own.start()
-    for item in spreads:
-        item.finish()
-    four = qkv_land.shape[3]
-    for far in range(2):
-        for near in range(2):
-            for y in range(2):
-                first = four * (4 * far + 2 * near + y)
-                w_qkv[first : first + four, :] = qkv_land[far, near, y]
-    store(w_qkv, w_qkv_out)
+    four = qkv_land.shape[4]
     per_part = SLOTS * HD
-    bias = jnp.concatenate(
-        [
-            member_lanes(vecs[2:3, :], p.me, per_part),
-            jnp.zeros((1, per_part), jnp.float32),
-            member_lanes(vecs[16:17, :], p.me, per_part),
-        ],
-        1,
-    )
-
-    def qkv_block(step, carry):
-        at = pl.ds(pl.multiple_of(step * 2 * count, 2 * count), 2 * count)
-        value = jnp.dot(h_first[at, :], w_qkv[...], preferred_element_type=jnp.float32)
-        qkv[at, :] = (value + bias).astype(jnp.bfloat16)
-        return carry
-
-    lax.fori_loop(0, MEMBERS // 2, qkv_block, 0)
-    store(qkv, qkv_out)
+    bias_q = member_lanes(vecs[2:3, :], p.me, per_part)
+    bias_v = member_lanes(vecs[16:17, :], p.me, per_part)
+
+    def project(pair):
+        columns = slice(384 * pair, 384 * pair + 384)
+        for item in spreads[2 * pair : 2 * pair + 2]:
+            item.finish()
+        for far in range(2):
+            for near in range(2):
+                for y in range(2):
+                    first = four * (4 * far + 2 * near + y)
+                    w_qkv[first : first + four, columns] = qkv_land[pair, far, near, y]
+        part = slice(128 * pair, 128 * pair + 128)
+        bias = jnp.concatenate(
+            [bias_q[:, part], jnp.zeros((1, 128), jnp.float32), bias_v[:, part]], 1
+        )
+
+        def qkv_block(step, carry):
+            at = pl.ds(pl.multiple_of(step * 2 * count, 2 * count), 2 * count)
+            value = jnp.dot(
+                h_first[at, :], w_qkv[:, columns], preferred_element_type=jnp.float32
+            )
+            qkv[at, columns] = (value + bias).astype(jnp.bfloat16)
+            return carry
+
+        lax.fori_loop(0, MEMBERS // 2, qkv_block, 0)
+
+    project(0)
+    for item in spreads[2:]:
+        item.middle()
     gather_back.last_hop()
     span = 2 * count
 
@@ -953,9 +980,9 @@
         def one_block(step, carry):
             at = pl.ds(pl.multiple_of(step * span, span), span)
             attn[pair, at, :] = attend_block(
-                qkv[at, 128 * pair : 128 * pair + 128],
-                qkv[:, 128 * (pairs + pair) : 128 * (pairs + pair) + 128],
-                qkv[:, 128 * (2 * pairs + pair) : 128 * (2 * pairs + pair) + 128],
+                qkv[at, 384 * pair : 384 * pair + 128],
+                qkv[:, 384 * pair + 128 : 384 * pair + 256],
+                qkv[:, 384 * pair + 256 : 384 * pair + 384],
                 row_pos[at, :],
                 col_pos[...],
             )
@@ -964,6 +991,9 @@
         lax.fori_loop(0, length // span, one_block, 0)
 
     one_pair(0)
+    project(1)
+    store(w_qkv, w_qkv_out)
+    store(qkv, qkv_out)
 
     @pl.when(beside)
     def _():
@@ -1077,11 +1107,12 @@
 
 
 def forward(x, back, order, vectors, weights):
-    rows, width = x.shape
+    width, rows = x.shape
     kind, high = jnp.bfloat16, jnp.float32
     unit, hidden = width // DEVICES, FF // MEMBERS
     four, cols = 4 * unit, 3 * SLOTS * HD
     length, pairs = MEMBERS * rows, SLOTS // 2
+    vec_cols = -(-vectors.shape[1] // 128) * 128
     any_space = pl.BlockSpec(memory_space=pl.ANY)
     vmem = pl.BlockSpec(memory_space=pltpu.VMEM)
     dma = pltpu.SemaphoreType.DMA
@@ -1093,7 +1124,7 @@
         forward_kernel,
         out_shape=[
             like(MEMBERS, rows, width),
-            like(GROUPS * vectors.shape[0], width, dtype=high),
+            like(GROUPS * 16, width, dtype=high),
             like(length, 1, dtype=high),
             like(1, length, dtype=high),
             like(width, cols),
@@ -1107,7 +1138,7 @@
             like(rows, width, dtype=high),
             like(MEMBERS, rows, width),
         ],
-        in_specs=[any_space] * 4 + [vmem],
+        in_specs=[vmem] * 5,
         out_specs=[any_space] + [vmem] * 3 + [any_space] * 3 + [vmem] + [any_space] * 2
         + [vmem] * 3 + [any_space],
         scratch_shapes=[
@@ -1119,12 +1150,12 @@
             pltpu.VMEM((hidden, width), kind),
             pltpu.VMEM(weights.shape, high),
             pltpu.VMEM((-(-width // 128), four, 128), high),
-            pltpu.VMEM((MEMBERS, four, cols), kind),
+            pltpu.VMEM((pairs, MEMBERS, four, cols // pairs), kind),
             pltpu.VMEM((3, MEMBERS, unit, hidden), kind),
             pltpu.VMEM((3, four, width), kind),
-            pltpu.VMEM(order.shape, order.dtype),
-            pltpu.VMEM((DEVICES,) + vectors.shape, kind),
-            pltpu.VMEM((2, 2, 2, four, cols), kind),
+            pltpu.VMEM((128, 128), order.dtype),
+            pltpu.VMEM((DEVICES, 16, vec_cols), kind),
+            pltpu.VMEM((pairs, 2, 2, 2, four, cols // pairs), kind),
             pltpu.VMEM((DEVICES, unit, hidden), kind),
             pltpu.VMEM((2, 2, four, width), kind),
             pltpu.VMEM((four, width), kind),
@@ -1140,14 +1171,18 @@
         ]
         + reduce_buffers(rows, width)
         + [
+            pltpu.VMEM((128, 128), order.dtype),
+            pltpu.VMEM((16, vec_cols), kind),
+            pltpu.VMEM((rows, width), kind),
+            pltpu.VMEM((rows, width), kind),
             dma((2, 4)),
-            dma((2, 8)),
+            dma((2, pairs, 8)),
             dma((3, 8)),
             dma((8,)),
             dma((2, 3)),
             dma((2, 7)),
             dma((2, 7)),
-            dma((2, 6)),
+            dma((2, 12)),
             dma((9 + 1,)),
             dma((2, 24)),
             dma((2, 3)),
@@ -1180,9 +1215,11 @@
 
 def middle_kernel(
     h_in, back_all, vecs, resid_own, w_fc_in, w_proj_in,
-    grad_fc, grad_proj, made, dresid, dbranch, sums, fc_sums,
+    grad_fc, grad_proj, proj_go, made, dresid, branch_all, sums, fc_sums,
     h_second, back, w_fc, w_proj, act, dpre, dh_part, made_part, g_fc, g_proj,
-    from_core, two, got, last, done, reduce_sem, load_sem, store_sem,
+    proj_y, from_core, two, got, last, done, reduce_sem,
+    load_sem, store_sem, fold_sem,
+    dbranch, branch_sem,
 ):
     p = Place()
     length, width = h_second.shape
@@ -1199,7 +1236,8 @@
         loads.append(copy)
     reduce = Reduce(p, half_of(dh_part, 1 - p.core), half_of(dh_part, p.core), from_core, two, got, last, done, reduce_sem)
     route = reduce.route
-    greet((route.first, route.second, route.other))
+    to_y = p.target(y=1 - p.y)
+    greet((route.first, route.second, route.other, to_y))
     bias_fc = jnp.zeros((1, hidden), jnp.float32)
     block = hidden // GROUPS
     for member in range(MEMBERS):
@@ -1234,30 +1272,6 @@
 
     lax.fori_loop(0, MEMBERS // 2, one_block, 0)
     reduce.begin()
-    chunk = 256
-
-    def one_proj(step, carry):
-        lanes = pl.ds(pl.multiple_of(step * chunk, chunk), chunk)
-        store_rows(g_proj, 0, dot_tn(act[...], back[:, lanes]), lanes)
-        return carry
-
-    lax.fori_loop(0, 3, one_proj, 0)
-    reduce.second()
-    lax.fori_loop(3, width // chunk, one_proj, 0)
-    tail = slice(width // chunk * chunk, width)
-    if width % chunk:
-        store_rows(g_proj, 0, dot_tn(act[...], back[:, tail]), tail)
-    stores = [pltpu.make_async_copy(g_proj, grad_proj, store_sem.at[0])]
-    stores[0].start()
-    for first in range(0, width, chunk):
-        size = min(chunk, width - first)
-        store_rows(
-            g_fc, first, dot_tn(h_second[:, first : first + size], dpre[...]), at=FC_POSITION
-        )
-        if first + size == 4 * chunk:
-            reduce.third()
-    stores.append(pltpu.make_async_copy(g_fc, grad_fc, store_sem.at[1]))
-    stores[1].start()
 
     def one_made(step, carry):
         at = pl.ds(pl.multiple_of(step * span, span), span)
@@ -1267,8 +1281,35 @@
         return carry
 
     lax.fori_loop(0, MEMBERS // 2, one_made, 0)
-    stores.append(pltpu.make_async_copy(made_part, made, store_sem.at[2]))
-    stores[2].start()
+    reduce.second()
+    stores = [pltpu.make_async_copy(made_part, made, store_sem.at[3])]
+    stores[0].start()
+    chunk = 256
+
+    def one_proj(step, carry):
+        lanes = pl.ds(pl.multiple_of(step * chunk, chunk), chunk)
+        store_rows(g_proj, 0, dot_tn(act[...], back[:, lanes]), lanes)
+        return carry
+
+    lax.fori_loop(0, width // chunk, one_proj, 0)
+    tail = slice(width // chunk * chunk, width)
+    if width % chunk:
+        store_rows(g_proj, 0, dot_tn(act[...], back[:, tail]), tail)
+    over_y = remote(
+        g_proj.at[2 * (1 - p.y) + 1 - p.far], proj_y, fold_sem, 0, to_y
+    )
+    over_y.start()
+    reduce.third()
+    stores.append(pltpu.make_async_copy(g_proj, grad_proj, store_sem.at[0]))
+    stores[-1].start()
+    for first in range(0, width, chunk):
+        size = min(chunk, width - first)
+        store_rows(
+            g_fc, first, dot_tn(h_second[:, first : first + size], dpre[...]), at=FC_POSITION
+        )
+    stores.append(pltpu.make_async_copy(g_fc, grad_fc, store_sem.at[1]))
+    stores[-1].start()
+
     dh = reduce.result()
     center = resid_own[...] - jnp.mean(resid_own[...], -1, keepdims=True)
     scale = lax.rsqrt(jnp.mean(center * center, -1, keepdims=True) + epsilon_norm)
@@ -1280,11 +1321,27 @@
     dresid[...] = value
     branch = low(value)
     dbranch[...] = branch
+    gather = Gather(p, branch_all, branch_sem)
+    for name, index, target in (
+        ("a", 0, gather.first), ("b", 1, gather.second), ("c", 2, gather.other),
+    ):
+        copy = remote(dbranch, branch_all.at[p.me], branch_sem, index, target)
+        copy.start()
+        gather.copies[name] = copy
+    stores.append(pltpu.make_async_copy(dbranch, branch_all.at[p.me], store_sem.at[2]))
+    stores[-1].start()
     sums[0:1, :] = jnp.sum(dh * hat, 0, keepdims=True)
     sums[1:2, :] = jnp.sum(dh, 0, keepdims=True)
     sums[2:3, :] = jnp.sum(wide(branch), 0, keepdims=True)
     sums[3:4, :] = jnp.sum(back_own, 0, keepdims=True)
     sums[4:8, :] = jnp.zeros((4, width), jnp.float32)
+    gather.second_hop()
+    gather.third_hop()
+    over_y.wait_recv()
+    proj_go[...] = low(wide(g_proj[2 * p.y + 1 - p.far]) + wide(proj_y[...]))
+    over_y.wait_send()
+    gather.last_hop()
+    gather.finish()
     reduce.sent()
     for copy in stores:
         copy.wait()
@@ -1311,14 +1368,15 @@
         out_shape=[
             like(DEVICES, four // 4, hidden),
             like(GROUPS, four, width),
+            like(four, width),
             like(MEMBERS, rows, width),
             like(rows, width, dtype=high),
-            like(rows, width),
+            like(MEMBERS, rows, width),
             like(8, width, dtype=high),
             like(1, hidden, dtype=high),
         ],
         in_specs=[any_space] * 2 + [vmem] * 2 + [any_space] * 2,
-        out_specs=[any_space] * 3 + [vmem] * 4,
+        out_specs=[any_space] * 2 + [vmem, any_space, vmem, any_space] + [vmem] * 2,
         scratch_shapes=[
             buffer(*h_second.shape),
             buffer(*back_all.shape),
@@ -1330,9 +1388,10 @@
             buffer(MEMBERS, rows, width),
             buffer(DEVICES, four // 4, hidden),
             buffer(GROUPS, four, width),
+            buffer(four, width),
         ]
         + reduce_buffers(rows, width)
-        + [dma((4,)), dma((3,))],
+        + [dma((4,)), dma((4,)), dma((2, 1)), buffer(rows, width), dma((2, 7))],
         compiler_params=pltpu.CompilerParams(
             collective_id=3, has_side_effects=True, vmem_limit_bytes=VMEM_BYTES
         ),
@@ -1382,23 +1441,22 @@
 
 
 def backward_kernel(
-    dbranch, made_in, grad_fc, grad_proj, attn, qkv, row_pos, col_pos, w_heads, w_qkv_in,
+    branch_in, made_in, grad_fc, grad_proj, proj_go, attn, qkv, row_pos, col_pos, w_heads, w_qkv_in,
     h_in, x_own, resid_own, dresid, vecs, sums, fc_sums,
     out_home, grad_home, qkv_back, fc_back, rows_back, vec_back,
-    branch_all, dattn, dqkv, key_sum, value_sum, w_qkv, h_first, made, dh_part,
-    fc_own, proj_own, g_qkv, g_heads, g_out, result, input_grad, vec_rows, vec_go, vec_got,
-    fc_y, proj_y, qkv_y, out_y, fc_go, proj_go, qkv_go, out_go,
+    branch_all, dattn, dqkv, key_sum, value_sum, w_qkv, h_first, dh_part, made, result,
+    fc_own, proj_own, g_qkv, g_heads, g_out, input_grad, vec_rows, vec_go, vec_got,
+    fc_y, proj_y, qkv_y, out_y, fc_go, qkv_go, out_go,
     fc_far, proj_far, qkv_far, out_far, fc_sum, proj_sum, qkv_sum, out_sum,
     core_a, two_a, got_a, last_a, done_a, sem_a, core_b, two_b, got_b, last_b, done_b, sem_b,
-    load_sem, branch_sem, fold_sem, tree_sem, vec_sem, home_sem,
+    load_sem, fold_sem, tree_sem, vec_sem, home_sem,
     qkv_send, qkv_recv, fc_send, fc_recv, rows_send, rows_recv,
 ):
     p = Place()
-    count, width = dbranch.shape
+    _, count, width = branch_in.shape
     length = MEMBERS * count
     four = grad_proj.shape[1]
     pairs = SLOTS // 2
-    per_part = SLOTS * HD
     loads = []
 
     def load(source, target):
@@ -1406,26 +1464,19 @@
         copy.start()
         loads.append(copy)
 
+    load(branch_in, branch_all)
+    load(half_of(made_in, p.core), made)
+    load(grad_proj.at[2 * p.y + p.far], proj_own)
     for far in range(2):
-        load(grad_proj.at[2 * p.y + far], proj_own.at[far])
         for near in range(2):
             load(grad_fc.at[far, p.y, near], fc_own.at[far, near])
-    load(half_of(made_in, p.core), made)
     load(w_qkv_in, w_qkv)
     load(h_in, h_first)
     greet_all(p)
-    gather = Gather(p, branch_all, branch_sem)
-    for name, index, target in (
-        ("a", 0, gather.first), ("b", 1, gather.second), ("c", 2, gather.other),
-    ):
-        copy = remote(dbranch, branch_all.at[p.me], branch_sem, index, target)
-        copy.start()
-        gather.copies[name] = copy
-    load(dbranch, branch_all.at[p.me])
-    proj_fold = Fold(
-        p, lambda far: grad_proj.at[2 * (1 - p.y) + far], lambda far: proj_own.at[far],
-        lambda far: proj_y.at[far], proj_go, proj_far, fold_sem, 0,
-    )
+    proj_over_y = remote(
+        grad_proj.at[2 * (1 - p.y) + p.far], proj_y, fold_sem, 0, p.target(y=1 - p.y)
+    )
+    proj_over_far = remote(proj_go, proj_far, fold_sem, 1, p.target(far=1 - p.far))
     fc_folds = [
         Fold(
             p, lambda far, near=near: grad_fc.at[far, 1 - p.y, near],
@@ -1437,23 +1488,23 @@
     ]
     qkv_folds = [
         Fold(
-            p, lambda far, near=near: g_qkv.at[4 * far + 2 * near + 1 - p.y],
-            lambda far, near=near: g_qkv.at[4 * far + 2 * near + p.y],
-            lambda far, near=near: qkv_y.at[far, near],
-            qkv_go.at[near], qkv_far.at[near], fold_sem, 9 + 3 * near,
-        )
-        for near in range(2)
+            p, lambda far, pair=pair: g_qkv.at[pair, pl.ds(4 * far + 2 * (1 - p.y), 2)],
+            lambda far, pair=pair: g_qkv.at[pair, pl.ds(4 * far + 2 * p.y, 2)],
+            lambda far, pair=pair: qkv_y.at[pair, far],
+            qkv_go.at[pair], qkv_far.at[pair], fold_sem, 9 + 3 * pair,
+        )
+        for pair in range(pairs)
     ]
-    proj_fold.begin()
+    reduce_made = Reduce(
+        p, half_of(made_in, 1 - p.core), made, core_a, two_a, got_a, last_a, done_a, sem_a
+    )
+    reduce_made.begin()
+    proj_over_far.start()
     for item in fc_folds:
         item.begin()
-    gather.second_hop()
-    gather.third_hop()
-    gather.last_hop()
     for copy in loads:
         copy.wait()
-    proj_fold.middle()
-    gather.finish()
+    proj_over_y.start()
     span = 2 * count
 
     def one_dattn(step, carry):
@@ -1465,18 +1516,12 @@
         return carry
 
     lax.fori_loop(0, length // span, one_dattn, 0)
-    reduce_made = Reduce(
-        p, half_of(made_in, 1 - p.core), made, core_a, two_a, got_a, last_a, done_a, sem_a
-    )
-    reduce_made.begin()
-    proj_fold.rest()
-
     def one_pair(pair):
         key_sum[...] = jnp.zeros_like(key_sum)
         value_sum[...] = jnp.zeros_like(value_sum)
 
         def columns(part):
-            return slice(128 * (pairs * part + pair), 128 * (pairs * part + pair) + 128)
+            return slice(384 * pair + 128 * part, 384 * pair + 128 * part + 128)
 
         def one_block(step, carry):
             at = pl.ds(pl.multiple_of(step * span, span), span)
@@ -1506,19 +1551,34 @@
         dqkv[:, columns(1)] = low(key_sum[...] * 0.125)
         dqkv[:, columns(2)] = low(value_sum[...])
 
+    chunk = 256
+
+    def one_grad(pair):
+        columns = slice(384 * pair, 384 * pair + 384)
+        for first in range(0, width, chunk):
+            size = min(chunk, width - first)
+            value = dot_tn(h_first[:, first : first + size], dqkv[:, columns])
+            store_rows(g_qkv.at[pair], first, value, at=(0, 2, 1, 3, 4, 6, 5, 7))
+        qkv_folds[pair].begin()
+
+    reduce_made.second()
     one_pair(0)
+    reduce_made.third()
+    one_grad(0)
     for item in fc_folds:
         item.middle()
     for item in fc_folds:
         item.rest()
-    reduce_made.second()
     one_pair(1)
-    reduce_made.third()
     for part in range(3):
-        last = 128 * (pairs * part + pairs - 1)
+        last = 384 * (pairs - 1) + 128 * part
         value = dqkv[:, last : last + 128]
         keep = jnp.logical_or(lane_of(value.shape) == 0, p.me == MEMBERS - 1)
         dqkv[:, last : last + 128] = jnp.where(keep, value, jnp.zeros_like(value))
+    one_grad(1)
+    qkv_folds[0].middle()
+    for item in qkv_folds:
+        item.rest()
 
     def one_part(step, carry):
         at = pl.ds(pl.multiple_of(step * span, span), span)
@@ -1530,23 +1590,22 @@
     lax.fori_loop(0, length // span, one_part, 0)
     reduce_dh = Reduce(
         p, half_of(dh_part, 1 - p.core), half_of(dh_part, p.core), core_b, two_b, got_b, last_b,
-        done_b, sem_b,
+        done_b, sem_b, True,
     )
     reduce_dh.begin()
-    chunk = 256
-    for first in range(0, width, chunk):
-        size = min(chunk, width - first)
-        store_rows(g_qkv, first, dot_tn(h_first[:, first : first + size], dqkv[...]))
-    for item in qkv_folds:
-        item.begin()
-    for item in qkv_folds:
-        item.rest()
+    home = p.target(
+        x=p.ctx % 2, near=p.ctx // 2 % 2, core=p.ctx // 4, y=p.fsdp // 2, far=p.fsdp % 2
+    )
+    turn(low(resid_own[...] + reduce_made.result() + vecs[33:34, :]), result)
+    moves = [Move(p, result, out_home, home_sem.at[0, 0], home_sem.at[1, 0], home)]
     reduce_dh.second()
-    proj_sum[...] = proj_fold.end()
+    proj_over_y.wait_recv()
+    proj_over_far.wait_recv()
+    proj_sum[...] = low(wide(proj_own[...]) + wide(proj_y[...]) + wide(proj_far[...]))
     target, part = shard_of(PROJ_FIRST + lookup(PROJ_UNIT, p.linear))
-    moves = [
+    moves.append(
         Move(p, proj_sum, rows_back.at[part], rows_send.at[0], rows_recv.at[part], target)
-    ]
+    )
     for pair in range(pairs):
         total = 0.0
         for block in range(MEMBERS):
@@ -1566,12 +1625,6 @@
         over_y.start()
 
     reduce_dh.third()
-    result[...] = low(resid_own[...] + reduce_made.result() + vecs[33:34, :])
-    home = p.target(
-        x=p.ctx % 2, near=p.ctx // 2 % 2, core=p.ctx // 4, y=p.fsdp // 2, far=p.fsdp % 2
-    )
-    moves.append(Move(p, result, out_home, home_sem.at[0, 0], home_sem.at[1, 0], home))
-
     for near in range(2):
         fc_sum[near] = fc_folds[near].end()
         for slot in range(4):
@@ -1600,7 +1653,7 @@
     scaled = dh * vecs[0:1, :]
     inner = jnp.mean(scaled * hat, -1, keepdims=True)
     value = (scaled - jnp.mean(scaled, -1, keepdims=True) - hat * inner) * scale
-    input_grad[...] = low(dresid[...] + value)
+    turn(low(dresid[...] + value), input_grad)
     moves.append(Move(p, input_grad, grad_home, home_sem.at[0, 1], home_sem.at[1, 1], home))
     bias_sums = jnp.sum(wide(dqkv[...]), 0, keepdims=True)
 
@@ -1620,8 +1673,15 @@
     heads = [head_start(member) * HD for member in range(MEMBERS)]
     vec_rows[0:1, :] = jnp.sum(dh * hat, 0, keepdims=True)
     vec_rows[1:2, :] = jnp.sum(dh, 0, keepdims=True)
-    vec_rows[2:3, :] = placed(bias_sums[:, :per_part], heads, p.me)
-    vec_rows[3:4, :] = placed(bias_sums[:, 2 * per_part :], heads, p.me)
+    for row, part in ((2, 0), (3, 2)):
+        value = jnp.concatenate(
+            [
+                bias_sums[:, 384 * pair + 128 * part : 384 * pair + 128 * part + 128]
+                for pair in range(pairs)
+            ],
+            1,
+        )
+        vec_rows[row : row + 1, :] = placed(value, heads, p.me)
     vec_rows[4:5, :] = sums[2:3, :]
     vec_rows[5:7, :] = sums[0:2, :]
     vec_rows[7:8, :] = sums[3:4, :]
@@ -1653,8 +1713,7 @@
 
     lax.fori_loop(1, DEVICES, vec_send, 0)
     pltpu.make_async_copy(vec_go.at[p.linear], vec_got.at[p.linear], vec_sem.at[1]).start()
-    for item in qkv_folds:
-        item.middle()
+    qkv_folds[1].middle()
     @pl.when(root)
     def _():
         over_far.wait_recv()
@@ -1664,22 +1723,24 @@
     moves.append(
         Move(p, out_sum, rows_back.at[part], rows_send.at[1], rows_recv.at[part], target, root)
     )
-    for near in range(2):
-        qkv_sum[near] = qkv_folds[near].end()
-        target = (0 * p.fsdp, 4 * p.far + 2 * near + p.y)
-        moves.append(
-            Move(
-                p, qkv_sum.at[near], qkv_back.at[p.me], qkv_send.at[near], qkv_recv.at[p.me],
-                target,
+    for pair in range(pairs):
+        qkv_sum[pair] = qkv_folds[pair].end()
+        for near in range(2):
+            target = (0 * p.fsdp, 4 * p.far + 2 * near + p.y)
+            moves.append(
+                Move(
+                    p, qkv_sum.at[pair, near], qkv_back.at[p.me, pair],
+                    qkv_send.at[pair, near], qkv_recv.at[p.me, pair], target,
+                )
             )
-        )
     arrived(vec_got, vec_sem.at[1])
     vec_back[...] = jnp.sum(vec_got[...], 0)
 
     @pl.when(p.fsdp == 0)
     def _():
         for member in range(MEMBERS):
-            arrived(qkv_back.at[member], qkv_recv.at[member])
+            for pair in range(pairs):
+                arrived(qkv_back.at[member, pair], qkv_recv.at[member, pair])
 
     for part in range(3):
         third = 3 * p.linear + part
@@ -1698,8 +1759,10 @@
     arrived(out_home, home_sem.at[1, 0])
     arrived(grad_home, home_sem.at[1, 1])
     arrived(vec_got.at[pl.ds(1, DEVICES - 1)], vec_sem.at[0])
-    for item in [proj_fold, reduce_made, reduce_dh] + fc_folds + qkv_folds + moves:
+    for item in [reduce_made, reduce_dh] + fc_folds + qkv_folds + moves:
         item.sent()
+    proj_over_y.wait_send()
+    proj_over_far.wait_send()
 
     @pl.when(jnp.logical_not(same_y))
     def _():
@@ -1711,11 +1774,11 @@
 
 
 def backward(
-    dbranch, made, grad_fc, grad_proj, attn, qkv, row_pos, col_pos, w_heads, w_qkv,
+    branch_all, made, grad_fc, grad_proj, proj_go, attn, qkv, row_pos, col_pos, w_heads, w_qkv,
     h_first, x_own, resid_own, dresid, vecs, sums, fc_sums,
 ):
     kind, high = jnp.bfloat16, jnp.float32
-    rows, width = dbranch.shape
+    _, rows, width = branch_all.shape
     length = MEMBERS * rows
     four, cols = width // MEMBERS, qkv.shape[1]
     unit, hidden = four // 4, fc_sums.shape[1]
@@ -1734,14 +1797,14 @@
     return pl.pallas_call(
         backward_kernel,
         out_shape=[
-            like(rows, width),
-            like(rows, width),
-            like(MEMBERS, four, cols),
+            like(width, rows),
+            like(width, rows),
+            like(MEMBERS, 2, four, cols // 2),
             like(3, MEMBERS, unit, hidden),
             like(3, four, width),
             like(8, used, dtype=high),
         ],
-        in_specs=[vmem] + [any_space] * 3 + [vmem] * 5 + [any_space] * 2 + [vmem] * 6,
+        in_specs=[any_space] * 4 + [vmem] * 6 + [any_space] * 2 + [vmem] * 6,
         out_specs=[any_space] * 5 + [vmem],
         scratch_shapes=[
             buffer(MEMBERS, rows, width),
@@ -1751,43 +1814,39 @@
             buffer(length, 2 * HD, dtype=high),
             buffer(*w_qkv.shape),
             buffer(*h_first.shape),
+            buffer(MEMBERS, rows, width),
             buffer(MEMBERS // 2, rows, width),
-            buffer(MEMBERS, rows, width),
+            buffer(width, rows),
             buffer(2, 2, 4, unit, hidden),
-            buffer(2, four, width),
-            buffer(MEMBERS, four, cols),
+            buffer(four, width),
+            buffer(2, MEMBERS, four, cols // 2),
             buffer(per_part, width, dtype=high),
             buffer(four, width),
-            buffer(rows, width),
-            buffer(rows, width),
+            buffer(width, rows),
             buffer(16, width, dtype=high),
             buffer(DEVICES, 8, used, dtype=high),
             buffer(DEVICES, 8, used, dtype=high),
         ]
         + [
-            buffer(2, 2, 4, unit, hidden), buffer(2, four, width), buffer(2, 2, four, cols),
-            buffer(four, width),
+            buffer(2, 2, 4, unit, hidden), buffer(four, width),
+            buffer(2, 2, 2, four, cols // 2), buffer(four, width),
+            buffer(2, 4, unit, hidden), buffer(2, 2, four, cols // 2), buffer(four, width),
         ]
         + [
-            buffer(2, 4, unit, hidden), buffer(four, width), buffer(2, four, cols),
+            buffer(2, 4, unit, hidden), buffer(four, width), buffer(2, 2, four, cols // 2),
             buffer(four, width),
         ]
         * 2
-        + [
-            buffer(2, 4, unit, hidden), buffer(four, width), buffer(2, four, cols),
-            buffer(four, width),
-        ]
         + reduce_buffers(rows, width)
         + reduce_buffers(rows, width)
         + [
             dma((12,)),
-            dma((2, 7)),
             dma((2, 15)),
             dma((2, 2)),
             dma((2,)),
             dma((2, 2)),
-            dma((2,)),
-            dma((8,)),
+            dma((2, 2)),
+            dma((8, 2)),
             dma((2, 4)),
             dma((3, 8)),
             dma((2,)),
@@ -1798,7 +1857,7 @@
         ),
         name="backward",
     )(
-        dbranch, made, grad_fc, grad_proj, attn, qkv, row_pos, col_pos, w_heads, w_qkv,
+        branch_all, made, grad_fc, grad_proj, proj_go, attn, qkv, row_pos, col_pos, w_heads, w_qkv,
         h_first, x_own, resid_own, dresid, vecs, sums, fc_sums,
     )
 
@@ -1828,22 +1887,23 @@
 
 
 def unlay_qkv(flat, tiles, back):
-    count = back.shape[1] // 2
+    count = back.shape[2] // 2
+    each = 3 * SLOTS // 2
     for member in range(MEMBERS):
-        for tile in range(back.shape[2] // 128):
-            tiles[member * (back.shape[2] // 128) + tile] = wide(
-                back[member, :, 128 * tile : 128 * tile + 128]
-            )
+        for pair in range(SLOTS // 2):
+            for part in range(3):
+                tiles[member * each + 3 * pair + part] = wide(
+                    back[member, pair, :, 128 * part : 128 * part + 128]
+                )
     halves = 3 * HEADS
 
     def half(index, lane):
         odd, at = divmod(index, halves)
         part, head = divmod(at, HEADS)
         member, slot = head_place(head)
-        col = 64 * (SLOTS * part + slot)
-        tile = member * (back.shape[2] // 128) + col // 128
+        tile = member * each + 3 * (slot // 2) + part
         return piece(
-            lambda _: tiles[tile, pl.ds(odd, count, stride=2), :], col % 128, lane, HD
+            lambda _: tiles[tile, pl.ds(odd, count, stride=2), :], HD * (slot % 2), lane, HD
         )
 
     for row in range(halves):
@@ -1898,7 +1958,9 @@
 
 
 def update_kernel(
-    qkv_in, fc_in, rows_in, weights, first, second, moment, squares, new,
+    qkv_in, fc_in, rows_in, vec_back, vectors, first_vec, second_vec,
+    weights, first, second,
+    moment_vec, squares_vec, new_vec, moment, squares, new,
     flat, tiles, qkv_back, fc_back, rows_back, sem,
 ):
     step = pl.program_id(0)
@@ -1906,6 +1968,13 @@
 
     @pl.when(step == 0)
     def _():
+        rows, cols = vectors.shape
+        result = adamw(
+            vectors[...], vec_back[:rows, :cols], first_vec[...], second_vec[...],
+            rate_vector, 0.0,
+        )
+        moment_vec[...], squares_vec[...], new_vec[...] = result
+
         @pl.when(linear < MEMBERS)
         def _():
             copy = pltpu.make_async_copy(qkv_in, qkv_back, sem.at[0])
@@ -1942,24 +2011,29 @@
     moment[...], squares[...], new[...] = result
 
 
-def update(qkv_back, fc_back, rows_back, weights, first, second):
+def update(
+    qkv_back, fc_back, rows_back, vec_back, vectors, first_vec, second_vec,
+    weights, first, second,
+):
     high = jnp.float32
     local = weights.shape[0]
     steps = 10
     size = -(-local // (16 * steps)) * 16
     block = pl.BlockSpec((size, 128), lambda i: (i, 0))
     any_space = pl.BlockSpec(memory_space=pl.ANY)
+    vmem = pl.BlockSpec(memory_space=pltpu.VMEM)
     kind = jax.ShapeDtypeStruct((local, 128), high)
-    tile_count = max(qkv_back.shape[0] * qkv_back.shape[2] // 128, MEMBERS * 7)
+    small = jax.ShapeDtypeStruct(vectors.shape, high)
+    tile_count = MEMBERS * max(3 * SLOTS // 2, -(-fc_back.shape[3] // 128))
     return pl.pallas_call(
         update_kernel,
         grid=(steps,),
-        in_specs=[any_space] * 3 + [block] * 3,
-        out_specs=[block] * 3,
-        out_shape=[kind] * 3,
+        in_specs=[any_space] * 3 + [vmem] * 4 + [block] * 3,
+        out_specs=[vmem] * 3 + [block] * 3,
+        out_shape=[small] * 3 + [kind] * 3,
         scratch_shapes=[
             pltpu.VMEM((size * steps, 128), high),
-            pltpu.VMEM((tile_count, qkv_back.shape[1], 128), high),
+            pltpu.VMEM((tile_count, qkv_back.shape[2], 128), high),
             pltpu.VMEM(qkv_back.shape, qkv_back.dtype),
             pltpu.VMEM(fc_back.shape, fc_back.dtype),
             pltpu.VMEM(rows_back.shape, rows_back.dtype),
@@ -1967,38 +2041,40 @@
         ],
         compiler_params=pltpu.CompilerParams(vmem_limit_bytes=VMEM_BYTES),
         name="update",
-    )(qkv_back, fc_back, rows_back, weights, first, second)
+    )(
+        qkv_back, fc_back, rows_back, vec_back, vectors, first_vec, second_vec, weights, first,
+        second,
+    )
 
 
 def per_device_groups(
     inputs, cotangent, slot_order, weights, vectors, first_w, second_w, first_vec, second_vec
 ):
-    seqs, rows, width = inputs.shape
+    _, rows, width = inputs.shape
     length = rows * MEMBERS
-    order = jnp.pad(slot_order, ((0, 127), (0, 128 - slot_order.shape[1])))
-    vec_rows, vec_cols = vectors.shape
-    padded = jnp.pad(vectors, ((0, 16 - vec_rows), (0, -vec_cols % 128)))
     (
         back_all, vecs, row_pos, col_pos, own_qkv, h_first, qkv, attn, own_fc, own_proj, w_heads,
         x_own, resid_own, h_second,
     ) = forward(
-        inputs.reshape(rows, width), cotangent.reshape(rows, width), order, padded, weights
-    )
-    grad_fc, grad_proj, made, dresid, dbranch, sums, fc_sums = middle(
+        inputs[0].T, cotangent[0].T, slot_order, vectors, weights
+    )
+    grad_fc, grad_proj, proj_go, made, dresid, branch_all, sums, fc_sums = middle(
         h_second.reshape(length, width), back_all.reshape(length, width), vecs, resid_own,
         own_fc, own_proj,
     )
-    outputs, input_grad, qkv_back, fc_back, rows_back, vec_back = backward(
-        dbranch, made, grad_fc.reshape((2, 2, 2, 4) + grad_fc.shape[1:]), grad_proj, attn, qkv,
-        row_pos, col_pos, w_heads, own_qkv, h_first, x_own, resid_own, dresid, vecs, sums,
-        fc_sums,
-    )
-    outputs = outputs.reshape(seqs, rows, width)
-    input_grad = input_grad.reshape(seqs, rows, width)
-    new_w = update(qkv_back, fc_back, rows_back, weights, first_w, second_w)
-    owned_vec = vec_back[:vec_rows, :vec_cols]
-    new_vec = adamw(vectors, owned_vec, first_vec, second_vec, rate_vector, 0.0)
-    return (outputs, input_grad, new_w[0], new_w[1], new_w[2], new_vec[0], new_vec[1], new_vec[2])
+    out_home, grad_home, qkv_back, fc_back, rows_back, vec_back = backward(
+        branch_all, made, grad_fc.reshape((2, 2, 2, 4) + grad_fc.shape[1:]), grad_proj, proj_go,
+        attn, qkv, row_pos, col_pos, w_heads, own_qkv, h_first, x_own, resid_own, dresid, vecs,
+        sums, fc_sums,
+    )
+    new = update(
+        qkv_back, fc_back, rows_back, vec_back, vectors, first_vec, second_vec, weights,
+        first_w, second_w,
+    )
+    moment_vec, squares_vec, new_vec, moment_w, squares_w, new_w = new
+    return (
+        out_home.T[None], grad_home.T[None], moment_w, squares_w, new_w, moment_vec, squares_vec, new_vec
+    )
 
 
 def solution(mesh):

time: 465 us -> 447 us (0.961)
  the two profiles are of different devices: /device:TPU:0 before, /device:TPU:4 now
where the time goes in v5:
time: 447 us; the launch traced here: 441 us
  Pallas kernels  438 us (98%)
    pallas_call x1, Pallas kernels, forward(): pl.pallas_call(forward_kernel, out_shape=[like(MEMBERS, rows, width), lik...  190 us
    pallas_call x1, Pallas kernels, backward(): pl.pallas_call(backward_kernel, out_shape=[like(width, rows), like(width,...  169 us
    pallas_call x1, Pallas kernels, middle(): pl.pallas_call(middle_kernel, out_shape=[like(DEVICES, four // 4, hidden)...  63 us
    pallas_call x1, Pallas kernels, update(): pl.pallas_call(update_kernel, grid=(steps,), in_specs=[any_space] * 3 + [...  16.2 us

profile of v5, /device:TPU:4, one launch (start us, length us, event | category | flops | bytes accessed | tf_op | source)
XLA Modules:
  0.0 440.8 jit_solution(10890701902421774557)
XLA Ops:
  0.6 190.0 %forward.1 = (bf16[8,128,1600]{2,1,0:T(8,128)(2,1)}, f32[64,1600]{1,0:T(8,128)}, f32[1024,1]{1,0:T(8,128)}, f32[1,1024]{1,0:T(1,128)}, bf16[1600,768]{1,0:T(8,12...) custom-call(bf16[1600,128]{1,0:T(8,128)(2,1)} %bitcast.20, ...), custom_call_target="tpu_custom_call" | custom-call | tf_op jit(solution)/shard_map/forward/pallas_call | solution.py:1123
  190.7 63.0 %middle.1 = (bf16[32,50,800]{2,1,0:T(8,128)(2,1)}, bf16[4,200,1600]{2,1,0:T(8,128)(2,1)}, bf16[200,1600]{1,0:T(8,128)(2,1)}, bf16[8,128,1600]{2,1,0:T(8,128)(2,1...) custom-call(bf16[1024,1600]{1,0:T(8,128)(2,1)} %bitcast.16, ...), custom_call_target="tpu_custom_call" | custom-call | tf_op jit(solution)/shard_map/middle/pallas_call | solution.py:1366
  253.7 169.1 %backward.1 = (bf16[1600,128]{1,0:T(8,128)(2,1)}, bf16[1600,128]{1,0:T(8,128)(2,1)}, bf16[8,2,200,384]{3,2,1,0:T(8,128)(2,1)}, bf16[3,8,50,800]{3,2,1,0:T(8,128)...) custom-call(bf16[8,128,1600]{2,1,0:T(8,128)(2,1)} %get-tuple-element.48.branch_in, ...), custom_call_target="tpu_custom_call" | custom-call | tf_op jit(solution)/shard_map/backward/pallas_call | solution.py:1797
  422.8 0.0 copy-start.1
  422.8 0.0 copy-start
  422.8 16.2 %update.1 = (f32[3,200]{1,0:T(4,128)}, f32[3,200]{1,0:T(4,128)}, f32[3,200]{1,0:T(4,128)}, f32[7500,128]{1,0:T(8,128)}, f32[7500,128]{1,0:T(8,128)}, /*index=5*/f32[7500,128]{1,0:T(8,128)}) custom-call(bf16[8,2,200,384]{3,2,1,0:T(8,128)(2,1)} %get-tuple-element.66.qkv_in, bf16[3,8,50,800]{3,2,1,0:T(8,128)(2,1)} %get-tuple-element.67.fc_in, ...), custom_call_target="tpu_custom_call" | custom-call | tf_op jit(solution)/shard_map/update/pallas_call | solution.py:2028
  439.1 0.0 copy-done.1
  439.1 0.8 copy.19
  439.8 0.0 copy-done
  439.8 0.8 copy.20
Async XLA Ops:
  422.8 16.3 %copy-start.1 = (bf16[1600,128]{1,0:T(8,128)(2,1)S(1)}, bf16[1600,128]{1,0:T(8,128)(2,1)}, u32[]{:S(2)}) copy-start(bf16[1600,128]{1,0:T(8,128)(2,1)} %get-tuple-element.64) | copy-start | bytes 1228804
  422.8 17.0 %copy-start = (bf16[1600,128]{1,0:T(8,128)(2,1)S(1)}, bf16[1600,128]{1,0:T(8,128)(2,1)}, u32[]{:S(2)}) copy-start(bf16[1600,128]{1,0:T(8,128)(2,1)} %get-tuple-element.65) | copy-start | bytes 1228804

commit v6 on v5

--- a/solution.py
+++ b/solution.py
@@ -307,6 +307,16 @@
         y = self.y if y is None else y
         return (2 * x + core, 4 * far + 2 * near + y)
 
+    def group_home(self):
+        x, core, far, near, y = self.x, self.core, self.far, self.near, self.y
+        new_x = (y + far + core) % 2
+        target = self.target(x=new_x, core=far, far=core, y=(x + core) % 2)
+        return target, 4 * far + 2 * near + new_x
+
+    def shard_home(self):
+        x, core, far, y = self.x, self.core, self.far, self.y
+        return self.target(x=(y + far) % 2, core=far, far=core, y=(x + core + far) % 2)
+
     def is_me(self, target):
         return jnp.logical_and(target[0] == self.fsdp, target[1] == self.ctx)
 
@@ -402,6 +412,14 @@
         self._go("b", 1, self.me, self.second)
         self._go("c", 2, self.me, self.other)
 
+    def begin_from(self, own):
+        for name, index, target in (
+            ("a", 0, self.first), ("b", 1, self.second), ("c", 2, self.other),
+        ):
+            item = remote(own, self.out.at[self.me], self.sems, index, target)
+            item.start()
+            self.copies[name] = item
+
     def second_hop(self):
         self.copies["a"].wait_recv()
         self._go("d", 3, self.of_first, self.second)
@@ -423,15 +441,16 @@
 
 
 class Spread:
-    def __init__(self, place, at, sems, first):
+    def __init__(self, place, at, sems, first, source=None):
         p = place
         self.at, self.sems, self.first = at, sems, first
         self.mine, self.theirs = at(p.far, p.y), at(1 - p.far, p.y)
+        self.source = self.mine if source is None else source
         self.to_far, self.to_y = p.target(far=1 - p.far), p.target(y=1 - p.y)
 
     def begin(self):
-        self.a = remote(self.mine, self.mine, self.sems, self.first, self.to_far)
-        self.b = remote(self.mine, self.mine, self.sems, self.first + 1, self.to_y)
+        self.a = remote(self.source, self.mine, self.sems, self.first, self.to_far)
+        self.b = remote(self.source, self.mine, self.sems, self.first + 1, self.to_y)
         self.a.start()
         self.b.start()
 
@@ -620,6 +639,14 @@
             target[lane : lane + 128, first : first + 128] = low(wide(part).T)
 
 
+def store_halves(target, block, value):
+    some = target.shape[2]
+    for place in range(2):
+        for half in range(2):
+            first = (2 * place + half) * some
+            target[half, block + place] = value[first : first + some]
+
+
 def half_of(blocks, core):
     return blocks.at[pl.ds(4 * core, 4)]
 
@@ -719,8 +746,9 @@
     w_heads, x_own, resid_own, h_second,
     x_all, w_qkv, h_first, qkv, w_fc, w_proj,
     flat, rows, qkv_pieces, fc_pieces, blocks, order, vec_all, qkv_land,
-    fc, proj, out, fc_part, proj_part, out_part, tail, next_tail, window, unit_rows, h_own,
-    branch, from_core, two, got, last, done, reduce_sem,
+    fc, proj, out, fc_part, fc_mine, proj_part, out_part, tail, next_tail, window, unit_rows, h_own,
+    branch, core_a, two_a, got_a, last_a, done_a, sem_a,
+    core_b, two_b, got_b, last_b, done_b, sem_b,
     order_pad, vec_pad, x_rows, back_rows, move_sem, qkv_sem, fc_send, fc_recv, rows_sem, x_sem, back_sem, spread_sem,
     own_sem, fc_sem, proj_sem, tree_sem, h_sem, store_sem,
 ):
@@ -745,9 +773,7 @@
     vec_pad[...] = jnp.zeros_like(vec_pad)
     vec_pad[: vec_in.shape[0], : vec_in.shape[1]] = vec_in[...]
     pl.semaphore_wait(barrier, DEVICES - 1)
-    home = p.target(
-        x=p.ctx % 2, near=p.ctx // 2 % 2, core=p.ctx // 4, y=p.fsdp // 2, far=p.fsdp % 2
-    )
+    home, home_member = p.group_home()
     owner = p.fsdp == 0
     qkv_moves = []
     for pair in range(pairs):
@@ -765,7 +791,7 @@
                 )
             )
     turn(x_in[...], x_rows)
-    x_move = Move(p, x_rows, x_all.at[p.ctx], move_sem.at[0, 0], move_sem.at[1, 0], home)
+    x_move = Move(p, x_rows, x_all.at[home_member], move_sem.at[0, 0], move_sem.at[1, 0], home)
     order_move = Move(p, order_pad, order, move_sem.at[0, 1], move_sem.at[1, 1], home)
     turn(back_in[...], back_rows)
 
@@ -853,7 +879,7 @@
             )
         )
     gather_x.last_hop()
-    back_move = Move(p, back_rows, back_all.at[p.ctx], move_sem.at[0, 3], move_sem.at[1, 3], home)
+    back_move = Move(p, back_rows, back_all.at[home_member], move_sem.at[0, 3], move_sem.at[1, 3], home)
     arrived(vec_all, move_sem.at[1, 2])
     cols = vec_pad.shape[-1]
     used = width // MEMBERS
@@ -871,12 +897,19 @@
     slots = order[0:1, :].astype(jnp.float32)
     lane = lax.broadcasted_iota(jnp.int32, (length, 128), 1)
     row = lax.broadcasted_iota(jnp.int32, (length, 128), 0)
-    spot = jnp.where(lane == row // BLOCK, slots, 0.0)
+    each = count // BLOCK
+
+    def slot_of(row):
+        member = row // count
+        turned = (member % 2 + member // 4 + p.far) % 2
+        return each * (member - member % 2 + turned) + row // BLOCK % each
+
+    spot = jnp.where(lane == slot_of(row), slots, 0.0)
     inner = lax.broadcasted_iota(jnp.int32, (length, 1), 0) % BLOCK
     row_pos[...] = jnp.sum(spot, 1, keepdims=True) * BLOCK + inner.astype(jnp.float32)
     lane = lax.broadcasted_iota(jnp.int32, (128, length), 1)
     row = lax.broadcasted_iota(jnp.int32, (128, length), 0)
-    spot = jnp.where(row == lane // BLOCK, 1.0, 0.0)
+    spot = jnp.where(row == slot_of(lane), 1.0, 0.0)
     inner = lax.broadcasted_iota(jnp.int32, (1, length), 1) % BLOCK
     found = jnp.dot(
         order[...].astype(jnp.bfloat16), spot.astype(jnp.bfloat16),
@@ -885,26 +918,6 @@
     col_pos[...] = found[0:1, :] * BLOCK + inner.astype(jnp.float32)
     for item in spreads[:2]:
         item.middle()
-    arrived(back_all.at[p.me], move_sem.at[1, 3])
-    gather_back = Gather(p, back_all, back_sem, True)
-    gather_back.begin()
-    gather_x.finish()
-
-    def norm_block(step, carry):
-        value = norm_rows(x_all[step].astype(jnp.float32), vecs[0:1, :], vecs[1:2, :])
-        h_first[pl.ds(pl.multiple_of(step * count, count), count), :] = value.astype(jnp.bfloat16)
-        return carry
-
-    lax.fori_loop(0, MEMBERS, norm_block, 0)
-    x_own[...] = x_all[p.me]
-    stores = []
-
-    def store(source, target):
-        copy = pltpu.make_async_copy(source, target, store_sem.at[len(stores)])
-        copy.start()
-        stores.append(copy)
-
-    store(h_first, h_first_out)
     to_far, to_y = p.target(far=1 - p.far), p.target(y=1 - p.y)
     same_y = p.y == out_root(p.me)
     root = jnp.logical_and(same_y, p.far == 0)
@@ -921,26 +934,23 @@
         out_y.start()
         out_own.start()
 
-    fc_far, fc_y, fc_later, own_copies = [], [], [], []
-    for slot in range(8):
-        arrived(fc_part.at[slot], fc_recv.at[slot])
-        landing = fc.at[fc_unit(p.far, p.y, slot)]
-        fc_far.append(remote(fc_part.at[slot], landing, fc_sem, slot, to_far))
-        fc_far[slot].start()
-        fc_y.append(remote(fc_part.at[slot], landing, fc_sem, 8 + slot, to_y))
-        fc_y[slot].start()
-        own_copies.append(pltpu.make_async_copy(fc_part.at[slot], landing, own_sem.at[slot]))
-        own_copies[slot].start()
-    gather_back.second_hop()
-    gather_back.third_hop()
-    arrived(proj_part, rows_sem.at[1, 0])
-    my_proj, far_proj = proj.at[p.y, p.far], proj.at[p.y, 1 - p.far]
-    proj_far = remote(proj_part, my_proj, proj_sem, 0, to_far)
-    proj_y = remote(proj_part, my_proj, proj_sem, 1, to_y)
-    proj_far.start()
-    proj_y.start()
-    proj_own = pltpu.make_async_copy(proj_part, my_proj, own_sem.at[9])
-    proj_own.start()
+    gather_x.finish()
+
+    def norm_block(step, carry):
+        value = norm_rows(x_all[step].astype(jnp.float32), vecs[0:1, :], vecs[1:2, :])
+        h_first[pl.ds(pl.multiple_of(step * count, count), count), :] = value.astype(jnp.bfloat16)
+        return carry
+
+    lax.fori_loop(0, MEMBERS, norm_block, 0)
+    x_own[...] = x_all[p.me]
+    stores = []
+
+    def store(source, target):
+        copy = pltpu.make_async_copy(source, target, store_sem.at[len(stores)])
+        copy.start()
+        stores.append(copy)
+
+    store(h_first, h_first_out)
     four = qkv_land.shape[4]
     per_part = SLOTS * HD
     bias_q = member_lanes(vecs[2:3, :], p.me, per_part)
@@ -973,7 +983,26 @@
     project(0)
     for item in spreads[2:]:
         item.middle()
-    gather_back.last_hop()
+
+    @pl.when(beside)
+    def _():
+        out_far.wait_recv()
+        out_later.start()
+
+    arrived(back_all.at[p.me], move_sem.at[1, 3])
+    gather_back = Gather(p, back_all, back_sem, True)
+    gather_back.begin()
+    fc_spreads = []
+    unit = fc_part.shape[1]
+    for half in range(2):
+        for slot in range(4):
+            arrived(fc_part.at[4 * half + slot], fc_recv.at[4 * half + slot])
+            fc_mine[half, unit * slot : unit * slot + unit, :] = fc_part[4 * half + slot]
+        item = Spread(
+            p, lambda far, y, half=half: fc.at[far, y, half], fc_sem, 3 * half, fc_mine.at[half]
+        )
+        item.begin()
+        fc_spreads.append(item)
     span = 2 * count
 
     def one_pair(pair):
@@ -992,21 +1021,23 @@
 
     one_pair(0)
     project(1)
+    gather_back.second_hop()
+    gather_back.third_hop()
+    arrived(proj_part, rows_sem.at[1, 0])
+    my_proj, far_proj = proj.at[p.y, p.far], proj.at[p.y, 1 - p.far]
+    proj_far = remote(proj_part, my_proj, proj_sem, 0, to_far)
+    proj_y = remote(proj_part, my_proj, proj_sem, 1, to_y)
+    proj_far.start()
+    proj_y.start()
+    proj_own = pltpu.make_async_copy(proj_part, my_proj, own_sem.at[9])
+    proj_own.start()
     store(w_qkv, w_qkv_out)
     store(qkv, qkv_out)
 
-    @pl.when(beside)
-    def _():
-        out_far.wait_recv()
-        out_later.start()
-
-    for slot in range(8):
-        fc_far[slot].wait_recv()
-        landing = fc.at[fc_unit(1 - p.far, p.y, slot)]
-        copy = remote(landing, landing, fc_sem, 16 + slot, to_y)
-        copy.start()
-        fc_later.append(copy)
+    for item in fc_spreads:
+        item.middle()
     one_pair(1)
+    gather_back.last_hop()
 
     @pl.when(root)
     def _():
@@ -1038,57 +1069,76 @@
         at = pl.ds(pl.multiple_of(step * span, span), span)
         heads = jnp.concatenate([attn[pair, at, :] for pair in range(pairs)], 1)
         value = low(jnp.dot(heads, unit_rows[...], preferred_element_type=jnp.float32))
-        branch[2 * step] = value[:count]
-        branch[2 * step + 1] = value[count:]
+        store_halves(branch, 2 * step, value)
         return carry
 
     lax.fori_loop(0, length // span, one_branch, 0)
-    reduce = Reduce(
-        p, half_of(branch, 1 - p.core), half_of(branch, p.core), from_core, two, got, last, done,
-        reduce_sem,
-    )
-    reduce.begin()
+    reduces = [
+        Reduce(
+            p, half_of(branch.at[half], 1 - p.core), half_of(branch.at[half], p.core), *buffers
+        )
+        for half, buffers in enumerate(
+            (
+                (core_a, two_a, got_a, last_a, done_a, sem_a),
+                (core_b, two_b, got_b, last_b, done_b, sem_b),
+            )
+        )
+    ]
+    for item in reduces:
+        item.begin()
     proj_far.wait_recv()
     proj_later = remote(far_proj, far_proj, proj_sem, 2, to_y)
     proj_later.start()
-    reduce.second()
-    reduce.third()
-    for item in fc_y + fc_later:
-        item.wait_recv()
-    for item in own_copies:
-        item.wait()
-    value = wide(x_own[...]) + reduce.result() + vecs[17:18, :]
-    resid_own[...] = value
-    h_own[...] = low(norm_rows(value, vecs[18:19, :], vecs[32:33, :]))
-    gather_h = Gather(p, h_second, h_sem)
-    for name, index, target in (
-        ("a", 0, gather_h.first), ("b", 1, gather_h.second), ("c", 2, gather_h.other),
-    ):
-        copy = remote(h_own, h_second.at[p.me], h_sem, index, target)
-        copy.start()
-        gather_h.copies[name] = copy
-    store(h_own, h_second.at[p.me])
-    unit = fc.shape[1]
-    for block in range(DEVICES):
-        w_fc[unit * block : unit * block + unit, :] = fc[block]
+    for item in reduces:
+        item.second()
+    for item in reduces:
+        item.third()
+    for item in fc_spreads:
+        item.finish()
+    gathers = []
+    some = count // 2
+    for half, item in enumerate(reduces):
+        at = slice(some * half, some * half + some)
+        value = wide(x_own[at, :]) + item.result() + vecs[17:18, :]
+        resid_own[at, :] = value
+        h_own[half] = low(norm_rows(value, vecs[18:19, :], vecs[32:33, :]))
+        gather = Gather(p, h_second.at[half], h_sem.at[half])
+        gather.begin_from(h_own.at[half])
+        gathers.append(gather)
+        store(h_own.at[half], h_second.at[half, p.me])
+    for group, units in enumerate(FC_OF_GROUP):
+        far, y = group // 2, group % 2
+        for half in range(2):
+            inside = jnp.logical_and(p.far == far, p.y == y)
+
+            @pl.when(inside)
+            def _(far=far, y=y, half=half):
+                fc[far, y, half] = fc_mine[half]
+
+            for slot in range(4):
+                first = unit * units[4 * half + slot]
+                w_fc[first : first + unit, :] = fc[far, y, half, unit * slot : unit * slot + unit]
     store(w_fc, w_fc_out)
-    gather_h.second_hop()
-    gather_h.third_hop()
+    for item in gathers:
+        item.second_hop()
+        item.third_hop()
     proj_y.wait_recv()
     proj_later.wait_recv()
     proj_own.wait()
     for group in range(GROUPS):
         w_proj[four * group : four * group + four, :] = proj[group // 2, group % 2]
     store(w_proj, w_proj_out)
-    gather_h.last_hop()
+    for item in gathers:
+        item.last_hop()
     send_tail.wait_recv()
     window[:reach, :] = wide(next_tail[...])
     w_heads[...] = low(window[pl.ds(pl.multiple_of(reach - begin, 8), span_rows), :])
-    for item in (gather_h, gather_back):
+    for item in gathers + [gather_back]:
         item.finish()
-    for item in fc_far + fc_y + fc_later + [proj_far, proj_y, proj_later, send_tail]:
+    for item in [proj_far, proj_y, proj_later, send_tail]:
         item.wait_send()
-    reduce.sent()
+    for item in reduces:
+        item.sent()
 
     @pl.when(root)
     def _():
@@ -1136,7 +1186,7 @@
             like(SLOTS * HD, width),
             like(rows, width),
             like(rows, width, dtype=high),
-            like(MEMBERS, rows, width),
+            like(2, MEMBERS, rows // 2, width),
         ],
         in_specs=[vmem] * 5,
         out_specs=[any_space] + [vmem] * 3 + [any_space] * 3 + [vmem] + [any_space] * 2
@@ -1156,20 +1206,22 @@
             pltpu.VMEM((128, 128), order.dtype),
             pltpu.VMEM((DEVICES, 16, vec_cols), kind),
             pltpu.VMEM((pairs, 2, 2, 2, four, cols // pairs), kind),
-            pltpu.VMEM((DEVICES, unit, hidden), kind),
+            pltpu.VMEM((2, 2, 2, four, hidden), kind),
             pltpu.VMEM((2, 2, four, width), kind),
             pltpu.VMEM((four, width), kind),
             pltpu.VMEM((8, unit, hidden), kind),
+            pltpu.VMEM((2, four, hidden), kind),
             pltpu.VMEM((four, width), kind),
             pltpu.VMEM((four, width), kind),
             pltpu.VMEM((64, width), kind),
             pltpu.VMEM((64, width), kind),
             pltpu.VMEM((64 + SLOTS * HD, width), high),
             pltpu.VMEM((SLOTS * HD, width), kind),
-            pltpu.VMEM((rows, width), kind),
-            pltpu.VMEM((MEMBERS, rows, width), kind),
+            pltpu.VMEM((2, rows // 2, width), kind),
+            pltpu.VMEM((2, MEMBERS, rows // 2, width), kind),
         ]
-        + reduce_buffers(rows, width)
+        + reduce_buffers(rows // 2, width)
+        + reduce_buffers(rows // 2, width)
         + [
             pltpu.VMEM((128, 128), order.dtype),
             pltpu.VMEM((16, vec_cols), kind),
@@ -1184,11 +1236,11 @@
             dma((2, 7)),
             dma((2, 12)),
             dma((9 + 1,)),
-            dma((2, 24)),
+            dma((2, 6)),
             dma((2, 3)),
             dma((2, 4)),
-            dma((2, 7)),
-            dma((6,)),
+            dma((2, 2, 7)),
+            dma((7,)),
         ],
         compiler_params=pltpu.CompilerParams(
             collective_id=1, has_side_effects=True, vmem_limit_bytes=VMEM_BYTES
@@ -1201,23 +1253,29 @@
 GELU_CUBE = 0.044715
 
 
-def store_rows(target, first, value, lanes=slice(None), at=None):
+def store_rows(target, first, value, lanes=slice(None), at=None, unit=None):
     places = at
-    size = target.shape[1]
+    size = target.shape[1] if unit is None else unit
     row = 0
     while row < value.shape[0]:
         block, at = divmod(first + row, size)
         count = min(size - at, value.shape[0] - row)
-        block = block if places is None else places[block]
-        target[block, at : at + count, lanes] = low(value[row : row + count])
+        if places is None:
+            target[block, at : at + count, lanes] = low(value[row : row + count])
+        else:
+            four = target.shape[1]
+            block, place = divmod(size * places[block], four)
+            at = at + place
+            target[block, at : at + count, lanes] = low(value[row : row + count])
         row += count
 
 
 def middle_kernel(
     h_in, back_all, vecs, resid_own, w_fc_in, w_proj_in,
-    grad_fc, grad_proj, proj_go, made, dresid, branch_all, sums, fc_sums,
+    grad_fc, proj_sum, made, dresid, branch_all, sums, fc_sums,
     h_second, back, w_fc, w_proj, act, dpre, dh_part, made_part, g_fc, g_proj,
-    proj_y, from_core, two, got, last, done, reduce_sem,
+    proj_y, proj_go, proj_far, core_a, two_a, got_a, last_a, done_a, sem_a,
+    core_b, two_b, got_b, last_b, done_b, sem_b,
     load_sem, store_sem, fold_sem,
     dbranch, branch_sem,
 ):
@@ -1226,18 +1284,34 @@
     count = length // MEMBERS
     hidden = act.shape[1]
     loads = []
-    for index, (source, target) in enumerate(
-        (
-            (h_in, h_second), (w_fc_in, w_fc), (back_all, back), (w_proj_in, w_proj),
-        )
-    ):
-        copy = pltpu.make_async_copy(source, target, load_sem.at[index])
+
+    def load(source, target):
+        copy = pltpu.make_async_copy(source, target, load_sem.at[len(loads)])
         copy.start()
         loads.append(copy)
-    reduce = Reduce(p, half_of(dh_part, 1 - p.core), half_of(dh_part, p.core), from_core, two, got, last, done, reduce_sem)
-    route = reduce.route
-    to_y = p.target(y=1 - p.y)
-    greet((route.first, route.second, route.other, to_y))
+
+    some = count // 2
+    for member in range(MEMBERS):
+        for half in range(2):
+            first = count * member + some * half
+            load(h_in.at[half, member], h_second.at[pl.ds(first, some)])
+    load(w_fc_in, w_fc)
+    load(back_all, back)
+    load(w_proj_in, w_proj)
+    reduces = [
+        Reduce(
+            p, half_of(dh_part.at[half], 1 - p.core), half_of(dh_part.at[half], p.core), *buffers
+        )
+        for half, buffers in enumerate(
+            (
+                (core_a, two_a, got_a, last_a, done_a, sem_a),
+                (core_b, two_b, got_b, last_b, done_b, sem_b),
+            )
+        )
+    ]
+    route = reduces[0].route
+    to_far, to_y = p.target(far=1 - p.far), p.target(y=1 - p.y)
+    greet((route.first, route.second, route.other, to_far, to_y))
     bias_fc = jnp.zeros((1, hidden), jnp.float32)
     block = hidden // GROUPS
     for member in range(MEMBERS):
@@ -1266,12 +1340,12 @@
         dpre[at, :] = dpre_block
         fc_sums[...] += jnp.sum(wide(dpre_block), 0, keepdims=True)
         value = low(dot_nt(dpre_block, w_fc[...]))
-        dh_part[2 * step] = value[:count]
-        dh_part[2 * step + 1] = value[count:]
+        store_halves(dh_part, 2 * step, value)
         return carry
 
     lax.fori_loop(0, MEMBERS // 2, one_block, 0)
-    reduce.begin()
+    for item in reduces:
+        item.begin()
 
     def one_made(step, carry):
         at = pl.ds(pl.multiple_of(step * span, span), span)
@@ -1281,8 +1355,9 @@
         return carry
 
     lax.fori_loop(0, MEMBERS // 2, one_made, 0)
-    reduce.second()
-    stores = [pltpu.make_async_copy(made_part, made, store_sem.at[3])]
+    for item in reduces:
+        item.second()
+    stores = [pltpu.make_async_copy(made_part, made, store_sem.at[2])]
     stores[0].start()
     chunk = 256
 
@@ -1295,61 +1370,70 @@
     tail = slice(width // chunk * chunk, width)
     if width % chunk:
         store_rows(g_proj, 0, dot_tn(act[...], back[:, tail]), tail)
-    over_y = remote(
-        g_proj.at[2 * (1 - p.y) + 1 - p.far], proj_y, fold_sem, 0, to_y
-    )
-    over_y.start()
-    reduce.third()
-    stores.append(pltpu.make_async_copy(g_proj, grad_proj, store_sem.at[0]))
-    stores[-1].start()
+    fold = Fold(
+        p, lambda far: g_proj.at[2 * (1 - p.y) + far], lambda far: g_proj.at[2 * p.y + far],
+        lambda far: proj_y.at[far], proj_go, proj_far, fold_sem, 0,
+    )
+    fold.begin()
+    for item in reduces:
+        item.third()
     for first in range(0, width, chunk):
         size = min(chunk, width - first)
         store_rows(
-            g_fc, first, dot_tn(h_second[:, first : first + size], dpre[...]), at=FC_POSITION
-        )
-    stores.append(pltpu.make_async_copy(g_fc, grad_fc, store_sem.at[1]))
+            g_fc, first, dot_tn(h_second[:, first : first + size], dpre[...]), at=FC_POSITION,
+            unit=width // DEVICES,
+        )
+    fold.rest()
+    fold.middle()
+    stores.append(pltpu.make_async_copy(g_fc, grad_fc, store_sem.at[0]))
     stores[-1].start()
 
-    dh = reduce.result()
-    center = resid_own[...] - jnp.mean(resid_own[...], -1, keepdims=True)
-    scale = lax.rsqrt(jnp.mean(center * center, -1, keepdims=True) + epsilon_norm)
-    hat = center * scale
-    back_own = wide(back[pl.ds(pl.multiple_of(p.me * count, count), count), :])
-    scaled = dh * vecs[18:19, :]
-    inner = jnp.mean(scaled * hat, -1, keepdims=True)
-    value = back_own + (scaled - jnp.mean(scaled, -1, keepdims=True) - hat * inner) * scale
-    dresid[...] = value
-    branch = low(value)
-    dbranch[...] = branch
-    gather = Gather(p, branch_all, branch_sem)
-    for name, index, target in (
-        ("a", 0, gather.first), ("b", 1, gather.second), ("c", 2, gather.other),
-    ):
-        copy = remote(dbranch, branch_all.at[p.me], branch_sem, index, target)
+    gathers = []
+    sums[...] = jnp.zeros_like(sums)
+    for half, item in enumerate(reduces):
+        at = slice(some * half, some * half + some)
+        dh = item.result()
+        center = resid_own[at, :] - jnp.mean(resid_own[at, :], -1, keepdims=True)
+        scale = lax.rsqrt(jnp.mean(center * center, -1, keepdims=True) + epsilon_norm)
+        hat = center * scale
+        first = pl.multiple_of(p.me * count + some * half, some)
+        back_own = wide(back[pl.ds(first, some), :])
+        scaled = dh * vecs[18:19, :]
+        inner = jnp.mean(scaled * hat, -1, keepdims=True)
+        value = back_own + (scaled - jnp.mean(scaled, -1, keepdims=True) - hat * inner) * scale
+        dresid[at, :] = value
+        part = low(value)
+        dbranch[half] = part
+        gather = Gather(p, branch_all.at[half], branch_sem.at[half])
+        gather.begin_from(dbranch.at[half])
+        gathers.append(gather)
+        copy = pltpu.make_async_copy(
+            dbranch.at[half], branch_all.at[half, p.me], store_sem.at[1 + 2 * half]
+        )
         copy.start()
-        gather.copies[name] = copy
-    stores.append(pltpu.make_async_copy(dbranch, branch_all.at[p.me], store_sem.at[2]))
-    stores[-1].start()
-    sums[0:1, :] = jnp.sum(dh * hat, 0, keepdims=True)
-    sums[1:2, :] = jnp.sum(dh, 0, keepdims=True)
-    sums[2:3, :] = jnp.sum(wide(branch), 0, keepdims=True)
-    sums[3:4, :] = jnp.sum(back_own, 0, keepdims=True)
-    sums[4:8, :] = jnp.zeros((4, width), jnp.float32)
-    gather.second_hop()
-    gather.third_hop()
-    over_y.wait_recv()
-    proj_go[...] = low(wide(g_proj[2 * p.y + 1 - p.far]) + wide(proj_y[...]))
-    over_y.wait_send()
-    gather.last_hop()
-    gather.finish()
-    reduce.sent()
+        stores.append(copy)
+        sums[0:1, :] += jnp.sum(dh * hat, 0, keepdims=True)
+        sums[1:2, :] += jnp.sum(dh, 0, keepdims=True)
+        sums[2:3, :] += jnp.sum(wide(part), 0, keepdims=True)
+        sums[3:4, :] += jnp.sum(back_own, 0, keepdims=True)
+    for item in gathers:
+        item.second_hop()
+        item.third_hop()
+    for item in gathers:
+        item.last_hop()
+    proj_sum[...] = fold.end()
+    for item in gathers:
+        item.finish()
+    fold.sent()
+    for item in reduces:
+        item.sent()
     for copy in stores:
         copy.wait()
 
 
 def middle(h_second, back_all, vecs, resid_own, w_fc, w_proj):
     kind, high = jnp.bfloat16, jnp.float32
-    length, width = h_second.shape
+    length, width = back_all.shape
     rows = length // MEMBERS
     hidden = w_proj.shape[0]
     four = width // MEMBERS
@@ -1366,32 +1450,37 @@
     return pl.pallas_call(
         middle_kernel,
         out_shape=[
-            like(DEVICES, four // 4, hidden),
-            like(GROUPS, four, width),
+            like(MEMBERS, four, hidden),
             like(four, width),
             like(MEMBERS, rows, width),
             like(rows, width, dtype=high),
-            like(MEMBERS, rows, width),
+            like(2, MEMBERS, rows // 2, width),
             like(8, width, dtype=high),
             like(1, hidden, dtype=high),
         ],
         in_specs=[any_space] * 2 + [vmem] * 2 + [any_space] * 2,
-        out_specs=[any_space] * 2 + [vmem, any_space, vmem, any_space] + [vmem] * 2,
+        out_specs=[any_space, vmem, any_space, vmem, any_space] + [vmem] * 2,
         scratch_shapes=[
-            buffer(*h_second.shape),
+            buffer(length, width),
             buffer(*back_all.shape),
             buffer(*w_fc.shape),
             buffer(*w_proj.shape),
             buffer(length, hidden),
             buffer(length, hidden),
+            buffer(2, MEMBERS, rows // 2, width),
             buffer(MEMBERS, rows, width),
-            buffer(MEMBERS, rows, width),
-            buffer(DEVICES, four // 4, hidden),
+            buffer(MEMBERS, four, hidden),
             buffer(GROUPS, four, width),
+            buffer(2, four, width),
+            buffer(four, width),
             buffer(four, width),
         ]
-        + reduce_buffers(rows, width)
-        + [dma((4,)), dma((4,)), dma((2, 1)), buffer(rows, width), dma((2, 7))],
+        + reduce_buffers(rows // 2, width)
+        + reduce_buffers(rows // 2, width)
+        + [
+            dma((2 * MEMBERS + 3,)), dma((4,)), dma((2, 3)), buffer(2, rows // 2, width),
+            dma((2, 2, 7)),
+        ],
         compiler_params=pltpu.CompilerParams(
             collective_id=3, has_side_effects=True, vmem_limit_bytes=VMEM_BYTES
         ),
@@ -1441,21 +1530,22 @@
 
 
 def backward_kernel(
-    branch_in, made_in, grad_fc, grad_proj, proj_go, attn, qkv, row_pos, col_pos, w_heads, w_qkv_in,
+    branch_in, made_in, grad_fc, proj_sum, attn, qkv, row_pos, col_pos, w_heads, w_qkv_in,
     h_in, x_own, resid_own, dresid, vecs, sums, fc_sums,
     out_home, grad_home, qkv_back, fc_back, rows_back, vec_back,
     branch_all, dattn, dqkv, key_sum, value_sum, w_qkv, h_first, dh_part, made, result,
-    fc_own, proj_own, g_qkv, g_heads, g_out, input_grad, vec_rows, vec_go, vec_got,
-    fc_y, proj_y, qkv_y, out_y, fc_go, qkv_go, out_go,
-    fc_far, proj_far, qkv_far, out_far, fc_sum, proj_sum, qkv_sum, out_sum,
+    fc_own, g_qkv, g_heads, g_out, input_grad, vec_rows, vec_go, vec_got,
+    fc_y, qkv_y, out_y, fc_go, qkv_go, out_go,
+    fc_far, qkv_far, out_far, fc_sum, qkv_sum, out_sum,
     core_a, two_a, got_a, last_a, done_a, sem_a, core_b, two_b, got_b, last_b, done_b, sem_b,
     load_sem, fold_sem, tree_sem, vec_sem, home_sem,
     qkv_send, qkv_recv, fc_send, fc_recv, rows_send, rows_recv,
 ):
     p = Place()
-    _, count, width = branch_in.shape
+    _, _, some, width = branch_in.shape
+    count = 2 * some
     length = MEMBERS * count
-    four = grad_proj.shape[1]
+    four = proj_sum.shape[0]
     pairs = SLOTS // 2
     loads = []
 
@@ -1464,19 +1554,16 @@
         copy.start()
         loads.append(copy)
 
-    load(branch_in, branch_all)
+    for member in range(MEMBERS):
+        for half in range(2):
+            load(branch_in.at[half, member], branch_all.at[member, pl.ds(some * half, some)])
     load(half_of(made_in, p.core), made)
-    load(grad_proj.at[2 * p.y + p.far], proj_own)
     for far in range(2):
         for near in range(2):
             load(grad_fc.at[far, p.y, near], fc_own.at[far, near])
     load(w_qkv_in, w_qkv)
     load(h_in, h_first)
     greet_all(p)
-    proj_over_y = remote(
-        grad_proj.at[2 * (1 - p.y) + p.far], proj_y, fold_sem, 0, p.target(y=1 - p.y)
-    )
-    proj_over_far = remote(proj_go, proj_far, fold_sem, 1, p.target(far=1 - p.far))
     fc_folds = [
         Fold(
             p, lambda far, near=near: grad_fc.at[far, 1 - p.y, near],
@@ -1499,12 +1586,14 @@
         p, half_of(made_in, 1 - p.core), made, core_a, two_a, got_a, last_a, done_a, sem_a
     )
     reduce_made.begin()
-    proj_over_far.start()
+    target, part = shard_of(PROJ_FIRST + lookup(PROJ_UNIT, p.linear))
+    moves = [
+        Move(p, proj_sum, rows_back.at[part], rows_send.at[0], rows_recv.at[part], target)
+    ]
     for item in fc_folds:
         item.begin()
     for copy in loads:
         copy.wait()
-    proj_over_y.start()
     span = 2 * count
 
     def one_dattn(step, carry):
@@ -1593,19 +1682,10 @@
         done_b, sem_b, True,
     )
     reduce_dh.begin()
-    home = p.target(
-        x=p.ctx % 2, near=p.ctx // 2 % 2, core=p.ctx // 4, y=p.fsdp // 2, far=p.fsdp % 2
-    )
+    home = p.shard_home()
     turn(low(resid_own[...] + reduce_made.result() + vecs[33:34, :]), result)
-    moves = [Move(p, result, out_home, home_sem.at[0, 0], home_sem.at[1, 0], home)]
+    moves.append(Move(p, result, out_home, home_sem.at[0, 0], home_sem.at[1, 0], home))
     reduce_dh.second()
-    proj_over_y.wait_recv()
-    proj_over_far.wait_recv()
-    proj_sum[...] = low(wide(proj_own[...]) + wide(proj_y[...]) + wide(proj_far[...]))
-    target, part = shard_of(PROJ_FIRST + lookup(PROJ_UNIT, p.linear))
-    moves.append(
-        Move(p, proj_sum, rows_back.at[part], rows_send.at[0], rows_recv.at[part], target)
-    )
     for pair in range(pairs):
         total = 0.0
         for block in range(MEMBERS):
@@ -1626,8 +1706,10 @@
 
     reduce_dh.third()
     for near in range(2):
-        fc_sum[near] = fc_folds[near].end()
+        block = fc_folds[near].end()
+        unit = fc_sum.shape[2]
         for slot in range(4):
+            fc_sum[near, slot] = block[unit * slot : unit * slot + unit]
             target, part = shard_of(FC_FIRST + fc_unit(p.far, p.y, 4 * near + slot))
             moves.append(
                 Move(
@@ -1761,8 +1843,6 @@
     arrived(vec_got.at[pl.ds(1, DEVICES - 1)], vec_sem.at[0])
     for item in [reduce_made, reduce_dh] + fc_folds + qkv_folds + moves:
         item.sent()
-    proj_over_y.wait_send()
-    proj_over_far.wait_send()
 
     @pl.when(jnp.logical_not(same_y))
     def _():
@@ -1774,11 +1854,11 @@
 
 
 def backward(
-    branch_all, made, grad_fc, grad_proj, proj_go, attn, qkv, row_pos, col_pos, w_heads, w_qkv,
+    branch_all, made, grad_fc, proj_sum, attn, qkv, row_pos, col_pos, w_heads, w_qkv,
     h_first, x_own, resid_own, dresid, vecs, sums, fc_sums,
 ):
     kind, high = jnp.bfloat16, jnp.float32
-    _, rows, width = branch_all.shape
+    rows, width = x_own.shape
     length = MEMBERS * rows
     four, cols = width // MEMBERS, qkv.shape[1]
     unit, hidden = four // 4, fc_sums.shape[1]
@@ -1804,7 +1884,7 @@
             like(3, four, width),
             like(8, used, dtype=high),
         ],
-        in_specs=[any_space] * 4 + [vmem] * 6 + [any_space] * 2 + [vmem] * 6,
+        in_specs=[any_space] * 3 + [vmem] * 6 + [any_space] * 2 + [vmem] * 6,
         out_specs=[any_space] * 5 + [vmem],
         scratch_shapes=[
             buffer(MEMBERS, rows, width),
@@ -1817,8 +1897,7 @@
             buffer(MEMBERS, rows, width),
             buffer(MEMBERS // 2, rows, width),
             buffer(width, rows),
-            buffer(2, 2, 4, unit, hidden),
-            buffer(four, width),
+            buffer(2, 2, four, hidden),
             buffer(2, MEMBERS, four, cols // 2),
             buffer(per_part, width, dtype=high),
             buffer(four, width),
@@ -1828,19 +1907,20 @@
             buffer(DEVICES, 8, used, dtype=high),
         ]
         + [
-            buffer(2, 2, 4, unit, hidden), buffer(four, width),
+            buffer(2, 2, four, hidden),
             buffer(2, 2, 2, four, cols // 2), buffer(four, width),
+            buffer(2, four, hidden), buffer(2, 2, four, cols // 2), buffer(four, width),
+        ]
+        + [
+            buffer(2, four, hidden), buffer(2, 2, four, cols // 2), buffer(four, width),
+        ]
+        + [
             buffer(2, 4, unit, hidden), buffer(2, 2, four, cols // 2), buffer(four, width),
         ]
-        + [
-            buffer(2, 4, unit, hidden), buffer(four, width), buffer(2, 2, four, cols // 2),
-            buffer(four, width),
-        ]
-        * 2
         + reduce_buffers(rows, width)
         + reduce_buffers(rows, width)
         + [
-            dma((12,)),
+            dma((2 * MEMBERS + 8,)),
             dma((2, 15)),
             dma((2, 2)),
             dma((2,)),
@@ -1857,7 +1937,7 @@
         ),
         name="backward",
     )(
-        branch_all, made, grad_fc, grad_proj, proj_go, attn, qkv, row_pos, col_pos, w_heads, w_qkv,
+        branch_all, made, grad_fc, proj_sum, attn, qkv, row_pos, col_pos, w_heads, w_qkv,
         h_first, x_own, resid_own, dresid, vecs, sums, fc_sums,
     )
 
@@ -2058,14 +2138,14 @@
     ) = forward(
         inputs[0].T, cotangent[0].T, slot_order, vectors, weights
     )
-    grad_fc, grad_proj, proj_go, made, dresid, branch_all, sums, fc_sums = middle(
-        h_second.reshape(length, width), back_all.reshape(length, width), vecs, resid_own,
+    grad_fc, proj_sum, made, dresid, branch_all, sums, fc_sums = middle(
+        h_second, back_all.reshape(length, width), vecs, resid_own,
         own_fc, own_proj,
     )
     out_home, grad_home, qkv_back, fc_back, rows_back, vec_back = backward(
-        branch_all, made, grad_fc.reshape((2, 2, 2, 4) + grad_fc.shape[1:]), grad_proj, proj_go,
-        attn, qkv, row_pos, col_pos, w_heads, own_qkv, h_first, x_own, resid_own, dresid, vecs,
-        sums, fc_sums,
+        branch_all, made, grad_fc.reshape((2, 2, 2) + grad_fc.shape[1:]), proj_sum, attn, qkv,
+        row_pos, col_pos, w_heads, own_qkv, h_first, x_own, resid_own, dresid, vecs, sums,
+        fc_sums,
     )
     new = update(
         qkv_back, fc_back, rows_back, vec_back, vectors, first_vec, second_vec, weights,

time: 447 us -> 429 us (0.960)
  the two profiles are of different devices: /device:TPU:4 before, /device:TPU:0 now
where the time goes in v6:
time: 429 us; the launch traced here: 424 us
  Pallas kernels  422 us (98%)
    pallas_call x1, Pallas kernels, forward(): pl.pallas_call(forward_kernel, out_shape=[like(MEMBERS, rows, width), lik...  189 us
    pallas_call x1, Pallas kernels, backward(): pl.pallas_call(backward_kernel, out_shape=[like(width, rows), like(width,...  139 us
    pallas_call x1, Pallas kernels, middle(): pl.pallas_call(middle_kernel, out_shape=[like(MEMBERS, four, hidden), lik...  77.5 us
    pallas_call x1, Pallas kernels, update(): pl.pallas_call(update_kernel, grid=(steps,), in_specs=[any_space] * 3 + [...  16.2 us

profile of v6, /device:TPU:0, one launch (start us, length us, event | category | flops | bytes accessed | tf_op | source)
XLA Modules:
  0.0 424.0 jit_solution(1626089093244314449)
XLA Ops:
  0.6 188.9 %forward.1 = (bf16[8,128,1600]{2,1,0:T(8,128)(2,1)}, f32[64,1600]{1,0:T(8,128)}, f32[1024,1]{1,0:T(8,128)}, f32[1,1024]{1,0:T(1,128)}, bf16[1600,768]{1,0:T(8,12...) custom-call(bf16[1600,128]{1,0:T(8,128)(2,1)} %bitcast.18, ...), custom_call_target="tpu_custom_call" | custom-call | tf_op jit(solution)/shard_map/forward/pallas_call | solution.py:1173
  189.5 77.5 %middle.1 = (bf16[8,200,800]{2,1,0:T(8,128)(2,1)}, bf16[200,1600]{1,0:T(8,128)(2,1)}, bf16[8,128,1600]{2,1,0:T(8,128)(2,1)}, f32[128,1600]{1,0:T(8,128)}, bf16[2...) custom-call(bf16[2,8,64,1600]{3,2,1,0:T(8,128)(2,1)} %get-tuple-element.41.h_in, ...), custom_call_target="tpu_custom_call" | custom-call | tf_op jit(solution)/shard_map/middle/pallas_call | solution.py:1450
  267.0 138.9 %backward.1 = (bf16[1600,128]{1,0:T(8,128)(2,1)}, bf16[1600,128]{1,0:T(8,128)(2,1)}, bf16[8,2,200,384]{3,2,1,0:T(8,128)(2,1)}, bf16[3,8,50,800]{3,2,1,0:T(8,128)...) custom-call(bf16[2,8,64,1600]{3,2,1,0:T(8,128)(2,1)} %get-tuple-element.47.branch_in, ...), custom_call_target="tpu_custom_call" | custom-call | tf_op jit(solution)/shard_map/backward/pallas_call | solution.py:1877
  406.0 0.0 copy-start.1
  406.0 0.0 copy-start
  406.0 16.2 %update.1 = (f32[3,200]{1,0:T(4,128)}, f32[3,200]{1,0:T(4,128)}, f32[3,200]{1,0:T(4,128)}, f32[7500,128]{1,0:T(8,128)}, f32[7500,128]{1,0:T(8,128)}, /*index=5*/f32[7500,128]{1,0:T(8,128)}) custom-call(bf16[8,2,200,384]{3,2,1,0:T(8,128)(2,1)} %get-tuple-element.64.qkv_in, bf16[3,8,50,800]{3,2,1,0:T(8,128)(2,1)} %get-tuple-element.65.fc_in, ...), custom_call_target="tpu_custom_call" | custom-call | tf_op jit(solution)/shard_map/update/pallas_call | solution.py:2108
  422.2 0.0 copy-done.1
  422.3 0.8 copy.19
  423.0 0.0 copy-done
  423.0 0.8 copy.20
Async XLA Ops:
  406.0 16.3 %copy-start.1 = (bf16[1600,128]{1,0:T(8,128)(2,1)S(1)}, bf16[1600,128]{1,0:T(8,128)(2,1)}, u32[]{:S(2)}) copy-start(bf16[1600,128]{1,0:T(8,128)(2,1)} %get-tuple-element.62) | copy-start | bytes 1228804
  406.0 17.0 %copy-start = (bf16[1600,128]{1,0:T(8,128)(2,1)S(1)}, bf16[1600,128]{1,0:T(8,128)(2,1)}, u32[]{:S(2)}) copy-start(bf16[1600,128]{1,0:T(8,128)(2,1)} %get-tuple-element.63) | copy-start | bytes 1228804

commit v7 on v6

--- a/solution.py
+++ b/solution.py
@@ -332,14 +332,20 @@
         return carry
 
     lax.fori_loop(1, DEVICES, one, 0)
-    pl.semaphore_wait(barrier, DEVICES - 1)
+
+
+def await_all():
+    pl.semaphore_wait(pltpu.get_barrier_semaphore(), DEVICES - 1)
 
 
 def greet(targets):
     barrier = pltpu.get_barrier_semaphore()
     for target in targets:
         pl.semaphore_signal(barrier, inc=1, device_id=target, device_id_type=MESH)
-    pl.semaphore_wait(barrier, len(targets))
+
+
+def await_greeted(count):
+    pl.semaphore_wait(pltpu.get_barrier_semaphore(), count)
 
 
 def remote(source, landing, sems, index, target):
@@ -1086,15 +1092,10 @@
     ]
     for item in reduces:
         item.begin()
-    proj_far.wait_recv()
-    proj_later = remote(far_proj, far_proj, proj_sem, 2, to_y)
-    proj_later.start()
     for item in reduces:
         item.second()
     for item in reduces:
         item.third()
-    for item in fc_spreads:
-        item.finish()
     gathers = []
     some = count // 2
     for half, item in enumerate(reduces):
@@ -1106,6 +1107,14 @@
         gather.begin_from(h_own.at[half])
         gathers.append(gather)
         store(h_own.at[half], h_second.at[half, p.me])
+    proj_far.wait_recv()
+    proj_later = remote(far_proj, far_proj, proj_sem, 2, to_y)
+    proj_later.start()
+    for item in gathers:
+        item.second_hop()
+        item.third_hop()
+    for item in fc_spreads:
+        item.finish()
     for group, units in enumerate(FC_OF_GROUP):
         far, y = group // 2, group % 2
         for half in range(2):
@@ -1119,9 +1128,6 @@
                 first = unit * units[4 * half + slot]
                 w_fc[first : first + unit, :] = fc[far, y, half, unit * slot : unit * slot + unit]
     store(w_fc, w_fc_out)
-    for item in gathers:
-        item.second_hop()
-        item.third_hop()
     proj_y.wait_recv()
     proj_later.wait_recv()
     proj_own.wait()
@@ -1344,6 +1350,7 @@
         return carry
 
     lax.fori_loop(0, MEMBERS // 2, one_block, 0)
+    await_greeted(5)
     for item in reduces:
         item.begin()
 
@@ -1538,6 +1545,7 @@
     fc_y, qkv_y, out_y, fc_go, qkv_go, out_go,
     fc_far, qkv_far, out_far, fc_sum, qkv_sum, out_sum,
     core_a, two_a, got_a, last_a, done_a, sem_a, core_b, two_b, got_b, last_b, done_b, sem_b,
+    core_c, two_c, got_c, last_c, done_c, sem_c,
     load_sem, fold_sem, tree_sem, vec_sem, home_sem,
     qkv_send, qkv_recv, fc_send, fc_recv, rows_send, rows_recv,
 ):
@@ -1564,6 +1572,27 @@
     load(w_qkv_in, w_qkv)
     load(h_in, h_first)
     greet_all(p)
+    for copy in loads[: 2 * MEMBERS]:
+        copy.wait()
+    span = 2 * count
+
+    def one_dattn(step, carry):
+        at = pl.ds(pl.multiple_of(step * span, span), span)
+        grad = jnp.concatenate([branch_all[2 * step], branch_all[2 * step + 1]], 0)
+        value = low(dot_nt(grad, w_heads[...]))
+        for pair in range(pairs):
+            dattn[pair, at, :] = value[:, 128 * pair : 128 * pair + 128]
+        return carry
+
+    lax.fori_loop(0, length // span, one_dattn, 0)
+    for pair in range(pairs):
+        total = 0.0
+        for block in range(MEMBERS):
+            at = slice(block * count, block * count + count)
+            total = total + dot_tn(attn[pair, at, :], branch_all[block])
+        g_heads[128 * pair : 128 * pair + 128, :] = total
+    g_out[...] = low(g_heads[pl.ds(pl.multiple_of(head_rows(p.me), 8), four), :])
+    await_all()
     fc_folds = [
         Fold(
             p, lambda far, near=near: grad_fc.at[far, 1 - p.y, near],
@@ -1592,19 +1621,8 @@
     ]
     for item in fc_folds:
         item.begin()
-    for copy in loads:
+    for copy in loads[2 * MEMBERS :]:
         copy.wait()
-    span = 2 * count
-
-    def one_dattn(step, carry):
-        at = pl.ds(pl.multiple_of(step * span, span), span)
-        grad = jnp.concatenate([branch_all[2 * step], branch_all[2 * step + 1]], 0)
-        value = low(dot_nt(grad, w_heads[...]))
-        for pair in range(pairs):
-            dattn[pair, at, :] = value[:, 128 * pair : 128 * pair + 128]
-        return carry
-
-    lax.fori_loop(0, length // span, one_dattn, 0)
     def one_pair(pair):
         key_sum[...] = jnp.zeros_like(key_sum)
         value_sum[...] = jnp.zeros_like(value_sum)
@@ -1672,27 +1690,29 @@
     def one_part(step, carry):
         at = pl.ds(pl.multiple_of(step * span, span), span)
         value = low(dot_nt(dqkv[at, :], w_qkv[...]))
-        dh_part[2 * step] = value[:count]
-        dh_part[2 * step + 1] = value[count:]
+        store_halves(dh_part, 2 * step, value)
         return carry
 
     lax.fori_loop(0, length // span, one_part, 0)
-    reduce_dh = Reduce(
-        p, half_of(dh_part, 1 - p.core), half_of(dh_part, p.core), core_b, two_b, got_b, last_b,
-        done_b, sem_b, True,
-    )
-    reduce_dh.begin()
+    reduces = [
+        Reduce(
+            p, half_of(dh_part.at[half], 1 - p.core), half_of(dh_part.at[half], p.core),
+            *buffers, True,
+        )
+        for half, buffers in enumerate(
+            (
+                (core_b, two_b, got_b, last_b, done_b, sem_b),
+                (core_c, two_c, got_c, last_c, done_c, sem_c),
+            )
+        )
+    ]
+    for item in reduces:
+        item.begin()
     home = p.shard_home()
     turn(low(resid_own[...] + reduce_made.result() + vecs[33:34, :]), result)
     moves.append(Move(p, result, out_home, home_sem.at[0, 0], home_sem.at[1, 0], home))
-    reduce_dh.second()
-    for pair in range(pairs):
-        total = 0.0
-        for block in range(MEMBERS):
-            at = slice(block * count, block * count + count)
-            total = total + dot_tn(attn[pair, at, :], branch_all[block])
-        g_heads[128 * pair : 128 * pair + 128, :] = total
-    g_out[...] = low(g_heads[pl.ds(pl.multiple_of(head_rows(p.me), 8), four), :])
+    for item in reduces:
+        item.second()
     root_y = out_root(p.me)
     same_y = p.y == root_y
     root = jnp.logical_and(same_y, p.far == 0)
@@ -1704,7 +1724,9 @@
     def _():
         over_y.start()
 
-    reduce_dh.third()
+    qkv_folds[1].middle()
+    for item in reduces:
+        item.third()
     for near in range(2):
         block = fc_folds[near].end()
         unit = fc_sum.shape[2]
@@ -1727,7 +1749,17 @@
         out_go[...] = low(wide(g_out[...]) + wide(out_y[...]))
         over_far.start()
 
-    dh = reduce_dh.result()
+    for pair in range(pairs):
+        qkv_sum[pair] = qkv_folds[pair].end()
+        for near in range(2):
+            target = (0 * p.fsdp, 4 * p.far + 2 * near + p.y)
+            moves.append(
+                Move(
+                    p, qkv_sum.at[pair, near], qkv_back.at[p.me, pair],
+                    qkv_send.at[pair, near], qkv_recv.at[p.me, pair], target,
+                )
+            )
+    dh = jnp.concatenate([item.result() for item in reduces], 0)
     x = wide(x_own[...])
     center = x - jnp.mean(x, -1, keepdims=True)
     scale = lax.rsqrt(jnp.mean(center * center, -1, keepdims=True) + epsilon_norm)
@@ -1795,7 +1827,6 @@
 
     lax.fori_loop(1, DEVICES, vec_send, 0)
     pltpu.make_async_copy(vec_go.at[p.linear], vec_got.at[p.linear], vec_sem.at[1]).start()
-    qkv_folds[1].middle()
     @pl.when(root)
     def _():
         over_far.wait_recv()
@@ -1805,16 +1836,6 @@
     moves.append(
         Move(p, out_sum, rows_back.at[part], rows_send.at[1], rows_recv.at[part], target, root)
     )
-    for pair in range(pairs):
-        qkv_sum[pair] = qkv_folds[pair].end()
-        for near in range(2):
-            target = (0 * p.fsdp, 4 * p.far + 2 * near + p.y)
-            moves.append(
-                Move(
-                    p, qkv_sum.at[pair, near], qkv_back.at[p.me, pair],
-                    qkv_send.at[pair, near], qkv_recv.at[p.me, pair], target,
-                )
-            )
     arrived(vec_got, vec_sem.at[1])
     vec_back[...] = jnp.sum(vec_got[...], 0)
 
@@ -1841,7 +1862,7 @@
     arrived(out_home, home_sem.at[1, 0])
     arrived(grad_home, home_sem.at[1, 1])
     arrived(vec_got.at[pl.ds(1, DEVICES - 1)], vec_sem.at[0])
-    for item in [reduce_made, reduce_dh] + fc_folds + qkv_folds + moves:
+    for item in [reduce_made] + reduces + fc_folds + qkv_folds + moves:
         item.sent()
 
     @pl.when(jnp.logical_not(same_y))
@@ -1894,7 +1915,7 @@
             buffer(length, 2 * HD, dtype=high),
             buffer(*w_qkv.shape),
             buffer(*h_first.shape),
-            buffer(MEMBERS, rows, width),
+            buffer(2, MEMBERS, rows // 2, width),
             buffer(MEMBERS // 2, rows, width),
             buffer(width, rows),
             buffer(2, 2, four, hidden),
@@ -1918,7 +1939,8 @@
             buffer(2, 4, unit, hidden), buffer(2, 2, four, cols // 2), buffer(four, width),
         ]
         + reduce_buffers(rows, width)
-        + reduce_buffers(rows, width)
+        + reduce_buffers(rows // 2, width)
+        + reduce_buffers(rows // 2, width)
         + [
             dma((2 * MEMBERS + 8,)),
             dma((2, 15)),
@@ -2097,7 +2119,7 @@
 ):
     high = jnp.float32
     local = weights.shape[0]
-    steps = 10
+    steps = 5
     size = -(-local // (16 * steps)) * 16
     block = pl.BlockSpec((size, 128), lambda i: (i, 0))
     any_space = pl.BlockSpec(memory_space=pl.ANY)

time: 429 us -> 428 us (level)
  the two profiles are of different devices: /device:TPU:0 before, /device:TPU:5 now
where the time goes in v7:
time: 428 us; the launch traced here: 423 us
  Pallas kernels  421 us (98%)
    pallas_call x1, Pallas kernels, forward(): pl.pallas_call(forward_kernel, out_shape=[like(MEMBERS, rows, width), lik...  186 us
    pallas_call x1, Pallas kernels, backward(): pl.pallas_call(backward_kernel, out_shape=[like(width, rows), like(width,...  141 us
    pallas_call x1, Pallas kernels, middle(): pl.pallas_call(middle_kernel, out_shape=[like(MEMBERS, four, hidden), lik...  78.3 us
    pallas_call x1, Pallas kernels, update(): pl.pallas_call(update_kernel, grid=(steps,), in_specs=[any_space] * 3 + [...  15 us

profile of v7, /device:TPU:5, one launch (start us, length us, event | category | flops | bytes accessed | tf_op | source)
XLA Modules:
  0.0 423.2 jit_solution(6068675349847075886)
XLA Ops:
  0.6 186.2 %forward.1 = (bf16[8,128,1600]{2,1,0:T(8,128)(2,1)}, f32[64,1600]{1,0:T(8,128)}, f32[1024,1]{1,0:T(8,128)}, f32[1,1024]{1,0:T(1,128)}, bf16[1600,768]{1,0:T(8,12...) custom-call(bf16[1600,128]{1,0:T(8,128)(2,1)} %bitcast.18, ...), custom_call_target="tpu_custom_call" | custom-call | tf_op jit(solution)/shard_map/forward/pallas_call | solution.py:1179
  186.9 78.3 %middle.1 = (bf16[8,200,800]{2,1,0:T(8,128)(2,1)}, bf16[200,1600]{1,0:T(8,128)(2,1)}, bf16[8,128,1600]{2,1,0:T(8,128)(2,1)}, f32[128,1600]{1,0:T(8,128)}, bf16[2...) custom-call(bf16[2,8,64,1600]{3,2,1,0:T(8,128)(2,1)} %get-tuple-element.41.h_in, ...), custom_call_target="tpu_custom_call" | custom-call | tf_op jit(solution)/shard_map/middle/pallas_call | solution.py:1457
  265.2 141.2 %backward.1 = (bf16[1600,128]{1,0:T(8,128)(2,1)}, bf16[1600,128]{1,0:T(8,128)(2,1)}, bf16[8,2,200,384]{3,2,1,0:T(8,128)(2,1)}, bf16[3,8,50,800]{3,2,1,0:T(8,128)...) custom-call(bf16[2,8,64,1600]{3,2,1,0:T(8,128)(2,1)} %get-tuple-element.47.branch_in, ...), custom_call_target="tpu_custom_call" | custom-call | tf_op jit(solution)/shard_map/backward/pallas_call | solution.py:1898
  406.4 0.0 copy-start.1
  406.4 0.0 copy-start
  406.4 15.0 %update.1 = (f32[3,200]{1,0:T(4,128)}, f32[3,200]{1,0:T(4,128)}, f32[3,200]{1,0:T(4,128)}, f32[7500,128]{1,0:T(8,128)}, f32[7500,128]{1,0:T(8,128)}, /*index=5*/f32[7500,128]{1,0:T(8,128)}) custom-call(bf16[8,2,200,384]{3,2,1,0:T(8,128)(2,1)} %get-tuple-element.64.qkv_in, bf16[3,8,50,800]{3,2,1,0:T(8,128)(2,1)} %get-tuple-element.65.fc_in, ...), custom_call_target="tpu_custom_call" | custom-call | tf_op jit(solution)/shard_map/update/pallas_call | solution.py:2130
  421.4 0.0 copy-done.1
  421.4 0.8 copy.19
  422.2 0.0 copy-done
  422.2 0.8 copy.20
Async XLA Ops:
  406.4 15.0 %copy-start.1 = (bf16[1600,128]{1,0:T(8,128)(2,1)S(1)}, bf16[1600,128]{1,0:T(8,128)(2,1)}, u32[]{:S(2)}) copy-start(bf16[1600,128]{1,0:T(8,128)(2,1)} %get-tuple-element.62) | copy-start | bytes 1228804
  406.4 15.8 %copy-start = (bf16[1600,128]{1,0:T(8,128)(2,1)S(1)}, bf16[1600,128]{1,0:T(8,128)(2,1)}, u32[]{:S(2)}) copy-start(bf16[1600,128]{1,0:T(8,128)(2,1)} %get-tuple-element.63) | copy-start | bytes 1228804
